TPU v7x, 32 devices: a whole 2x2x4 slice. The times are simulated.
32 devices in a mesh: facet: 4 (over y, core), sub: 8 (over z, x).
Axes of the slice: x: 2, y: 2, z: 4, core: 2. Of those that a mesh axis runs over, the one named last changes fastest.
Arguments:
- facet_strips: bfloat16 [2, 16384, 4096], P(None, 'facet', 'sub'), may hold values from -6 to 6
- row_window: float32 [4096], replicated, may hold values from 0.25 to 1.75
- col_window: float32 [4096], P('sub'), may hold values from 0.25 to 1.75
- row_offsets: int32 [4], replicated, may hold values from 0 to 3584
- col_offsets: int32 [4], replicated, may hold values from 0 to 3584
- tile_owner: int32 [8, 4, 128, 1], P('sub', 'facet'), may hold values from 0 to 7; in each aligned block of 128 rows (0 to 127, 128 to 255, ..., all dimensions but the last counted through in order) at most 64 rows name the same one
- measured: float32 [4, 8, 512, 2, 128], P('facet', 'sub'), may hold values from -12 to 12
- vis_weight: float32 [4, 8, 512, 128], P('facet', 'sub'), may hold values from 0.1 to 1
- uvw_pixels: int32 [4, 8, 512, 3, 128], P('facet', 'sub'), may hold values from 0 to 15
- vis_count: int32 [4, 8, 512], P('facet', 'sub'), may hold values from 1 to 128
Outputs:
- facet_update: bfloat16 [2, 16384, 4096], P(None, 'facet', 'sub')
Inputs may be any that keep to these rules, and one draw needn't show every extreme that they name: Among the tiles of one row block of the subgrids of one facet index (the entries of tile_owner at one s and the 1 subgrids of one index of facet), no owner is named more than 64 times, and one owner is named exactly 64 times by some row block.
All inputs are finite; a program needn't handle non-finite values.
Results may differ from a plain program's by a relative error of at most 0.024.
Values may be sent and summed in bfloat16 or wider, within the bound.
No kernel may reach another device: no remote copies, remote signals or barrier semaphores. Data moves between devices by JAX's collectives and lax.ppermute only.
A program may use at most 128 MiB of HBM per device.

v0:
```python
from functools import partial
import math

import jax
import jax.numpy as jnp
from jax import lax
from jax.sharding import PartitionSpec as P

SG = 512
RADIX = 64
TS = 16


kernel_width = 2.5
kernel_norm = 0.565


def contract(pattern, first, other):
    return jnp.einsum(pattern, first, other, preferred_element_type=jnp.float32)


def angle_table(row_count, col_count, length):
    lefts = jnp.arange(row_count, dtype=jnp.int32)[:, None]
    rights = jnp.arange(col_count, dtype=jnp.int32)[None, :]
    turn_count = (lefts * rights % length).astype(jnp.float32)
    angles = turn_count * (2.0 * math.pi / length)
    return (jnp.cos(angles), jnp.sin(angles))


def complex_matrix(extent, direction):
    cosine, sine_table = angle_table(extent, extent, extent)
    sine_table = direction * sine_table
    upper = jnp.stack([cosine, -sine_table], axis=1)
    lower = jnp.stack([sine_table, cosine], axis=1)
    return jnp.stack([upper, lower], axis=0).astype(jnp.bfloat16)


def apply_twist(values, cosine, sine_table, direction):
    real_part = values[:, 0]
    imag_part = values[:, 1]
    sine_table = direction * sine_table
    return jnp.stack(
        [cosine * real_part - sine_table * imag_part, sine_table * real_part + cosine * imag_part],
        axis=1,
    ).astype(jnp.bfloat16)


def rows_forward(values, radix_size):
    batches = values.shape[0]
    length = values.shape[2]
    columns = values.shape[3]
    second = length // radix_size
    shaped = values.reshape(batches, 2, radix_size, second, columns)
    inner_sum = contract("akzn,bznqc->bakqc", complex_matrix(radix_size, -1.0), shaped)
    cosine, sine_table = angle_table(radix_size, second, length)
    turned = apply_twist(inner_sum, cosine[:, :, None], sine_table[:, :, None], -1.0)
    outer_sum = contract("ajzq,bzkqc->bajkc", complex_matrix(second, -1.0), turned)
    return outer_sum.reshape(batches, 2, length, columns)


def rows_backward(values, radix_size):
    batches = values.shape[0]
    length = values.shape[2]
    columns = values.shape[3]
    second = length // radix_size
    shaped = values.reshape(batches, 2, second, radix_size, columns)
    inner_sum = contract("ajzq,bzqkc->bajkc", complex_matrix(second, 1.0), shaped)
    cosine, sine_table = angle_table(second, radix_size, length)
    turned = apply_twist(inner_sum, cosine[:, :, None], sine_table[:, :, None], 1.0)
    outer_sum = contract("anzk,bzjkc->banjc", complex_matrix(radix_size, 1.0), turned)
    return outer_sum.reshape(batches, 2, length, columns)


def cols_forward(values, radix_size):
    batches = values.shape[0]
    middle = values.shape[2]
    length = values.shape[3]
    second = length // radix_size
    shaped = values.reshape(batches, 2, middle, radix_size, second)
    inner_sum = contract("akzn,bzmnq->bamkq", complex_matrix(radix_size, -1.0), shaped)
    cosine, sine_table = angle_table(radix_size, second, length)
    turned = apply_twist(inner_sum, cosine, sine_table, -1.0)
    outer_sum = contract("ajzq,bzmkq->bamjk", complex_matrix(second, -1.0), turned)
    return outer_sum.reshape(batches, 2, middle, length)


def cols_backward(values, radix_size):
    batches = values.shape[0]
    middle = values.shape[2]
    length = values.shape[3]
    second = length // radix_size
    shaped = values.reshape(batches, 2, middle, second, radix_size)
    inner_sum = contract("ajzq,bzmqk->bamjk", complex_matrix(second, 1.0), shaped)
    cosine, sine_table = angle_table(second, radix_size, length)
    turned = apply_twist(inner_sum, cosine, sine_table, 1.0)
    outer_sum = contract("anzk,bzmjk->bamnj", complex_matrix(radix_size, 1.0), turned)
    return outer_sum.reshape(batches, 2, middle, length)


def rotate(values, facet_index, offsets, facet_count, direction):
    turn_count = (facet_index * offsets % facet_count).astype(jnp.float32)
    angles = turn_count * (2.0 * math.pi / facet_count)
    extra = (1,) * (values.ndim - 2)
    cosine = jnp.cos(angles).reshape(angles.shape + extra)
    sine_table = direction * jnp.sin(angles).reshape(angles.shape + extra)
    real_part = values[:, 0]
    imag_part = values[:, 1]
    return jnp.stack(
        [cosine * real_part - sine_table * imag_part, sine_table * real_part + cosine * imag_part],
        axis=1,
    )


def kernel_rows(centre, w_plane, tile_size):
    pixels = jnp.arange(tile_size, dtype=jnp.int32)
    offset = pixels[None, :, None] - centre[:, None, :]
    falloff = kernel_norm * jnp.exp(-jnp.square(offset.astype(jnp.float32) / kernel_width))
    square = jnp.square(pixels - tile_size // 2)
    turn_count = w_plane[:, None, :] * square[None, :, None] % (tile_size * tile_size)
    angles = turn_count.astype(jnp.float32) * (2.0 * math.pi / (tile_size * tile_size))
    return jnp.stack([falloff * jnp.cos(angles), -falloff * jnp.sin(angles)], axis=2).astype(
        jnp.bfloat16
    )


def visit_slots(slot_tiles, measured, weight, uvw_pixels, counts, tile_size):
    slots = slot_tiles.shape[0]
    visits = measured.shape[2]
    stacked_grid = slot_tiles.reshape(slots, 2 * tile_size, tile_size)
    row_kernel = kernel_rows(uvw_pixels[:, 0], uvw_pixels[:, 2], tile_size)
    col_kernel = kernel_rows(uvw_pixels[:, 1], uvw_pixels[:, 2], tile_size)
    products = contract(
        "sab,sbv->sav", stacked_grid, col_kernel.reshape(slots, tile_size, 2 * visits)
    )
    products = products.reshape(slots, 2, tile_size, 2, visits)
    part_real = products[:, 0, :, 0] - products[:, 1, :, 1]
    part_imag = products[:, 0, :, 1] + products[:, 1, :, 0]
    row_real = row_kernel[:, :, 0].astype(jnp.float32)
    row_imag = row_kernel[:, :, 1].astype(jnp.float32)
    pred_real = jnp.sum(row_real * part_real - row_imag * part_imag, axis=1)
    pred_imag = jnp.sum(row_real * part_imag + row_imag * part_real, axis=1)
    live_mask = jnp.arange(visits, dtype=jnp.int32)[None, :] < counts[:, None]
    res_real = jnp.where(live_mask, weight * (measured[:, 0] - pred_real), 0.0)
    res_imag = jnp.where(live_mask, weight * (measured[:, 1] - pred_imag), 0.0)
    spread_real = row_real * res_real[:, None, :] + row_imag * res_imag[:, None, :]
    spread_imag = row_real * res_imag[:, None, :] - row_imag * res_real[:, None, :]
    spread = (
        jnp.stack([spread_real, spread_imag], axis=1)
        .astype(jnp.bfloat16)
        .reshape(slots, 2 * tile_size, visits)
    )
    regrid = contract("sav,sbv->sab", spread, col_kernel.reshape(slots, 2 * tile_size, visits))
    regrid = regrid.reshape(slots, 2, tile_size, tile_size, 2)
    tile_real = regrid[:, 0, :, :, 0] + regrid[:, 1, :, :, 1]
    tile_imag = regrid[:, 1, :, :, 0] - regrid[:, 0, :, :, 1]
    return (
        jnp.stack([tile_real, tile_imag], axis=1)
        .astype(jnp.bfloat16)
        .reshape(slots, 2 * tile_size * tile_size)
    )


def routing(owners, sub_count):
    matches = (owners[:, None] == jnp.arange(sub_count, dtype=jnp.int32)[None, :]).astype(jnp.int32)
    return jnp.sum(jnp.cumsum(matches, axis=0) * matches, axis=1) - 1


def place_all(running, blocks, offsets):
    block_count = blocks.shape[0]
    block_rows = blocks.shape[2]
    row_index = (offsets[:, None] + jnp.arange(block_rows, dtype=jnp.int32)[None, :]).reshape(-1)
    values = jnp.transpose(blocks, (1, 0, 2, 3)).reshape(
        2, block_count * block_rows, blocks.shape[3]
    )
    return running.at[:, row_index, :].add(values.astype(jnp.float32))


def cut_columns(one_block, col_start):
    return lax.dynamic_slice_in_dim(one_block, col_start, SG, 2)


def embed_columns(one_block, col_start, full_width):
    canvas = jnp.zeros(one_block.shape[:-1] + (full_width,), jnp.bfloat16)
    return lax.dynamic_update_slice_in_dim(canvas, one_block, col_start, one_block.ndim - 1)


def column_images(blocks, starts, full_width):
    placed = jax.vmap(partial(embed_columns, full_width=full_width))(blocks, starts)
    images = cols_backward(placed, RADIX) * (1.0 / math.sqrt(full_width))
    return lax.optimization_barrier(images.astype(jnp.bfloat16))


def per_device(
    facet_strips,
    row_window,
    col_window,
    row_offsets,
    col_offsets,
    tile_owner,
    measured,
    vis_weight,
    uvw_pixels,
    vis_count,
):
    sub_count = lax.axis_size("sub")
    facet_count = lax.axis_size("facet")
    my_facet = lax.axis_index("facet")
    length = facet_strips.shape[1]
    strip_width = facet_strips.shape[2]
    total_subgrids = row_offsets.shape[0]
    my_subgrids = total_subgrids // facet_count
    full_width = strip_width * sub_count
    row_block = SG // sub_count
    prepared = (
        facet_strips.astype(jnp.float32) * row_window[None, :, None] * col_window[None, None, :]
    ).astype(jnp.bfloat16)
    spectrum = (rows_forward(prepared[None], RADIX)[0] * (1.0 / math.sqrt(length))).astype(
        jnp.bfloat16
    )

    def take_rows(row_start):
        return lax.dynamic_slice_in_dim(spectrum, row_start, SG, 1)

    contributions = jax.vmap(take_rows)(row_offsets)
    row_blocks = lax.all_to_all(contributions, "sub", split_axis=2, concat_axis=3, tiled=True)
    spectra = cols_forward(row_blocks, RADIX) * (1.0 / math.sqrt(full_width))
    extracted = jax.vmap(cut_columns)(spectra, col_offsets)
    offsets_here = row_offsets
    summed = lax.psum_scatter(
        rotate(extracted, my_facet, offsets_here, facet_count, -1.0).astype(jnp.bfloat16),
        "facet",
        scatter_dimension=0,
        tiled=True,
    )
    tile_rows = row_block // TS
    tile_cols = SG // TS
    tile_data = summed.reshape(my_subgrids, 2, tile_rows, TS, tile_cols, TS)
    tile_data = jnp.transpose(tile_data, (0, 2, 4, 1, 3, 5)).reshape(
        my_subgrids * tile_rows * tile_cols, 2 * TS * TS
    )
    owners = tile_owner.reshape(-1)
    capacity = measured.shape[2] // sub_count
    slot_index = owners * capacity + routing(owners, sub_count)
    chooser = (
        slot_index[None, :] == jnp.arange(sub_count * capacity, dtype=jnp.int32)[:, None]
    ).astype(jnp.bfloat16)
    outgoing = jnp.dot(chooser, tile_data, preferred_element_type=jnp.float32).astype(jnp.bfloat16)
    values_here = measured[0, 0]
    weights_here = vis_weight[0, 0]
    pixels_here = uvw_pixels[0, 0]
    counts_here = vis_count[0, 0]
    arrived = lax.all_to_all(outgoing, "sub", split_axis=0, concat_axis=0, tiled=True)
    answered = visit_slots(arrived, values_here, weights_here, pixels_here, counts_here, TS)
    returned = lax.all_to_all(answered, "sub", split_axis=0, concat_axis=0, tiled=True)
    my_tiles = jnp.einsum(
        "st,sf->tf", chooser, returned, preferred_element_type=jnp.float32
    ).astype(jnp.bfloat16)
    my_tiles = my_tiles.reshape(my_subgrids, tile_rows, tile_cols, 2, TS, TS)
    residual_block = jnp.transpose(my_tiles, (0, 3, 1, 4, 2, 5)).reshape(
        my_subgrids, 2, row_block, SG
    )
    running = jnp.zeros((2, length, strip_width), jnp.float32)
    own_starts = lax.dynamic_slice_in_dim(col_offsets, my_facet * my_subgrids, my_subgrids, 0)
    images = column_images(residual_block, own_starts, full_width)
    strip_images = lax.all_to_all(images, "sub", split_axis=3, concat_axis=2, tiled=True)
    offsets_here = row_offsets
    turned = rotate(
        lax.all_gather(strip_images, "facet", axis=0, tiled=True).astype(jnp.float32),
        my_facet,
        offsets_here,
        facet_count,
        1.0,
    )
    turned = lax.optimization_barrier(turned.astype(jnp.bfloat16))
    running = place_all(running, turned, offsets_here)
    sums_bf = running.astype(jnp.bfloat16)
    update = rows_backward(sums_bf[None], RADIX)[0] * (1.0 / math.sqrt(length))
    return (update * row_window[None, :, None] * col_window[None, None, :]).astype(jnp.bfloat16)


def solution(mesh):
    in_specs = (
        P(None, "facet", "sub"),
        P(),
        P("sub"),
        P(),
        P(),
        P("sub", "facet", None, None),
        P("facet", "sub", None, None, None),
        P("facet", "sub", None, None),
        P("facet", "sub", None, None, None),
        P("facet", "sub", None),
    )
    out_specs = P(None, "facet", "sub")
    return jax.shard_map(
        per_device, mesh=mesh, in_specs=in_specs, out_specs=out_specs, check_vma=False
    )
```

profile of v0, /device:TPU:0, one launch (start us, length us, event | category | flops | bytes accessed | tf_op | source)
XLA Modules:
  0.0 918.4 jit_solution(15494109007475796952)
XLA Ops:
  7.1 7.9 multiply_convert_fusion.1
  15.6 10.2 %convolution_bitcast_fusion.2 = f32[1,2,64,64,512]{4,2,1,3,0:T(8,128)S(1)} fusion(bf16[2,64,64,512,1]{3,2,1,0,4:T(8,128)(2,1)} %bitcast.383, bf16[1,64,2,64]{3,1,2,0:T(8,128)(2,1)S(1)} %get-tuple-element.92, bf16[1,64,2,64]{3,1,2,0:T(8,128)(2,1)S(1)} %get-tuple-element.93), kind=kOutput, calls=%fused_computation.13 | convolution fusion | flops 1073807360 | bytes 25198592 | tf_op jit(solution)/shard_map/akzn,bznqc->bakqc/dot_general | solution.py:19
  31.2 7.6 maximum_bitcast_fusion
  38.8 17.3 %fusion.18 = bf16[1,2,64,64,512]{4,2,1,3,0:T(8,128)(2,1)} fusion(bf16[2,64,64,512,1]{3,1,2,0,4:T(8,128)(2,1)} %maximum_bitcast_fusion, bf16[1,64,2,64]{3,1,2,0:T(8,128)(2,1)S(1)} %get-tuple-element.92, bf16[1,64,2,64]{3,1,2,0:T(8,128)(2,1)S(1)} %get-tuple-element.93), kind=kOutput, calls=%fused_computation.44 | convolution fusion | flops 1082195968 | bytes 16809984 | tf_op jit(solution)/shard_map/ajzq,bzkqc->bajkc/dot_general | solution.py:19
  56.2 11.5 %copy.281 = bf16[1,2,64,64,512]{4,3,2,1,0:T(8,128)(2,1)} copy(bf16[1,2,64,64,512]{4,2,1,3,0:T(8,128)(2,1)} %fusion.18) | data formatting | bytes 16777216 | tf_op jit(solution)/shard_map/convert_element_type | solution.py:217
  67.8 19.9 %while.2 = (s32[]{:T(128)}, bf16[2,4096,512]{2,1,0:T(8,128)(2,1)}, s32[4,3]{1,0:T(4,128)S(1)}, bf16[4,2,512,512]{3,1,0,2:T(2,128)(2,1)}, s32[]{:T(128)}) while((s32[]{:T(128)}, bf16[2,4096,512]{2,1,0:T(8,128)(2,1)}, s32[4,3]{1,0:T(4,128)S(1)}, bf16[4,2,512,512]{3,1,0,2:T(2,128)(2,1)}, s32[]{:T(128)}) %tuple.58), condition=%wide.while_cond.1, body=%wide.while_body.1.sunk | while | flops 2 | bytes 4194917 | solution.py:222
  87.7 7.4 all-to-all-start
  95.3 93.1 %all-to-all-done = bf16[4,2,512,512]{3,1,0,2:T(2,128)(2,1)} async-done(((bf16[4,2,512,512]{3,1,0,2:T(2,128)(2,1)}), bf16[4,2,512,512]{3,1,0,2:T(2,128)(2,1)}, u32[]{:S(2)}, u32[]{:S(2)}) %all-to-all-start) | async-done | bytes 4194336 | tf_op jit(solution)/shard_map/all_to_all | solution.py:225
  188.4 6.5 copy.406
  194.9 11.5 %reshape.778 = bf16[4,2,64,64,64]{4,3,2,1,0:T(8,128)(2,1)} reshape(bf16[4,2,64,8,512]{4,3,2,1,0:T(8,128)(2,1)} %bitcast.388) | data formatting | bytes 8388608 | tf_op jit(solution)/shard_map/reshape | solution.py:79
  215.1 10.3 %fusion = f32[4,2,64,64,64]{3,4,1,2,0:T(8,128)} fusion(bf16[4,1,64,64,64]{3,4,1,2,0:T(8,128)(2,1)} %get-tuple-element.68, bf16[4,1,64,64,64]{3,4,1,2,0:T(8,128)(2,1)S(1)} %get-tuple-element.67, bf16[1,64,2,64]{3,1,2,0:T(8,128)(2,1)S(1)} %get-tuple-element.92, bf16[1,64,2,64]{3,1,2,0:T(8,128)(2,1)S(1)} %get-tuple-element.93), kind=kOutput, calls=%fused_computation.6 | convolution fusion | flops 547422208 | bytes 12615680 | tf_op jit(solution)/shard_map/ajzq,bzmkq->bamjk/dot_general | solution.py:19
  225.4 26.8 %copy.355 = f32[4,2,64,64,64]{2,1,0,4,3:T(2,128)} copy(f32[4,2,64,64,64]{3,4,1,2,0:T(8,128)} %fusion) | data formatting | bytes 16777216 | tf_op jit(solution)/shard_map/mul | solution.py:226
  252.2 9.2 gather_fusion
  269.6 19.3 %reduce-scatter.2.cloned.1.call-done = bf16[1,2,64,512]{3,2,1,0:T(8,128)(2,1)} async-done(((bf16[4,2,64,512]{3,2,1,0:T(8,128)(2,1)}), bf16[1,2,64,512]{3,2,1,0:T(8,128)(2,1)}) %reduce-scatter.2.cloned.1.call-update) | async-done | bytes 131088 | tf_op jit(solution)/shard_map/reduce_scatter | solution.py:229
  298.5 18.5 %fusion.48 = (bf16[512,16,1,128]{3,1,0,2:T(8,128)(2,1)S(1)}, bf16[512,16,1,128]{3,1,0,2:T(8,128)(2,1)S(1)}) fusion(s32[512,128]{1,0:T(8,128)S(1)} %get-tuple-element.86, s32[16]{0:T(128)S(1)} %add_multiply_fusion, s32[512,128]{1,0:T(8,128)S(1)} %get-tuple-element.87), kind=kLoop, calls=%fused_computation.87 | loop fusion | flops 26214400 | bytes 4718656 | tf_op jit(solution)/shard_map/mul | solution.py:121
  319.4 7.5 copy.295
  332.2 7.9 copy.297
  343.8 10.3 %fusion.118 = f32[512,32,256]{2,1,0:T(8,128)} fusion(bf16[512,32,16]{1,2,0:T(8,128)(2,1)S(1)} %copy.296, bf16[512,16,256]{2,1,0:T(8,128)(2,1)} %copy.297), kind=kOutput, calls=%fused_computation.210 | convolution fusion | flops 134217728 | bytes 21495808 | tf_op jit(solution)/shard_map/sab,sbv->sav/dot_general | solution.py:19
  354.1 19.3 %copy.298 = f32[512,32,256]{0,2,1:T(8,128)} copy(f32[512,32,256]{2,1,0:T(8,128)} %fusion.118) | data formatting | bytes 33554432 | tf_op jit(solution)/shard_map/sab,sbv->sav/dot_general | solution.py:19
  373.4 12.6 %fusion.115 = (f32[512,1,16,1,128]{0,4,3,2,1:T(8,128)}, f32[512,1,16,1,128]{0,4,3,2,1:T(8,128)}, f32[512,1,16,1,128]{0,4,3,2,1:T(8,128)}, f32[512,1,16,1,128]{0,4,3,2,1:T(8,128)}) fusion(f32[512,2,16,2,128]{0,4,3,2,1:T(8,128)} %bitcast.381), kind=kLoop, calls=%fused_computation.207 | loop fusion | bytes 33554432 | tf_op jit(solution)/shard_map/slice | solution.py:136
  407.9 24.4 %fusion.30 = (f32[512,128]{1,0:T(8,128)S(1)}, f32[512,128]{1,0:T(8,128)S(1)}) fusion(f32[512,1,16,1,128]{4,2,0,3,1:T(8,128)} %copy.374, f32[512,1,16,1,128]{4,2,0,3,1:T(8,128)} %copy.375, f32[512,1,16,1,128]{4,2,0,3,1:T(8,128)} %copy.372, f32[512,1,16,1,128]{4,2,0,3,1:T(8,128)} %copy.373, s32[16]{0:T(128)S(1)} %add_multiply_fusion, ...), kind=kLoop, calls=%fused_computation.58 | loop fusion | flops 38666240 | bytes 17825856 | tf_op jit(solution)/shard_map/reduce_sum | solution.py:140
  432.5 19.3 %fusion.34 = (bf16[512,1,16,128]{3,2,0,1:T(8,128)(2,1)S(1)}, bf16[512,1,16,128]{3,2,0,1:T(8,128)(2,1)S(1)}) fusion(f32[512,128]{1,0:T(8,128)S(1)} %get-tuple-element.84, f32[512,128]{1,0:T(8,128)S(1)} %get-tuple-element.83, s32[16]{0:T(128)S(1)} %add_multiply_fusion, s32[512,128]{1,0:T(8,128)S(1)} %copy-done.2, s32[512,128]{1,0:T(8,128)S(1)} %get-tuple-element.85), kind=kLoop, calls=%fused_computation.62 | loop fusion | flops 36700160 | bytes 5242944 | tf_op jit(solution)/shard_map/convert.28
  481.4 7.6 all-to-all-done.2
  510.1 28.8 %all_to_all.51 = bf16[8,2,32768]{2,1,0:T(2,128)(2,1)} all-to-all(bf16[8,2,32768]{2,1,0:T(2,128)(2,1)S(1)} %reshape.855), channel_id=1, replica_groups=mesh['facet'=4,'sub'=8] {'sub'}, dimensions={0} | all-to-all | bytes 2097152 | tf_op jit(solution)/shard_map/all_to_all | solution.py:265
  545.7 32.7 %all-gather.2.cloned.1.call-done = bf16[4,2,512,512]{3,2,1,0:T(8,128)(2,1)} async-done(((bf16[1,2,512,512]{3,2,1,0:T(8,128)(2,1)}), bf16[4,2,512,512]{3,2,1,0:T(8,128)(2,1)}) %all-gather.2.cloned.1.call-update) | async-done | bytes 4194320 | tf_op jit(solution)/shard_map/all_gather | solution.py:268
  584.7 16.5 %copy.325 = f32[2048,2,512]{2,1,0:T(2,128)} copy(f32[2048,2,512]{2,0,1:T(8,128)S(1)} %bitcast.385) | data formatting | bytes 16777216 | tf_op jit(solution)/shard_map/convert_element_type | solution.py:175
  607.2 238.0 %scatter_fusion = f32[2,4096,512]{2,0,1:T(2,128)} fusion(f32[2,4096,512]{2,0,1:T(2,128)} %broadcast_in_dim.14, s32[2048]{0:T(1024)S(1)} %bitcast.401, f32[2048,2,512]{2,1,0:T(2,128)} %copy.325), kind=kCustom, calls=%fused_computation.1 | custom fusion | flops 2097152 | bytes 25174016 | tf_op jit(solution)/shard_map/scatter-add | solution.py:175
  845.2 9.3 %convert_element_type.350 = bf16[2,4096,512]{2,0,1:T(2,128)(2,1)} convert(f32[2,4096,512]{2,0,1:T(2,128)} %scatter_fusion) | non-fusion elementwise | flops 4194304 | bytes 25165824 | tf_op jit(solution)/shard_map/convert_element_type | solution.py:276
  854.6 15.2 %fusion.15 = f32[1,2,64,64,512]{4,2,3,1,0:T(8,128)S(1)} fusion(bf16[2,64,64,512]{3,0,2,1:T(2,128)(2,1)} %bitcast.384, bf16[1,64,2,64]{3,1,2,0:T(8,128)(2,1)S(1)} %copy-done.5, bf16[1,64,2,64]{3,1,2,0:T(8,128)(2,1)S(1)} %copy-done.4), kind=kOutput, calls=%fused_computation.41 | convolution fusion | flops 1073807360 | bytes 25198592 | tf_op jit(solution)/shard_map/ajzq,bzqkc->bajkc/dot_general | solution.py:19
  873.5 6.3 maximum_bitcast_fusion.3
  879.9 10.2 %convolution_bitcast_fusion = f32[1,2,64,64,512]{4,2,1,3,0:T(8,128)S(1)} fusion(bf16[2,64,64,512,1]{3,1,2,0,4:T(8,128)(2,1)} %maximum_bitcast_fusion.3, bf16[1,64,2,64]{3,1,2,0:T(8,128)(2,1)S(1)} %copy-done.5, bf16[1,64,2,64]{3,1,2,0:T(8,128)(2,1)S(1)} %copy-done.4), kind=kOutput, calls=%fused_computation.11 | convolution fusion | flops 1073807360 | bytes 25198592 | tf_op jit(solution)/shard_map/anzk,bzjkc->banjc/dot_general | solution.py:19
  890.1 16.8 %copy.329 = f32[1,2,64,64,512]{4,3,2,1,0:T(8,128)S(1)} copy(f32[1,2,64,64,512]{4,2,1,3,0:T(8,128)S(1)} %convolution_bitcast_fusion) | data formatting | bytes 33554432 | tf_op jit(solution)/shard_map/anzk,bzjkc->banjc/transpose | solution.py:19
  (140 shorter events, 161.9 us)
Async XLA Ops:
  56.2 11.6 %copy-start.10 = (s32[4]{0:T(128)S(1)}, s32[4]{0:T(128)}, u32[]{:S(2)}) copy-start(s32[4]{0:T(128)} %param.15) | copy-start | bytes 52
  87.7 7.5 copy-start.13
  87.7 100.7 %all-to-all-start = ((bf16[4,2,512,512]{3,1,0,2:T(2,128)(2,1)}), bf16[4,2,512,512]{3,1,0,2:T(2,128)(2,1)}, u32[]{:S(2)}, u32[]{:S(2)}) async-start(bf16[4,2,512,512]{3,1,0,2:T(2,128)(2,1)} %get-tuple-element.24), calls=%async_computation | async-start | bytes 8388608 | tf_op jit(solution)/shard_map/all_to_all | solution.py:225
  95.1 193.7 %reduce-scatter.2.cloned.1.call-start = ((), (), s32[]{:S(2)}) async-start(), calls=%async_computation.5 | async-start | bytes 655360 | tf_op jit(solution)/shard_map/reduce_scatter | solution.py:229
  264.0 4.0 copy-start.9
  269.6 47.4 %copy-start.1 = (s32[512,128]{1,0:T(8,128)}, s32[512,128]{1,0:T(8,128)S(1)}, u32[]{:S(2)}) copy-start(s32[512,128]{1,0:T(8,128)S(1)} %get-tuple-element.87) | copy-start | bytes 786436
  292.8 47.4 %all-to-all-start.1 = ((bf16[8,64,512]{2,1,0:T(8,128)(2,1)}), bf16[8,64,512]{2,1,0:T(8,128)(2,1)S(1)}, u32[]{:S(2)}, u32[]{:S(2)}) async-start(bf16[8,64,512]{2,1,0:T(8,128)(2,1)} %bitcast.53), calls=%async_computation.2 | async-start | bytes 1048576 | tf_op jit(solution)/shard_map/all_to_all | solution.py:252
  332.2 7.9 copy-start.3
  402.4 5.5 copy-start.2
  407.9 24.4 %copy-start.6 = (f32[1,1,512,128]{3,2,1,0:T(8,128)S(1)}, f32[1,1,512,128]{3,2,1,0:T(8,128)}, u32[]{:S(2)}) copy-start(f32[1,1,512,128]{3,2,1,0:T(8,128)} %param.19) | copy-start | bytes 786436
  407.9 24.4 %copy-start.11 = (s32[1,1,512]{2,1,0:T(1,128)S(1)}, s32[1,1,512]{2,1,0:T(1,128)}, u32[]{:S(2)}) copy-start(s32[1,1,512]{2,1,0:T(1,128)} %param.21) | copy-start | bytes 6148
  452.2 2.2 copy-start
  466.4 11.4 %copy-start.14 = (s32[1,3]{1,0:T(1,128)S(1)}, s32[1,3]{1,0:T(1,128)}, u32[]{:S(2)}) copy-start(s32[1,3]{1,0:T(1,128)} %constant.159.clone.1) | copy-start | bytes 40
  466.4 12.2 %copy-start.12 = (s32[4]{0:T(128)S(1)}, s32[4]{0:T(128)}, u32[]{:S(2)}) copy-start(s32[4]{0:T(128)} %constant.160.clone.1) | copy-start | bytes 52
  469.0 20.0 %all-to-all-start.2 = ((bf16[8,64,512]{2,1,0:T(8,128)(2,1)}), bf16[8,64,512]{2,1,0:T(8,128)(2,1)S(1)}, u32[]{:S(2)}, u32[]{:S(2)}) async-start(bf16[8,64,512]{2,1,0:T(8,128)(2,1)} %copy.311), calls=%async_computation.3 | async-start | bytes 1048576 | tf_op jit(solution)/shard_map/all_to_all | solution.py:254
  475.0 103.4 %all-gather.2.cloned.1.call-start = ((), (), s32[]{:S(2)}) async-start(), calls=%async_computation.6 | async-start | bytes 5242880 | tf_op jit(solution)/shard_map/all_gather | solution.py:268
  489.9 6.9 copy-start.4
  489.9 6.9 copy-start.5
  538.9 6.7 copy-start.7
  890.1 16.9 %copy-start.8 = (f32[512]{0:T(512)S(1)}, f32[512]{0:T(512)}, u32[]{:S(2)}) copy-start(f32[512]{0:T(512)} %param.14) | copy-start | bytes 6148
Sparse Core Ops, SparseCore 0:
  268.1 20.7 reduce-scatter.1
  545.7 32.6 all-gather.1
where the time goes:
time: 937 us; the launch traced here: 918 us
  other arithmetic  365 us (39%)
  local copies, waits for them, and re-layouts  247 us (26%)
  waiting for transfers between devices  153 us (16%)
  matrix products  89.5 us (10%)
  blocking collectives  28.8 us (3%)
  starting transfers between devices  19.1 us (2%)
  between operations  16.5 us (2%)
    scatter-add x1, other arithmetic, place_all(): return running.at[:, row_index, :].add(values.astype(jnp.float32))  238 us
    all_to_all x1, waiting for transfers between devices, per_device(): lax.all_to_all(contributions, 'sub', split_axis=2, concat_axis=3, tiled=T...  93.1 us
    dot_general x10, matrix products, contract(): return jnp.einsum(pattern, first, other, preferred_element_type=jnp.float32)  87.5 us
    all_gather x1, waiting for transfers between devices, per_device(): lax.all_gather(strip_images, 'facet', axis=0, tiled=True)  32.7 us
    unnamed x41, local copies, waits for them, and re-layouts  31.2 us
    all_to_all x1, blocking collectives, per_device(): lax.all_to_all(images, 'sub', split_axis=3, concat_axis=2, tiled=True)  28.8 us
    another operation x8, other arithmetic  27.9 us
    mul x1, local copies, waits for them, and re-layouts, per_device(): spectra = cols_forward(row_blocks, RADIX) * (1.0 / math.sqrt(full_width))  26.8 us
  transfers between devices with their start and end apart: 5, of which 4 were waited for; matrix products, arithmetic and copies ran while one was open for 5% of the time, Pallas kernels for 0%

commit v1 on v0

v1 whole, which is shorter than its diff:
```python
from functools import partial
import math

import jax
import jax.numpy as jnp
import numpy as np
from jax import lax
from jax.experimental import pallas as pl
from jax.experimental.pallas import tpu as pltpu
from jax.sharding import PartitionSpec as P

SG = 512
TS = 16
LANES = 128
GROUP = LANES // TS

kernel_width = 2.5
kernel_norm = 0.565

VMEM_LIMIT = 56 * 1024 * 1024
F32 = jnp.float32
BF16 = jnp.bfloat16


def column_order():
    lane = np.arange(SG)
    chunk, b, cl = lane // LANES, (lane % LANES) // GROUP, lane % GROUP
    return TS * (GROUP * chunk + cl) + b


def column_tables(full_width):
    turns = np.outer(np.arange(full_width, dtype=np.int64), column_order()) % full_width
    angles = turns * (2.0 * np.pi / full_width)
    return (
        jnp.asarray(np.cos(angles).astype(BF16)),
        jnp.asarray((-np.sin(angles)).astype(BF16)),
    )


def row_tables(length):
    q = np.arange(TS)[:, None] + TS * np.arange(SG // TS)[None, :]
    turns = (q[:, :, None] * np.arange(length // TS)[None, None, :]) % length
    angles = turns * (2.0 * np.pi / length)
    return (
        jnp.asarray(np.cos(angles).astype(np.float32)),
        jnp.asarray((-np.sin(angles)).astype(np.float32)),
    )


def pixel_tables():
    a = np.arange(TS)[:, None]
    lane = np.arange(LANES)[None, :] % TS
    fall = kernel_norm * np.exp(-np.square((a - lane) / kernel_width))
    angles = ((lane * np.square(a - TS // 2)) % (TS * TS)) * (2.0 * np.pi / (TS * TS))
    stacked = np.stack([fall, np.cos(angles), -np.sin(angles)])
    return jnp.asarray(
        np.broadcast_to(stacked[:, :, None, :], (3, TS, GROUP, LANES)).astype(np.float32)
    )


def group_tables():
    rows = 2 * TS * GROUP
    expand = (np.arange(rows)[:, None] // GROUP == np.arange(2 * TS)[None, :]).astype(BF16)
    mask = (
        np.arange(rows)[:, None] % GROUP == np.arange(LANES)[None, :] % GROUP
    ).astype(np.float32)
    return jnp.asarray(expand), jnp.asarray(expand.T.copy()), jnp.asarray(mask)


def radix4(x, direction):
    (r0, i0), (r1, i1), (r2, i2), (r3, i3) = x
    sr, si, dr, di = r0 + r2, i0 + i2, r0 - r2, i0 - i2
    tr, ti, er, ei = r1 + r3, i1 + i3, r1 - r3, i1 - i3
    if direction < 0:
        fr, fi = ei, -er
    else:
        fr, fi = -ei, er
    return [(sr + tr, si + ti), (dr + fr, di + fi), (sr - tr, si - ti), (dr - fr, di - fi)]


def turn(value, step, direction):
    r, i = value
    step = step % TS
    if step == 0:
        return value
    if step == 4:
        return (-i, r) if direction > 0 else (i, -r)
    angle = direction * 2.0 * math.pi * step / TS
    if step == 2:
        h = math.sqrt(0.5)
        return (h * (r - i), h * (r + i)) if direction > 0 else (h * (r + i), h * (i - r))
    if step == 6:
        h = math.sqrt(0.5)
        return (-h * (r + i), h * (r - i)) if direction > 0 else (h * (i - r), -h * (r + i))
    c, s = math.cos(angle), math.sin(angle)
    return (c * r - s * i, s * r + c * i)


def dft16(x, direction):
    inner = [radix4([x[4 * a + b] for a in range(4)], direction) for b in range(4)]
    out = [None] * 16
    for c in range(4):
        column = radix4([turn(inner[b][c], b * c, direction) for b in range(4)], direction)
        for d in range(4):
            out[c + 4 * d] = column[d]
    return out


def fill_matrix(off_ref, t_r, t_i, d_ref, write, count):
    def per_q1(q1, carry):
        a_r, a_i = t_r[q1], t_i[q1]
        for jr in range(count):
            d_r, d_i = d_ref[jr, 0:1, :], d_ref[jr, 1:2, :]
            m_r = a_r * d_r - a_i * d_i
            m_i = a_r * d_i + a_i * d_r
            upper = jnp.concatenate([m_r, -m_i], axis=1)
            lower = jnp.concatenate([m_i, m_r], axis=1)
            block = jnp.concatenate([upper, lower], axis=0).astype(BF16)
            write(jnp.bitwise_and(off_ref[jr] + q1, TS - 1), jr, block)
        return carry

    lax.fori_loop(0, TS, per_q1, 0)


def rows_forward_kernel(
    off_ref, x_ref, rw_ref, tr_ref, ti_ref, d_ref, l_ref, out_ref, mat, inner
):
    count = d_ref.shape[0]
    quarter = tr_ref.shape[2]
    width = x_ref.shape[2]
    part = 2 * (SG // TS)

    @pl.when(pl.program_id(0) == 0)
    def _():
        def write(k1, jr, block):
            mat[k1, jr * part : (jr + 1) * part, :] = block

        fill_matrix(off_ref, tr_ref, ti_ref, d_ref, write, count)

    def butterfly(chunk, carry):
        n2 = pl.multiple_of(chunk * 16, 16)
        for lane in range(0, width, LANES):
            values = []
            for n1 in range(TS):
                rows = pl.ds(pl.multiple_of(n1 * quarter + n2, 16), 16)
                window = rw_ref[rows, :]
                values.append(
                    tuple(
                        x_ref[z, rows, lane : lane + LANES].astype(F32) * window for z in range(2)
                    )
                )
            for k1, pair in enumerate(dft16(values, -1)):
                for z in range(2):
                    rows = pl.ds(pl.multiple_of(z * quarter + n2, 16), 16)
                    inner[k1, rows, lane : lane + LANES] = pair[z].astype(BF16)
        return carry

    lax.fori_loop(0, quarter // 16, butterfly, 0)

    def per_k1(k1, carry):
        sums = jnp.dot(mat[k1], inner[k1], preferred_element_type=F32)
        for jr in range(count):
            q1 = jnp.bitwise_and(k1 - off_ref[jr], TS - 1)
            real = sums[jr * part : jr * part + part // 2]
            imag = sums[jr * part + part // 2 : (jr + 1) * part]
            l_r, l_i = l_ref[jr, 0:1, :], l_ref[jr, 1:2, :]
            out_ref[jr, 0, q1] = (real * l_r - imag * l_i).astype(BF16)
            out_ref[jr, 1, q1] = (real * l_i + imag * l_r).astype(BF16)
        return carry

    lax.fori_loop(0, TS, per_k1, 0)


def rows_forward(offsets, strips, window, tables, turns, levels):
    _, length, width = strips.shape
    count = offsets.shape[0]
    quarter = length // TS
    q2 = SG // TS
    block = min(2 * LANES, width)
    return pl.pallas_call(
        rows_forward_kernel,
        grid_spec=pltpu.PrefetchScalarGridSpec(
            num_scalar_prefetch=1,
            grid=(width // block,),
            in_specs=[
                pl.BlockSpec((2, length, block), lambda c, o: (0, 0, c)),
                pl.BlockSpec((length, LANES), lambda c, o: (0, 0)),
                pl.BlockSpec((TS, q2, quarter), lambda c, o: (0, 0, 0)),
                pl.BlockSpec((TS, q2, quarter), lambda c, o: (0, 0, 0)),
                pl.BlockSpec((count, 2, quarter), lambda c, o: (0, 0, 0)),
                pl.BlockSpec((count, 2, block), lambda c, o: (0, 0, c)),
            ],
            out_specs=pl.BlockSpec((count, 2, TS, q2, block), lambda c, o: (0, 0, 0, 0, c)),
            scratch_shapes=[
                pltpu.VMEM((TS, count * 2 * q2, 2 * quarter), BF16),
                pltpu.VMEM((TS, 2 * quarter, block), BF16),
            ],
        ),
        out_shape=jax.ShapeDtypeStruct((count, 2, TS, q2, width), BF16),
        compiler_params=pltpu.CompilerParams(vmem_limit_bytes=VMEM_LIMIT),
        name="rows_forward",
    )(offsets, strips, window, *tables, turns, levels)


def cols_forward_kernel(me_ref, r_ref, fr_ref, fi_ref, a_ref, b_ref, full):
    subs, tile_rows = a_ref.shape[1], a_ref.shape[2] // (2 * TS)
    half = a_ref.shape[3]
    real, imag = r_ref[0, 0], r_ref[0, 1]
    f_r, f_i = fr_ref[...], fi_ref[...]
    for z, (u, v) in enumerate(((f_r, -f_i), (f_i, f_r))):
        sums = jnp.dot(real, u, preferred_element_type=F32)
        sums += jnp.dot(imag, v, preferred_element_type=F32)
        for chunk in range(SG // LANES):
            full[z, chunk] = sums[:, chunk * LANES : (chunk + 1) * LANES]

    me = me_ref[0]
    per_half = half // LANES

    def per_block(s, carry):
        place = jnp.bitwise_xor(s, me)
        for r2 in range(tile_rows):
            for z in range(2):
                rows = pl.ds(r2 * 2 * TS + z * TS, TS)
                for chunk in range(SG // LANES):
                    picked = full[z, chunk, pl.ds(s * tile_rows + r2, TS, stride=SG // TS), :]
                    out_ref = a_ref if chunk < per_half else b_ref
                    lane = (chunk % per_half) * LANES
                    out_ref[0, place, rows, lane : lane + LANES] = picked.astype(BF16)
        return carry

    lax.fori_loop(0, subs, per_block, 0)


def cols_forward(me, rows, tables, sub_count, first, step):
    count, _, _, width = rows.shape
    used = len(range(first, count, step))
    block_rows = 2 * SG // sub_count
    half = SG // 2
    shape = jax.ShapeDtypeStruct((used, sub_count, block_rows, half), BF16)
    return pl.pallas_call(
        cols_forward_kernel,
        grid_spec=pltpu.PrefetchScalarGridSpec(
            num_scalar_prefetch=1,
            grid=(used,),
            in_specs=[
                pl.BlockSpec((1, 2, SG, width), lambda j, m: (first + step * j, 0, 0, 0)),
                pl.BlockSpec((width, SG), lambda j, m: (m[0], 0)),
                pl.BlockSpec((width, SG), lambda j, m: (m[0], 0)),
            ],
            out_specs=[
                pl.BlockSpec((1, sub_count, block_rows, half), lambda j, m: (j, 0, 0, 0))
            ] * 2,
            scratch_shapes=[pltpu.VMEM((2, SG // LANES, SG, LANES), F32)],
        ),
        out_shape=[shape, shape],
        compiler_params=pltpu.CompilerParams(vmem_limit_bytes=VMEM_LIMIT),
        name="cols_forward",
    )(me, rows, *tables)


def route_kernel(me_ref, owner_ref, *refs):
    subs = len(refs) - 8
    parts, outs = refs[:4], refs[4 : 4 + subs]
    where_ref, held, slots, counts = refs[4 + subs :]
    tile_rows = held.shape[0]
    chunks = SG // LANES
    groups = outs[0].shape[0]
    me = me_ref[0]
    for h in range(2):
        total = parts[2 * h][...].astype(F32) + parts[2 * h + 1][...].astype(F32)
        for r2 in range(tile_rows):
            for c in range(chunks // 2):
                held[r2, h * (chunks // 2) + c] = total[
                    r2 * 2 * TS : (r2 + 1) * 2 * TS, c * LANES : (c + 1) * LANES
                ]

    def clear(g, carry):
        slots[g] = jnp.zeros(slots.shape[1:], F32)
        return carry

    lax.fori_loop(0, slots.shape[0], clear, 0)
    for o in range(subs):
        counts[o] = 0
    lane = lax.broadcasted_iota(jnp.int32, (2 * TS, LANES), 1) % GROUP

    def per_chunk(n, carry):
        value = held[n // chunks, n % chunks]
        for cl in range(GROUP):
            t = n * GROUP + cl
            owner = owner_ref[t]
            rank = counts[owner]
            counts[owner] = rank + 1
            g = jnp.bitwise_xor(owner, me) * groups + rank // GROUP
            sl = rank % GROUP
            where_ref[t] = g * GROUP + sl
            moved = pltpu.roll(value, jnp.bitwise_and(sl - cl, LANES - 1), 1)
            slots[g] = jnp.where(lane == sl, moved, slots[g])
        return carry

    lax.fori_loop(0, tile_rows * chunks, per_chunk, 0)
    for o in range(subs):
        outs[o][...] = slots[o * groups : (o + 1) * groups].astype(BF16)


def route(me, owners, parts, sub_count, groups):
    rows = parts[0].shape[0]
    tile_rows = rows // (2 * TS)
    smem = pl.BlockSpec(memory_space=pltpu.SMEM)
    vmem = pl.BlockSpec(memory_space=pltpu.VMEM)
    block = jax.ShapeDtypeStruct((groups, 2 * TS, LANES), BF16)
    return pl.pallas_call(
        route_kernel,
        in_specs=[smem, smem] + [vmem] * 4,
        out_specs=[vmem] * sub_count + [smem],
        out_shape=[block] * sub_count + [jax.ShapeDtypeStruct(owners.shape, jnp.int32)],
        scratch_shapes=[
            pltpu.VMEM((tile_rows, SG // LANES, 2 * TS, LANES), F32),
            pltpu.VMEM((sub_count * groups, 2 * TS, LANES), F32),
            pltpu.SMEM((sub_count,), jnp.int32),
        ],
        compiler_params=pltpu.CompilerParams(vmem_limit_bytes=VMEM_LIMIT),
        name="route",
    )(me, owners, *parts)


def unroute_kernel(where_ref, *refs):
    subs = len(refs) - 3
    ins, (a_ref, b_ref, slots) = refs[:subs], refs[subs:]
    groups = ins[0].shape[0]
    chunks = SG // LANES
    for o in range(subs):
        slots[o * groups : (o + 1) * groups] = ins[o][...].astype(F32)
    lane = lax.broadcasted_iota(jnp.int32, (2 * TS, LANES), 1) % GROUP

    def per_row(r2, carry):
        rows = pl.ds(pl.multiple_of(r2 * 2 * TS, 2 * TS), 2 * TS)
        for chunk in range(chunks):
            total = jnp.zeros((2 * TS, LANES), F32)
            for cl in range(GROUP):
                slot = where_ref[(r2 * chunks + chunk) * GROUP + cl]
                moved = pltpu.roll(
                    slots[slot // GROUP], jnp.bitwise_and(cl - slot % GROUP, LANES - 1), 1
                )
                total = jnp.where(lane == cl, moved, total)
            out_ref = a_ref if chunk < chunks // 2 else b_ref
            at = (chunk % (chunks // 2)) * LANES
            out_ref[rows, at : at + LANES] = total.astype(BF16)
        return carry

    lax.fori_loop(0, a_ref.shape[0] // (2 * TS), per_row, 0)


def unroute(where, blocks, rows):
    groups = blocks[0].shape[0]
    smem = pl.BlockSpec(memory_space=pltpu.SMEM)
    vmem = pl.BlockSpec(memory_space=pltpu.VMEM)
    half = jax.ShapeDtypeStruct((rows, SG // 2), BF16)
    return pl.pallas_call(
        unroute_kernel,
        in_specs=[smem] + [vmem] * len(blocks),
        out_specs=[vmem] * 2,
        out_shape=[half] * 2,
        scratch_shapes=[pltpu.VMEM((len(blocks) * groups, 2 * TS, LANES), F32)],
        compiler_params=pltpu.CompilerParams(vmem_limit_bytes=VMEM_LIMIT),
        name="unroute",
    )(where, *blocks)


def visit_kernel(me_ref, *refs):
    subs = (len(refs) - 7) // 2
    ins, outs = refs[:subs], refs[7 + subs :]
    meas_ref, weight_ref, pixel_ref, pix_ref, expand_ref, gather_ref, mask_ref = refs[
        subs : subs + 7
    ]
    groups = ins[0].shape[0]
    rows = TS * GROUP
    me = me_ref[0]

    def look_up(table, index):
        return jnp.concatenate(
            [jnp.take_along_axis(pix_ref[table, a], index, axis=1) for a in range(TS)], axis=0
        )

    def one_group(in_ref, out_ref, g, first):
        at = pl.ds(pl.multiple_of(first + g * GROUP, GROUP), GROUP)
        fall_x = look_up(0, pixel_ref[0, at, :])
        fall_y = look_up(0, pixel_ref[1, at, :])
        w0 = pixel_ref[2, at, :]
        cosine, sine = look_up(1, w0), look_up(2, w0)
        row_r, row_i = fall_x * cosine, fall_x * sine
        col = jnp.concatenate([fall_y * cosine, fall_y * sine], axis=1).astype(BF16)
        spread_out = jnp.dot(expand_ref[...], in_ref[g], preferred_element_type=F32)
        blocks = (spread_out * mask_ref[...]).astype(BF16)
        sums = jnp.dot(blocks, col, preferred_element_type=F32)
        part_r = sums[:rows, :LANES] - sums[rows:, LANES:]
        part_i = sums[:rows, LANES:] + sums[rows:, :LANES]
        pred_r = jnp.sum((row_r * part_r - row_i * part_i).reshape(TS, GROUP, LANES), axis=0)
        pred_i = jnp.sum((row_r * part_i + row_i * part_r).reshape(TS, GROUP, LANES), axis=0)
        weight = weight_ref[at, :]
        res_r = jnp.tile(weight * (meas_ref[0, at, :] - pred_r), (TS, 1))
        res_i = jnp.tile(weight * (meas_ref[1, at, :] - pred_i), (TS, 1))
        s_r = (row_r * res_r + row_i * res_i).astype(BF16)
        s_i = (row_r * res_i - row_i * res_r).astype(BF16)
        both = jnp.concatenate(
            [jnp.concatenate([s_r, s_i], axis=1), jnp.concatenate([s_i, -s_r], axis=1)], axis=0
        )
        grid = lax.dot_general(
            both, col, (((1,), (1,)), ((), ())), preferred_element_type=F32
        )
        grid = (grid * mask_ref[...]).astype(BF16)
        out_ref[g] = jnp.dot(gather_ref[...], grid, preferred_element_type=F32).astype(BF16)

    for r in range(subs):
        first = jnp.bitwise_xor(me, r) * (groups * GROUP)

        def body(g, carry, r=r, first=first):
            one_group(ins[r], outs[r], g, first)
            return carry

        lax.fori_loop(0, groups, body, 0)


def visit(me, blocks, measured, weight, pixels, tables):
    vmem = pl.BlockSpec(memory_space=pltpu.VMEM)
    smem = pl.BlockSpec(memory_space=pltpu.SMEM)
    return pl.pallas_call(
        visit_kernel,
        in_specs=[smem] + [vmem] * (len(blocks) + 7),
        out_specs=[vmem] * len(blocks),
        out_shape=[jax.ShapeDtypeStruct(b.shape, b.dtype) for b in blocks],
        compiler_params=pltpu.CompilerParams(vmem_limit_bytes=VMEM_LIMIT),
        name="visit",
    )(me, *blocks, measured, weight, pixels, *tables)


def cols_backward_kernel(me_ref, off_ref, a_ref, b_ref, fr_ref, fi_ref, l_ref, out_ref, image):
    subs, rows = a_ref.shape[1], a_ref.shape[2]
    tile_rows = rows // (2 * TS)
    half = a_ref.shape[3]
    width = fr_ref.shape[0]
    block = tile_rows * TS
    me = me_ref[0]

    def pick(ref, z):
        value = ref[0].reshape(subs, tile_rows, 2, TS, half)[:, :, z]
        return value.reshape(subs * block, half)

    def times(left, right):
        return lax.dot_general(left, right, (((1,), (1,)), ((), ())), preferred_element_type=F32)

    parts = [(pick(ref, 0), pick(ref, 1)) for ref in (a_ref, b_ref)]
    real = imag = 0.0
    for h, (p_r, p_i) in enumerate(parts):
        f_r = fr_ref[:, h * half : (h + 1) * half]
        f_i = fi_ref[:, h * half : (h + 1) * half]
        real += times(p_r, f_r) + times(p_i, f_i)
        imag += times(p_i, f_r) + times(p_r, -f_i)
    l_r, l_i = l_ref[0, 0:1, :], l_ref[0, 1:2, :]
    for z, value in enumerate((real * l_r + imag * l_i, imag * l_r - real * l_i)):
        for s in range(subs):
            at = pl.ds(pl.multiple_of(jnp.bitwise_xor(s, me) * block, TS), block)
            for chunk in range(width // LANES):
                image[z, chunk, at, :] = value[
                    s * block : (s + 1) * block, chunk * LANES : (chunk + 1) * LANES
                ]
    off = off_ref[pl.program_id(0)]
    q2 = SG // TS

    def per_q1(q1, carry):
        k1 = jnp.bitwise_and(off + q1, TS - 1)
        for z in range(2):
            for chunk in range(width // LANES):
                picked = image[z, chunk, pl.ds(q1, q2, stride=TS), :]
                out_ref[k1, z * q2 : (z + 1) * q2, chunk * LANES : (chunk + 1) * LANES] = (
                    picked.astype(BF16)
                )
        return carry

    lax.fori_loop(0, TS, per_q1, 0)


def cols_backward(me, offsets, halves, tables, levels):
    count, subs, rows, half = halves[0].shape
    width = levels.shape[2]
    part = 2 * (SG // TS)
    return pl.pallas_call(
        cols_backward_kernel,
        grid_spec=pltpu.PrefetchScalarGridSpec(
            num_scalar_prefetch=2,
            grid=(count,),
            in_specs=[pl.BlockSpec((1, subs, rows, half), lambda j, m, o: (j, 0, 0, 0))] * 2
            + [pl.BlockSpec((width, SG), lambda j, m, o: (m[0], 0))] * 2
            + [pl.BlockSpec((1, 2, width), lambda j, m, o: (j, 0, 0))],
            out_specs=pl.BlockSpec((TS, part, width), lambda j, m, o: (0, j, 0)),
            scratch_shapes=[pltpu.VMEM((2, width // LANES, SG, LANES), F32)],
        ),
        out_shape=jax.ShapeDtypeStruct((TS, count * part, width), BF16),
        compiler_params=pltpu.CompilerParams(vmem_limit_bytes=VMEM_LIMIT),
        name="cols_backward",
    )(me, offsets, *halves, *tables, levels)


def transposed_kernel(off_ref, tr_ref, ti_ref, d_ref, out_ref, mat):
    part = 2 * (SG // TS)

    def write(k1, jr, block):
        mat[k1, jr * part : (jr + 1) * part, :] = block.astype(F32)

    fill_matrix(off_ref, tr_ref, ti_ref, d_ref, write, d_ref.shape[0])

    def per_k1(k1, carry):
        out_ref[k1] = mat[k1].T.astype(BF16)
        return carry

    lax.fori_loop(0, TS, per_k1, 0)


def transposed_matrix(offsets, tables, turns):
    count, _, quarter = turns.shape
    part = 2 * (SG // TS)
    vmem = pl.BlockSpec(memory_space=pltpu.VMEM)
    return pl.pallas_call(
        transposed_kernel,
        in_specs=[pl.BlockSpec(memory_space=pltpu.SMEM)] + [vmem] * 3,
        out_specs=vmem,
        out_shape=jax.ShapeDtypeStruct((TS, 2 * quarter, count * part), BF16),
        scratch_shapes=[pltpu.VMEM((TS, count * part, 2 * quarter), F32)],
        compiler_params=pltpu.CompilerParams(vmem_limit_bytes=VMEM_LIMIT),
        name="transposed_matrix",
    )(offsets, *tables, turns)


def rows_backward_kernel(image_ref, mat_ref, rw_ref, out_ref, middle):
    quarter = mat_ref.shape[1] // 2
    width = image_ref.shape[2]

    def per_k1(k1, carry):
        middle[k1] = jnp.dot(mat_ref[k1], image_ref[k1], preferred_element_type=F32)
        return carry

    lax.fori_loop(0, TS, per_k1, 0)

    def butterfly(chunk, carry):
        n2 = pl.multiple_of(chunk * 16, 16)
        for lane in range(0, width, LANES):
            values = [
                tuple(
                    middle[k1, pl.ds(pl.multiple_of(z * quarter + n2, 16), 16), lane : lane + LANES]
                    for z in range(2)
                )
                for k1 in range(TS)
            ]
            for n1, pair in enumerate(dft16(values, 1)):
                rows = pl.ds(pl.multiple_of(n1 * quarter + n2, 16), 16)
                window = rw_ref[rows, :]
                for z in range(2):
                    out_ref[z, rows, lane : lane + LANES] = (pair[z] * window).astype(BF16)
        return carry

    lax.fori_loop(0, quarter // 16, butterfly, 0)


def rows_backward(images, matrix, window):
    _, depth, width = images.shape
    length = window.shape[0]
    quarter = length // TS
    block = min(2 * LANES, width)
    return pl.pallas_call(
        rows_backward_kernel,
        grid=(width // block,),
        in_specs=[
            pl.BlockSpec((TS, depth, block), lambda c: (0, 0, c)),
            pl.BlockSpec((TS, 2 * quarter, depth), lambda c: (0, 0, 0)),
            pl.BlockSpec((length, LANES), lambda c: (0, 0)),
        ],
        out_specs=pl.BlockSpec((2, length, block), lambda c: (0, 0, c)),
        out_shape=jax.ShapeDtypeStruct((2, length, width), BF16),
        scratch_shapes=[pltpu.VMEM((TS, 2 * quarter, block), F32)],
        compiler_params=pltpu.CompilerParams(vmem_limit_bytes=VMEM_LIMIT),
        name="rows_backward",
    )(images, matrix, window)


def swap(value, axis, bit):
    return lax.ppermute(value, axis, [(i, i ^ bit) for i in range(lax.axis_size(axis))])


def bits_of(axis):
    return [(axis, 1 << n) for n in range(lax.axis_size(axis).bit_length() - 1)]


def orders():
    facet, sub = bits_of("facet")[1:], bits_of("sub")
    rest = facet[1:] + sub[1:]
    return facet[:1] + sub[:1] + rest, sub[:1] + facet[:1] + rest


def dimensions():
    return bits_of("facet")[:0:-1] + bits_of("sub")[::-1]


def sum_blocks(kept, sent):
    result = []
    for kept_half, sent_half, order in zip(kept, sent, orders()):
        value = kept_half + swap(sent_half, "facet", 1)
        dims = dimensions()
        value = value.reshape((2,) * len(dims) + value.shape[2:])
        for step in order:
            at = dims.index(step)
            dims.remove(step)
            mine = lax.index_in_dim(value, 0, at, keepdims=False)
            arrived = swap(lax.index_in_dim(value, 1, at, keepdims=False), *step)
            value = mine + arrived if dims else None
        result += [mine, arrived]
    return result


def gather_blocks(halves, facet_count, sub_count):
    result = []
    for value, order in zip(halves, orders()):
        shape = value.shape
        have = []
        every = dimensions()
        for step in order[::-1]:
            at = len([d for d in every if d in have and every.index(d) < every.index(step)])
            have.append(step)
            value = jnp.stack([value, swap(value, *step)], axis=at)
        value = value.reshape((facet_count // 2, sub_count) + shape)
        result.append((value, swap(value, "facet", 1)))
    return result


def per_device(
    facet_strips,
    row_window,
    col_window,
    row_offsets,
    col_offsets,
    tile_owner,
    measured,
    vis_weight,
    uvw_pixels,
    vis_count,
):
    sub_count = lax.axis_size("sub")
    facet_count = lax.axis_size("facet")
    my_facet = lax.axis_index("facet")
    my_sub = lax.axis_index("sub")
    _, length, strip_width = facet_strips.shape
    count = row_offsets.shape[0]
    full_width = strip_width * sub_count
    quarter = length // TS
    me = my_sub.reshape(1).astype(jnp.int32)

    relative = jnp.arange(count, dtype=jnp.int32)
    chosen = (relative[:, None] ^ my_facet) == relative[None, :]
    rows_at = jnp.sum(jnp.where(chosen, row_offsets[None, :], 0), axis=1)
    cols_at = jnp.sum(jnp.where(chosen, col_offsets[None, :], 0), axis=1)

    n2 = jnp.arange(quarter, dtype=jnp.int32)
    theta = (my_facet * rows_at % facet_count) * (length // facet_count)
    angles = ((n2[None, :] * rows_at[:, None] + theta[:, None]) % length).astype(F32) * (
        2.0 * math.pi / length
    )
    turns = jnp.stack([jnp.cos(angles), -jnp.sin(angles)], axis=1)
    c = my_sub * strip_width + jnp.arange(strip_width, dtype=jnp.int32)
    angles = (c[None, :] * cols_at[:, None] % full_width).astype(F32) * (2.0 * math.pi / full_width)
    level = col_window[None, :] * (1.0 / math.sqrt(length * full_width))
    levels = jnp.stack([level * jnp.cos(angles), -level * jnp.sin(angles)], axis=1)
    window = jnp.broadcast_to(row_window[:, None], (length, LANES))
    row_consts = row_tables(length)
    col_consts = column_tables(full_width)

    spectrum = rows_forward(rows_at, facet_strips, window, row_consts, turns, levels)
    spectrum = spectrum.reshape(count, 2, SG, strip_width)
    sent = cols_forward(me, spectrum, col_consts, sub_count, 1, 2)
    kept = cols_forward(me, spectrum, col_consts, sub_count, 0, 2)
    parts = sum_blocks(kept, sent)

    owners = tile_owner.reshape(-1)
    slots = measured.shape[2]
    capacity = slots // sub_count
    padded = -(-capacity // GROUP) * GROUP
    groups = padded // GROUP

    def per_slot(value):
        if padded == capacity:
            return value
        value = value.reshape((sub_count, capacity) + value.shape[1:])
        value = jnp.pad(value, ((0, 0), (0, padded - capacity)) + ((0, 0),) * (value.ndim - 2))
        return value.reshape((sub_count * padded,) + value.shape[2:])

    visits = vis_weight.shape[3]
    live = jnp.arange(visits, dtype=jnp.int32)[None, :] < vis_count[0, 0][:, None]
    weights = per_slot(jnp.where(live, vis_weight[0, 0], 0.0))
    values = jnp.transpose(per_slot(measured[0, 0]), (1, 0, 2))
    pixels = jnp.transpose(per_slot(uvw_pixels[0, 0]), (1, 0, 2))

    routed = route(me, owners, parts, sub_count, groups)
    outgoing, where = routed[:-1], routed[-1]
    arrived = [outgoing[0]] + [swap(outgoing[r], "sub", r) for r in range(1, sub_count)]
    answered = visit(
        me, arrived, values, weights, pixels, (pixel_tables(),) + group_tables()
    )
    returned = [answered[0]] + [swap(answered[r], "sub", r) for r in range(1, sub_count)]
    halves = unroute(where, returned, 2 * SG // sub_count)

    matrix = transposed_matrix(rows_at, row_consts, turns)
    (a_own, a_other), (b_own, b_other) = gather_blocks(halves, facet_count, sub_count)
    own = cols_backward(me, rows_at[0::2], (a_own, b_own), col_consts, levels[0::2])
    other = cols_backward(me, rows_at[1::2], (a_other, b_other), col_consts, levels[1::2])
    part = 2 * (SG // TS)
    images = jnp.stack(
        [
            own.reshape(TS, count // 2, part, strip_width),
            other.reshape(TS, count // 2, part, strip_width),
        ],
        axis=2,
    ).reshape(TS, count * part, strip_width)
    return rows_backward(images, matrix, window)


def solution(mesh):
    in_specs = (
        P(None, "facet", "sub"),
        P(),
        P("sub"),
        P(),
        P(),
        P("sub", "facet", None, None),
        P("facet", "sub", None, None, None),
        P("facet", "sub", None, None),
        P("facet", "sub", None, None, None),
        P("facet", "sub", None),
    )
    out_specs = P(None, "facet", "sub")
    return jax.shard_map(
        per_device, mesh=mesh, in_specs=in_specs, out_specs=out_specs, check_vma=False
    )
```

time: 937 us -> 249 us (0.27); the launches traced: 918 us -> 249 us
  other arithmetic: 365 us -> 12.5 us
  local copies, waits for them, and re-layouts: 247 us -> 10.1 us
  Pallas kernels: 0 us -> 131 us
  waiting for transfers between devices: 153 us -> 47.5 us
  matrix products: 89.5 us -> 0 us
  blocking collectives: 28.8 us -> 0 us
  starting transfers between devices: 19.1 us -> 47.2 us
  between operations: 16.5 us -> 0.42 us
    scatter-add x1 -> x0, other arithmetic: 238 us -> none  [place_all(): return running.at[:, row_index, :].add(values.astype(jnp.float32))]
    pallas_call x0 -> x10, Pallas kernels: none -> 131 us  [the longest x1 45.2 us: visit(): pl.pallas_call(visit_kernel, in_specs=[smem] + [vmem] * (len(blocks) + 7)...]
    all_to_all x3 -> x0, waiting for transfers between devices: 101 us -> none  [the longest x1 93.1 us: per_device(): lax.all_to_all(contributions, 'sub', split_axis=2, concat_axis=3, tiled=T...]
    dot_general x12 -> x0, matrix products: 89.5 us -> none  [the longest x10 87.5 us: contract(): return jnp.einsum(pattern, first, other, preferred_element_type=jnp.float32)]
    convert_element_type x9 -> x0, local copies, waits for them, and re-layouts: 55.6 us -> none  [the longest x3 20.8 us: kernel_rows(): jnp.stack([falloff * jnp.cos(angles), -falloff * jnp.sin(angles)], axis=2)]
    ppermute x0 -> x34, waiting for transfers between devices: none -> 47.5 us  [swap(): lax.ppermute(value, axis, [(i, i ^ bit) for i in range(lax.axis_size(axis...]
    ppermute x0 -> x34, starting transfers between devices: none -> 47.2 us  [swap(): lax.ppermute(value, axis, [(i, i ^ bit) for i in range(lax.axis_size(axis...]
    another operation x21 -> x11, other arithmetic: 54.5 us -> 7.34 us  [the longest x1 4.01 us: per_device(): jnp.stack([own.reshape(TS, count // 2, part, strip_width), other.reshape(...]
  transfers between devices with their start and end apart: 5 -> 34, of which waited for: 4 -> 16; matrix products, arithmetic and copies ran while one was open for 5% -> 4% of each run, Pallas kernels for 0% -> 10%
where the time goes in v1:
time: 249 us
  Pallas kernels  131 us (53%)
  waiting for transfers between devices  47.5 us (19%)
  starting transfers between devices  47.2 us (19%)
  other arithmetic  12.5 us (5%)
  local copies, waits for them, and re-layouts  10.1 us (4%)
    ppermute x34, waiting for transfers between devices, swap(): lax.ppermute(value, axis, [(i, i ^ bit) for i in range(lax.axis_size(axis...  47.5 us
    ppermute x34, starting transfers between devices, swap(): lax.ppermute(value, axis, [(i, i ^ bit) for i in range(lax.axis_size(axis...  47.2 us
    pallas_call x1, Pallas kernels, visit(): pl.pallas_call(visit_kernel, in_specs=[smem] + [vmem] * (len(blocks) + 7)...  45.2 us
    pallas_call x1, Pallas kernels, rows_forward(): pl.pallas_call(rows_forward_kernel, grid_spec=pltpu.PrefetchScalarGridSpe...  19.6 us
    pallas_call x1, Pallas kernels, rows_backward(): pl.pallas_call(rows_backward_kernel, grid=(width // block,), in_specs=[pl...  17.6 us
    pallas_call x2, Pallas kernels, cols_backward(): pl.pallas_call(cols_backward_kernel, grid_spec=pltpu.PrefetchScalarGridSp...  17.5 us
    pallas_call x2, Pallas kernels, cols_forward(): pl.pallas_call(cols_forward_kernel, grid_spec=pltpu.PrefetchScalarGridSpe...  17.4 us
    pallas_call x1, Pallas kernels, transposed_matrix(): pl.pallas_call(transposed_kernel, in_specs=[pl.BlockSpec(memory_space=plt...  6.51 us
  transfers between devices with their start and end apart: 34, of which 16 were waited for; matrix products, arithmetic and copies ran while one was open for 4% of the time, Pallas kernels for 10%

profile of v1, /device:TPU:0, one launch (start us, length us, event | category | flops | bytes accessed | tf_op | source)
XLA Modules:
  0.0 248.8 jit_solution(4999238145689386759)
XLA Ops:
  3.4 2.6 %broadcast_in_dim.41.rw_ref = f32[4096,128]{1,0:T(8,128)} broadcast(f32[4096]{0:T(1024)} %param.19), dimensions={0} | broadcast | bytes 2113536 | tf_op jit(solution)/shard_map/broadcast_in_dim | solution.py:670
  6.0 19.6 %rows_forward.1 = bf16[4,2,16,32,512]{4,3,2,1,0:T(8,128)(2,1)} custom-call(s32[4]{0:T(128)} %copy-done.24, bf16[2,4096,512]{2,1,0:T(8,128)(2,1)} %x_ref.1, f32[4096,128]{1,0:T(8,128)} %broadcast_in_dim.41.rw_ref, f32[16,32,256]{2,1,0:T(8,128)} %constant.73.clone.tr_ref, f32[16,32,256]{2,1,0:T(8,128)} %constant.74.clone.ti_ref, ...), custom_call_target="tpu_custom_call" | custom-call | tf_op jit(solution)/shard_map/rows_forward/pallas_call | solution.py:180
  25.7 8.7 %cols_forward.3 = (bf16[2,8,128,256]{3,2,1,0:T(8,128)(2,1)}, bf16[2,8,128,256]{3,2,1,0:T(8,128)(2,1)}) custom-call(s32[1]{0:T(128)} %bitcast.me_ref, bf16[4,2,512,512]{3,2,1,0:T(8,128)(2,1)} %bitcast.85, bf16[4096,512]{1,0:T(8,128)(2,1)} %constant.75.clone.fr_ref, bf16[4096,512]{1,0:T(8,128)(2,1)} %constant.76.clone.fi_ref), custom_call_target="tpu_custom_call" | custom-call | tf_op jit(solution)/shard_map/cols_forward/pallas_call | solution.py:240
  34.9 8.7 %cols_forward.2 = (bf16[2,8,128,256]{3,2,1,0:T(8,128)(2,1)}, bf16[2,8,128,256]{3,2,1,0:T(8,128)(2,1)}) custom-call(s32[1]{0:T(128)} %bitcast.me_ref, bf16[4,2,512,512]{3,2,1,0:T(8,128)(2,1)} %bitcast.86, bf16[4096,512]{1,0:T(8,128)(2,1)} %constant.75.clone.fr_ref, bf16[4096,512]{1,0:T(8,128)(2,1)} %constant.76.clone.fi_ref), custom_call_target="tpu_custom_call" | custom-call | tf_op jit(solution)/shard_map/cols_forward/pallas_call | solution.py:240
  45.4 3.0 %collective-permute-start.1 = (bf16[2,2,2,128,256]{4,3,0,1,2:T(8,128)(2,1)S(1)}, bf16[2,2,2,128,256]{4,3,0,1,2:T(8,128)(2,1)S(1)}, u32[]{:S(2)}, u32[]{:S(2)}) collective-permute-start(bf16[2,2,2,128,256]{4,3,0,1,2:T(8,128)(2,1)S(1)} %copy.47), channel_id=1, source_target_pairs={{0,16},{8,24},{16,0},{24,8},{1,17},{9,25},{17,1},{25,9},{2,18},{10... | collective-permute-start | bytes 1572872 | tf_op jit(solution)/shard_map/ppermute | solution.py:585
  50.5 10.0 %collective-permute-done.1 = bf16[2,2,2,128,256]{4,3,0,1,2:T(8,128)(2,1)S(1)} collective-permute-done((bf16[2,2,2,128,256]{4,3,0,1,2:T(8,128)(2,1)S(1)}, bf16[2,2,2,128,256]{4,3,0,1,2:T(8,128)(2,1)S(1)}, u32[]{:S(2)}, u32[]{:S(2)}) %collective-permute-start.1) | collective-permute-done | bytes 524320 | tf_op jit(solution)/shard_map/ppermute | solution.py:585
  60.6 1.8 collective-permute-start.2
  64.0 4.3 %collective-permute-done.2 = bf16[2,2,128,256]{3,2,0,1:T(8,128)(2,1)S(1)} collective-permute-done((bf16[2,2,128,256]{3,2,0,1:T(8,128)(2,1)S(1)}, bf16[2,2,128,256]{3,2,0,1:T(8,128)(2,1)S(1)}, u32[]{:S(2)}, u32[]{:S(2)}) %collective-permute-start.2) | collective-permute-done | bytes 262176 | tf_op jit(solution)/shard_map/ppermute | solution.py:585
  71.4 2.4 collective-permute-done.3
  74.4 2.2 collective-permute-start.4
  80.6 1.8 collective-permute-done.9.refs_3_
  83.1 4.4 %route.1 = (bf16[8,32,128]{2,1,0:T(8,128)(2,1)}, bf16[8,32,128]{2,1,0:T(8,128)(2,1)}, bf16[8,32,128]{2,1,0:T(8,128)(2,1)}, bf16[8,32,128]{2,1,0:T(8,128)(2,1)}, ...) custom-call(s32[1]{0:T(128)} %bitcast.me_ref, ...), custom_call_target="tpu_custom_call" | custom-call | tf_op jit(solution)/shard_map/route/pallas_call | solution.py:311
  92.8 2.2 collective-permute-start.14
  94.9 2.6 %collective-permute-start.15 = (bf16[8,32,128]{2,1,0:T(8,128)(2,1)}, bf16[8,32,128]{2,1,0:T(8,128)(2,1)S(1)}, u32[]{:S(2)}, u32[]{:S(2)}) collective-permute-start(bf16[8,32,128]{2,1,0:T(8,128)(2,1)} %get-tuple-element.39), channel_id=1, source_target_pairs={{0,6},{1,7},{2,4},{3,5},{4,2},{5,3},{6,0},{7,1},{8,14},{9,15},{10,... | collective-permute-start | bytes 196616 | tf_op jit(solution)/shard_map/ppermute | solution.py:585
  101.3 3.4 %collective-permute-done.16.refs_7_ = bf16[8,32,128]{2,1,0:T(8,128)(2,1)S(1)} collective-permute-done((bf16[8,32,128]{2,1,0:T(8,128)(2,1)}, bf16[8,32,128]{2,1,0:T(8,128)(2,1)S(1)}, u32[]{:S(2)}, u32[]{:S(2)}) %collective-permute-start.16) | collective-permute-done | bytes 65568 | tf_op jit(solution)/shard_map/ppermute | solution.py:585
  105.4 45.2 %visit.1 = (bf16[8,32,128]{2,1,0:T(8,128)(2,1)}, bf16[8,32,128]{2,1,0:T(8,128)(2,1)}, bf16[8,32,128]{2,1,0:T(8,128)(2,1)}, bf16[8,32,128]{2,1,0:T(8,128)(2,1)}, ...) custom-call(s32[1]{0:T(128)} %bitcast.me_ref, ...), custom_call_target="tpu_custom_call" | custom-call | tf_op jit(solution)/shard_map/visit/pallas_call | solution.py:426
  151.1 2.9 %collective-permute-start.19 = (bf16[8,32,128]{2,1,0:T(8,128)(2,1)}, bf16[8,32,128]{2,1,0:T(8,128)(2,1)S(1)}, u32[]{:S(2)}, u32[]{:S(2)}) collective-permute-start(bf16[8,32,128]{2,1,0:T(8,128)(2,1)} %get-tuple-element.44), channel_id=1, source_target_pairs={{0,3},{1,2},{2,1},{3,0},{4,7},{5,6},{6,5},{7,4},{8,11},{9,10},{10,... | collective-permute-start | bytes 196616 | tf_op jit(solution)/shard_map/ppermute | solution.py:585
  154.1 2.9 %collective-permute-start.21 = (bf16[8,32,128]{2,1,0:T(8,128)(2,1)}, bf16[8,32,128]{2,1,0:T(8,128)(2,1)S(1)}, u32[]{:S(2)}, u32[]{:S(2)}) collective-permute-start(bf16[8,32,128]{2,1,0:T(8,128)(2,1)} %get-tuple-element.46), channel_id=1, source_target_pairs={{0,5},{1,4},{2,7},{3,6},{4,1},{5,0},{6,3},{7,2},{8,13},{9,12},{10,... | collective-permute-start | bytes 196616 | tf_op jit(solution)/shard_map/ppermute | solution.py:585
  158.2 3.6 %collective-permute-start.23 = (bf16[8,32,128]{2,1,0:T(8,128)(2,1)}, bf16[8,32,128]{2,1,0:T(8,128)(2,1)S(1)}, u32[]{:S(2)}, u32[]{:S(2)}) collective-permute-start(bf16[8,32,128]{2,1,0:T(8,128)(2,1)} %get-tuple-element.48), channel_id=1, source_target_pairs={{0,7},{1,6},{2,5},{3,4},{4,3},{5,2},{6,1},{7,0},{8,15},{9,14},{10,... | collective-permute-start | bytes 196616 | tf_op jit(solution)/shard_map/ppermute | solution.py:585
  163.3 2.4 collective-permute-done.23.refs_7_
  166.3 2.9 %unroute.1 = (bf16[128,256]{1,0:T(8,128)(2,1)}, bf16[128,256]{1,0:T(8,128)(2,1)}) custom-call(s32[128]{0:T(128)} %get-tuple-element.32.where_ref, bf16[8,32,128]{2,1,0:T(8,128)(2,1)} %get-tuple-element.41.refs_0_, bf16[8,32,128]{2,1,0:T(8,128)(2,1)} %copy-done.12, bf16[8,32,128]{2,1,0:T(8,128)(2,1)} %copy-done.14, bf16[8,32,128]{2,1,0:T(8,128)(2,1)} %copy-done.15, ...), custom_call_target="tpu_custom_call" | custom-call | tf_op jit(solution)/shard_map/unroute/pallas_call | solution.py:358
  169.2 2.9 %collective-permute-start.24 = (bf16[128,256]{1,0:T(8,128)(2,1)}, bf16[128,256]{1,0:T(8,128)(2,1)S(1)}, u32[]{:S(2)}, u32[]{:S(2)}) collective-permute-start(bf16[128,256]{1,0:T(8,128)(2,1)} %get-tuple-element.49), channel_id=1, source_target_pairs={{0,4},{1,5},{2,6},{3,7},{4,0},{5,1},{6,2},{7,3},{8,12},{9,13},{10,... | collective-permute-start | bytes 196616 | tf_op jit(solution)/shard_map/ppermute | solution.py:585
  172.1 3.2 %collective-permute-done.28 = bf16[128,256]{1,0:T(8,128)(2,1)S(1)} collective-permute-done((bf16[128,256]{1,0:T(8,128)(2,1)}, bf16[128,256]{1,0:T(8,128)(2,1)S(1)}, u32[]{:S(2)}, u32[]{:S(2)}) %collective-permute-start.28) | collective-permute-done | bytes 65568 | tf_op jit(solution)/shard_map/ppermute | solution.py:585
  177.2 2.0 collective-permute-start.25
  179.1 2.0 collective-permute-done.29
  183.9 4.5 %collective-permute-done.30 = bf16[2,2,128,256]{3,2,0,1:T(8,128)(2,1)S(1)} collective-permute-done((bf16[2,2,128,256]{3,2,0,1:T(8,128)(2,1)S(1)}, bf16[2,2,128,256]{3,2,0,1:T(8,128)(2,1)S(1)}, u32[]{:S(2)}, u32[]{:S(2)}) %collective-permute-start.30) | collective-permute-done | bytes 262176 | tf_op jit(solution)/shard_map/ppermute | solution.py:585
  191.0 6.8 %collective-permute-done.31 = bf16[2,2,2,128,256]{4,3,1,2,0:T(8,128)(2,1)S(1)} collective-permute-done((bf16[2,2,2,128,256]{4,3,1,2,0:T(8,128)(2,1)S(1)}, bf16[2,2,2,128,256]{4,3,1,2,0:T(8,128)(2,1)S(1)}, u32[]{:S(2)}, u32[]{:S(2)}) %collective-permute-start.31) | collective-permute-done | bytes 524320 | tf_op jit(solution)/shard_map/ppermute | solution.py:585
  201.5 6.5 %transposed_matrix.1.mat_ref = bf16[16,512,256]{2,1,0:T(8,128)(2,1)} custom-call(s32[4]{0:T(128)} %copy-done.24, f32[16,32,256]{2,1,0:T(8,128)} %constant.73.clone.tr_ref, f32[16,32,256]{2,1,0:T(8,128)} %constant.74.clone.ti_ref, f32[4,2,256]{2,1,0:T(2,128)} %pad_maximum_fusion.10.d_ref), custom_call_target="tpu_custom_call" | custom-call | tf_op jit(solution)/shard_map/transposed_matrix/pallas_call | solution.py:522
  208.6 8.7 %cols_backward.2 = bf16[16,128,512]{2,1,0:T(8,128)(2,1)} custom-call(s32[1]{0:T(128)} %bitcast.me_ref, s32[2]{0:T(128)} %slice.62.off_ref, bf16[2,8,128,256]{3,2,1,0:T(8,128)(2,1)} %copy-done.2, bf16[2,8,128,256]{3,2,1,0:T(8,128)(2,1)} %bitcast.91, bf16[4096,512]{1,0:T(8,128)(2,1)} %constant.75.clone.fr_ref, bf16[4096,512]{1,0:T(8,128)(2,1)} %constant.76.clone.fi_ref, ...), custom_call_target="tpu_custom_call" | custom-call | tf_op jit(solution)/shard_map/cols_backward/pallas_call | solution.py:486
  218.4 8.8 %cols_backward.3 = bf16[16,128,512]{2,1,0:T(8,128)(2,1)} custom-call(s32[1]{0:T(128)} %bitcast.me_ref, s32[2]{0:T(128)} %slice.80.off_ref, bf16[2,8,128,256]{3,2,1,0:T(8,128)(2,1)} %copy-done.3, bf16[2,8,128,256]{3,2,1,0:T(8,128)(2,1)} %collective-permute-done.33.b_ref, bf16[4096,512]{1,0:T(8,128)(2,1)} %constant.75.clone.fr_ref, ...), custom_call_target="tpu_custom_call" | custom-call | tf_op jit(solution)/shard_map/cols_backward/pallas_call | solution.py:486
  227.2 4.0 %pad_maximum_fusion = bf16[16,2,2,64,512]{4,3,2,1,0:T(8,128)(2,1)} fusion(bf16[16,2,1,64,512]{4,3,2,1,0:T(8,128)(2,1)} %bitcast.89, bf16[16,2,1,64,512]{4,3,2,1,0:T(8,128)(2,1)S(1)} %bitcast.88), kind=kLoop, calls=%fused_computation | loop fusion | flops 2097152 | bytes 8388608 | tf_op jit(solution)/shard_map/stack | solution.py:713
  231.2 17.6 %rows_backward.1 = bf16[2,4096,512]{2,1,0:T(8,128)(2,1)} custom-call(bf16[16,256,512]{2,1,0:T(8,128)(2,1)} %bitcast.87, bf16[16,512,256]{2,1,0:T(8,128)(2,1)} %transposed_matrix.1.mat_ref, f32[4096,128]{1,0:T(8,128)} %broadcast_in_dim.41.rw_ref), custom_call_target="tpu_custom_call" | custom-call | tf_op jit(solution)/shard_map/rows_backward/pallas_call | solution.py:568
  (146 shorter events, 43.6 us)
Async XLA Ops:
  34.4 9.2 %collective-permute-start = (bf16[2,8,128,256]{3,2,1,0:T(8,128)(2,1)}, bf16[2,8,128,256]{3,2,1,0:T(8,128)(2,1)S(1)}, u32[]{:S(2)}, u32[]{:S(2)}) collective-permute-start(bf16[2,8,128,256]{3,2,1,0:T(8,128)(2,1)} %get-tuple-element.29), channel_id=1, source_target_pairs={{0,8},{8,0},{16,24},{24,16},{1,9},{9,1},{17,25},{25,17},{2,10},{10... | collective-permute-start | bytes 3145736 | tf_op jit(solution)/shard_map/ppermute | solution.py:585
  34.8 13.6 %collective-permute-start.5 = (bf16[2,8,128,256]{3,2,1,0:T(8,128)(2,1)}, bf16[2,8,128,256]{3,2,1,0:T(8,128)(2,1)S(1)}, u32[]{:S(2)}, u32[]{:S(2)}) collective-permute-start(bf16[2,8,128,256]{3,2,1,0:T(8,128)(2,1)} %get-tuple-element.31), channel_id=1, source_target_pairs={{0,8},{8,0},{16,24},{24,16},{1,9},{9,1},{17,25},{25,17},{2,10},{10... | collective-permute-start | bytes 3145736 | tf_op jit(solution)/shard_map/ppermute | solution.py:585
  45.4 15.1 %collective-permute-start.1 = (bf16[2,2,2,128,256]{4,3,0,1,2:T(8,128)(2,1)S(1)}, bf16[2,2,2,128,256]{4,3,0,1,2:T(8,128)(2,1)S(1)}, u32[]{:S(2)}, u32[]{:S(2)}) collective-permute-start(bf16[2,2,2,128,256]{4,3,0,1,2:T(8,128)(2,1)S(1)} %copy.47), channel_id=1, source_target_pairs={{0,16},{8,24},{16,0},{24,8},{1,17},{9,25},{17,1},{25,9},{2,18},{10... | collective-permute-start | bytes 1572872 | tf_op jit(solution)/shard_map/ppermute | solution.py:585
  48.9 13.6 %collective-permute-start.6 = (bf16[2,2,2,128,256]{4,3,1,2,0:T(8,128)(2,1)S(1)}, bf16[2,2,2,128,256]{4,3,1,2,0:T(8,128)(2,1)S(1)}, u32[]{:S(2)}, u32[]{:S(2)}) collective-permute-start(bf16[2,2,2,128,256]{4,3,1,2,0:T(8,128)(2,1)S(1)} %bitcast.99), channel_id=1, source_target_pairs={{0,1},{1,0},{2,3},{3,2},{4,5},{5,4},{6,7},{7,6},{8,9},{9,8},{10,11... | collective-permute-start | bytes 1572872 | tf_op jit(solution)/shard_map/ppermute | solution.py:585
  60.6 7.7 %collective-permute-start.2 = (bf16[2,2,128,256]{3,2,0,1:T(8,128)(2,1)S(1)}, bf16[2,2,128,256]{3,2,0,1:T(8,128)(2,1)S(1)}, u32[]{:S(2)}, u32[]{:S(2)}) collective-permute-start(bf16[2,2,128,256]{3,2,0,1:T(8,128)(2,1)S(1)} %slice_bitcast_fusion.2), channel_id=1, source_target_pairs={{0,1},{1,0},{2,3},{3,2},{4,5},{5,4},{6,7},{7,6},{8,9},{9,8},{10,11... | collective-permute-start | bytes 786440 | tf_op jit(solution)/shard_map/ppermute | solution.py:585
  62.6 7.3 %collective-permute-start.7 = (bf16[2,2,128,256]{3,2,0,1:T(8,128)(2,1)S(1)}, bf16[2,2,128,256]{3,2,0,1:T(8,128)(2,1)S(1)}, u32[]{:S(2)}, u32[]{:S(2)}) collective-permute-start(bf16[2,2,128,256]{3,2,0,1:T(8,128)(2,1)S(1)} %slice_bitcast_fusion), channel_id=1, source_target_pairs={{0,16},{8,24},{16,0},{24,8},{1,17},{9,25},{17,1},{25,9},{2,18},{10... | collective-permute-start | bytes 786440 | tf_op jit(solution)/shard_map/ppermute | solution.py:585
  68.4 5.4 %collective-permute-start.3 = (bf16[2,128,256]{2,1,0:T(8,128)(2,1)S(1)}, bf16[2,128,256]{2,1,0:T(8,128)(2,1)S(1)}, u32[]{:S(2)}, u32[]{:S(2)}) collective-permute-start(bf16[2,128,256]{2,1,0:T(8,128)(2,1)S(1)} %slice_bitcast_fusion.6), channel_id=1, source_target_pairs={{0,2},{1,3},{2,0},{3,1},{4,6},{5,7},{6,4},{7,5},{8,10},{9,11},{10,... | collective-permute-start | bytes 393224 | tf_op jit(solution)/shard_map/ppermute | solution.py:585
  70.0 6.7 %collective-permute-start.8 = (bf16[2,128,256]{2,1,0:T(8,128)(2,1)S(1)}, bf16[2,128,256]{2,1,0:T(8,128)(2,1)S(1)}, u32[]{:S(2)}, u32[]{:S(2)}) collective-permute-start(bf16[2,128,256]{2,1,0:T(8,128)(2,1)S(1)} %slice_bitcast_fusion.4), channel_id=1, source_target_pairs={{0,2},{1,3},{2,0},{3,1},{4,6},{5,7},{6,4},{7,5},{8,10},{9,11},{10,... | collective-permute-start | bytes 393224 | tf_op jit(solution)/shard_map/ppermute | solution.py:585
  74.4 6.2 %collective-permute-start.4 = (bf16[128,256]{1,0:T(8,128)(2,1)S(1)}, bf16[128,256]{1,0:T(8,128)(2,1)S(1)}, u32[]{:S(2)}, u32[]{:S(2)}) collective-permute-start(bf16[128,256]{1,0:T(8,128)(2,1)S(1)} %get-tuple-element.69), channel_id=1, source_target_pairs={{0,4},{1,5},{2,6},{3,7},{4,0},{5,1},{6,2},{7,3},{8,12},{9,13},{10,... | collective-permute-start | bytes 196616 | tf_op jit(solution)/shard_map/ppermute | solution.py:585
  87.5 7.4 %collective-permute-start.10 = (bf16[8,32,128]{2,1,0:T(8,128)(2,1)}, bf16[8,32,128]{2,1,0:T(8,128)(2,1)S(1)}, u32[]{:S(2)}, u32[]{:S(2)}) collective-permute-start(bf16[8,32,128]{2,1,0:T(8,128)(2,1)} %get-tuple-element.34), channel_id=1, source_target_pairs={{0,1},{1,0},{2,3},{3,2},{4,5},{5,4},{6,7},{7,6},{8,9},{9,8},{10,11... | collective-permute-start | bytes 196616 | tf_op jit(solution)/shard_map/ppermute | solution.py:585
  89.1 8.5 %collective-permute-start.11 = (bf16[8,32,128]{2,1,0:T(8,128)(2,1)}, bf16[8,32,128]{2,1,0:T(8,128)(2,1)S(1)}, u32[]{:S(2)}, u32[]{:S(2)}) collective-permute-start(bf16[8,32,128]{2,1,0:T(8,128)(2,1)} %get-tuple-element.35), channel_id=1, source_target_pairs={{0,2},{1,3},{2,0},{3,1},{4,6},{5,7},{6,4},{7,5},{8,10},{9,11},{10,... | collective-permute-start | bytes 196616 | tf_op jit(solution)/shard_map/ppermute | solution.py:585
  90.6 9.8 %collective-permute-start.12 = (bf16[8,32,128]{2,1,0:T(8,128)(2,1)}, bf16[8,32,128]{2,1,0:T(8,128)(2,1)S(1)}, u32[]{:S(2)}, u32[]{:S(2)}) collective-permute-start(bf16[8,32,128]{2,1,0:T(8,128)(2,1)} %get-tuple-element.36), channel_id=1, source_target_pairs={{0,3},{1,2},{2,1},{3,0},{4,7},{5,6},{6,5},{7,4},{8,11},{9,10},{10,... | collective-permute-start | bytes 196616 | tf_op jit(solution)/shard_map/ppermute | solution.py:585
  91.1 9.3 %collective-permute-start.13 = (bf16[8,32,128]{2,1,0:T(8,128)(2,1)}, bf16[8,32,128]{2,1,0:T(8,128)(2,1)S(1)}, u32[]{:S(2)}, u32[]{:S(2)}) collective-permute-start(bf16[8,32,128]{2,1,0:T(8,128)(2,1)} %get-tuple-element.37), channel_id=1, source_target_pairs={{0,4},{1,5},{2,6},{3,7},{4,0},{5,1},{6,2},{7,3},{8,12},{9,13},{10,... | collective-permute-start | bytes 196616 | tf_op jit(solution)/shard_map/ppermute | solution.py:585
  92.8 7.7 %collective-permute-start.14 = (bf16[8,32,128]{2,1,0:T(8,128)(2,1)}, bf16[8,32,128]{2,1,0:T(8,128)(2,1)S(1)}, u32[]{:S(2)}, u32[]{:S(2)}) collective-permute-start(bf16[8,32,128]{2,1,0:T(8,128)(2,1)} %get-tuple-element.38), channel_id=1, source_target_pairs={{0,5},{1,4},{2,7},{3,6},{4,1},{5,0},{6,3},{7,2},{8,13},{9,12},{10,... | collective-permute-start | bytes 196616 | tf_op jit(solution)/shard_map/ppermute | solution.py:585
  94.9 6.4 %collective-permute-start.15 = (bf16[8,32,128]{2,1,0:T(8,128)(2,1)}, bf16[8,32,128]{2,1,0:T(8,128)(2,1)S(1)}, u32[]{:S(2)}, u32[]{:S(2)}) collective-permute-start(bf16[8,32,128]{2,1,0:T(8,128)(2,1)} %get-tuple-element.39), channel_id=1, source_target_pairs={{0,6},{1,7},{2,4},{3,5},{4,2},{5,3},{6,0},{7,1},{8,14},{9,15},{10,... | collective-permute-start | bytes 196616 | tf_op jit(solution)/shard_map/ppermute | solution.py:585
  97.6 7.2 %collective-permute-start.16 = (bf16[8,32,128]{2,1,0:T(8,128)(2,1)}, bf16[8,32,128]{2,1,0:T(8,128)(2,1)S(1)}, u32[]{:S(2)}, u32[]{:S(2)}) collective-permute-start(bf16[8,32,128]{2,1,0:T(8,128)(2,1)} %get-tuple-element.40), channel_id=1, source_target_pairs={{0,7},{1,6},{2,5},{3,4},{4,3},{5,2},{6,1},{7,0},{8,15},{9,14},{10,... | collective-permute-start | bytes 196616 | tf_op jit(solution)/shard_map/ppermute | solution.py:585
  150.6 6.4 %collective-permute-start.17 = (bf16[8,32,128]{2,1,0:T(8,128)(2,1)}, bf16[8,32,128]{2,1,0:T(8,128)(2,1)S(1)}, u32[]{:S(2)}, u32[]{:S(2)}) collective-permute-start(bf16[8,32,128]{2,1,0:T(8,128)(2,1)} %get-tuple-element.42), channel_id=1, source_target_pairs={{0,1},{1,0},{2,3},{3,2},{4,5},{5,4},{6,7},{7,6},{8,9},{9,8},{10,11... | collective-permute-start | bytes 196616 | tf_op jit(solution)/shard_map/ppermute | solution.py:585
  151.1 7.0 %collective-permute-start.18 = (bf16[8,32,128]{2,1,0:T(8,128)(2,1)}, bf16[8,32,128]{2,1,0:T(8,128)(2,1)S(1)}, u32[]{:S(2)}, u32[]{:S(2)}) collective-permute-start(bf16[8,32,128]{2,1,0:T(8,128)(2,1)} %get-tuple-element.43), channel_id=1, source_target_pairs={{0,2},{1,3},{2,0},{3,1},{4,6},{5,7},{6,4},{7,5},{8,10},{9,11},{10,... | collective-permute-start | bytes 196616 | tf_op jit(solution)/shard_map/ppermute | solution.py:585
  151.1 10.6 %collective-permute-start.19 = (bf16[8,32,128]{2,1,0:T(8,128)(2,1)}, bf16[8,32,128]{2,1,0:T(8,128)(2,1)S(1)}, u32[]{:S(2)}, u32[]{:S(2)}) collective-permute-start(bf16[8,32,128]{2,1,0:T(8,128)(2,1)} %get-tuple-element.44), channel_id=1, source_target_pairs={{0,3},{1,2},{2,1},{3,0},{4,7},{5,6},{6,5},{7,4},{8,11},{9,10},{10,... | collective-permute-start | bytes 196616 | tf_op jit(solution)/shard_map/ppermute | solution.py:585
  154.1 7.7 %collective-permute-start.20 = (bf16[8,32,128]{2,1,0:T(8,128)(2,1)}, bf16[8,32,128]{2,1,0:T(8,128)(2,1)S(1)}, u32[]{:S(2)}, u32[]{:S(2)}) collective-permute-start(bf16[8,32,128]{2,1,0:T(8,128)(2,1)} %get-tuple-element.45), channel_id=1, source_target_pairs={{0,4},{1,5},{2,6},{3,7},{4,0},{5,1},{6,2},{7,3},{8,12},{9,13},{10,... | collective-permute-start | bytes 196616 | tf_op jit(solution)/shard_map/ppermute | solution.py:585
  154.1 7.7 %collective-permute-start.21 = (bf16[8,32,128]{2,1,0:T(8,128)(2,1)}, bf16[8,32,128]{2,1,0:T(8,128)(2,1)S(1)}, u32[]{:S(2)}, u32[]{:S(2)}) collective-permute-start(bf16[8,32,128]{2,1,0:T(8,128)(2,1)} %get-tuple-element.46), channel_id=1, source_target_pairs={{0,5},{1,4},{2,7},{3,6},{4,1},{5,0},{6,3},{7,2},{8,13},{9,12},{10,... | collective-permute-start | bytes 196616 | tf_op jit(solution)/shard_map/ppermute | solution.py:585
  157.0 6.3 %collective-permute-start.22 = (bf16[8,32,128]{2,1,0:T(8,128)(2,1)}, bf16[8,32,128]{2,1,0:T(8,128)(2,1)S(1)}, u32[]{:S(2)}, u32[]{:S(2)}) collective-permute-start(bf16[8,32,128]{2,1,0:T(8,128)(2,1)} %get-tuple-element.47), channel_id=1, source_target_pairs={{0,6},{1,7},{2,4},{3,5},{4,2},{5,3},{6,0},{7,1},{8,14},{9,15},{10,... | collective-permute-start | bytes 196616 | tf_op jit(solution)/shard_map/ppermute | solution.py:585
  158.2 7.5 %collective-permute-start.23 = (bf16[8,32,128]{2,1,0:T(8,128)(2,1)}, bf16[8,32,128]{2,1,0:T(8,128)(2,1)S(1)}, u32[]{:S(2)}, u32[]{:S(2)}) collective-permute-start(bf16[8,32,128]{2,1,0:T(8,128)(2,1)} %get-tuple-element.48), channel_id=1, source_target_pairs={{0,7},{1,6},{2,5},{3,4},{4,3},{5,2},{6,1},{7,0},{8,15},{9,14},{10,... | collective-permute-start | bytes 196616 | tf_op jit(solution)/shard_map/ppermute | solution.py:585
  169.2 6.1 %collective-permute-start.28 = (bf16[128,256]{1,0:T(8,128)(2,1)}, bf16[128,256]{1,0:T(8,128)(2,1)S(1)}, u32[]{:S(2)}, u32[]{:S(2)}) collective-permute-start(bf16[128,256]{1,0:T(8,128)(2,1)} %get-tuple-element.50), channel_id=1, source_target_pairs={{0,4},{1,5},{2,6},{3,7},{4,0},{5,1},{6,2},{7,3},{8,12},{9,13},{10,... | collective-permute-start | bytes 196616 | tf_op jit(solution)/shard_map/ppermute | solution.py:585
  169.2 7.1 %collective-permute-start.24 = (bf16[128,256]{1,0:T(8,128)(2,1)}, bf16[128,256]{1,0:T(8,128)(2,1)S(1)}, u32[]{:S(2)}, u32[]{:S(2)}) collective-permute-start(bf16[128,256]{1,0:T(8,128)(2,1)} %get-tuple-element.49), channel_id=1, source_target_pairs={{0,4},{1,5},{2,6},{3,7},{4,0},{5,1},{6,2},{7,3},{8,12},{9,13},{10,... | collective-permute-start | bytes 196616 | tf_op jit(solution)/shard_map/ppermute | solution.py:585
  177.2 5.4 %collective-permute-start.25 = (bf16[2,128,256]{2,1,0:T(8,128)(2,1)S(1)}, bf16[2,128,256]{2,1,0:T(8,128)(2,1)S(1)}, u32[]{:S(2)}, u32[]{:S(2)}) collective-permute-start(bf16[2,128,256]{2,1,0:T(8,128)(2,1)S(1)} %get-tuple-element.66), channel_id=1, source_target_pairs={{0,2},{1,3},{2,0},{3,1},{4,6},{5,7},{6,4},{7,5},{8,10},{9,11},{10,... | collective-permute-start | bytes 393224 | tf_op jit(solution)/shard_map/ppermute | solution.py:585
  181.2 7.3 %collective-permute-start.30 = (bf16[2,2,128,256]{3,2,0,1:T(8,128)(2,1)S(1)}, bf16[2,2,128,256]{3,2,0,1:T(8,128)(2,1)S(1)}, u32[]{:S(2)}, u32[]{:S(2)}) collective-permute-start(bf16[2,2,128,256]{3,2,0,1:T(8,128)(2,1)S(1)} %get-tuple-element.60), channel_id=1, source_target_pairs={{0,16},{8,24},{16,0},{24,8},{1,17},{9,25},{17,1},{25,9},{2,18},{10... | collective-permute-start | bytes 786440 | tf_op jit(solution)/shard_map/ppermute | solution.py:585
  182.6 7.5 %collective-permute-start.26 = (bf16[2,2,128,256]{3,2,0,1:T(8,128)(2,1)S(1)}, bf16[2,2,128,256]{3,2,0,1:T(8,128)(2,1)S(1)}, u32[]{:S(2)}, u32[]{:S(2)}) collective-permute-start(bf16[2,2,128,256]{3,2,0,1:T(8,128)(2,1)S(1)} %get-tuple-element.62), channel_id=1, source_target_pairs={{0,1},{1,0},{2,3},{3,2},{4,5},{5,4},{6,7},{7,6},{8,9},{9,8},{10,11... | collective-permute-start | bytes 786440 | tf_op jit(solution)/shard_map/ppermute | solution.py:585
  188.5 9.2 %collective-permute-start.31 = (bf16[2,2,2,128,256]{4,3,1,2,0:T(8,128)(2,1)S(1)}, bf16[2,2,2,128,256]{4,3,1,2,0:T(8,128)(2,1)S(1)}, u32[]{:S(2)}, u32[]{:S(2)}) collective-permute-start(bf16[2,2,2,128,256]{4,3,1,2,0:T(8,128)(2,1)S(1)} %get-tuple-element.58), channel_id=1, source_target_pairs={{0,1},{1,0},{2,3},{3,2},{4,5},{5,4},{6,7},{7,6},{8,9},{9,8},{10,11... | collective-permute-start | bytes 1572872 | tf_op jit(solution)/shard_map/ppermute | solution.py:585
  190.2 9.2 %collective-permute-start.27 = (bf16[2,2,2,128,256]{4,3,0,1,2:T(8,128)(2,1)S(1)}, bf16[2,2,2,128,256]{4,3,0,1,2:T(8,128)(2,1)S(1)}, u32[]{:S(2)}, u32[]{:S(2)}) collective-permute-start(bf16[2,2,2,128,256]{4,3,0,1,2:T(8,128)(2,1)S(1)} %pad_maximum_fusion.3), channel_id=1, source_target_pairs={{0,16},{8,24},{16,0},{24,8},{1,17},{9,25},{17,1},{25,9},{2,18},{10... | collective-permute-start | bytes 1572872 | tf_op jit(solution)/shard_map/ppermute | solution.py:585
  199.6 17.7 %collective-permute-start.32 = (bf16[2,8,128,256]{3,2,1,0:T(8,128)(2,1)S(1)}, bf16[2,8,128,256]{3,2,1,0:T(8,128)(2,1)S(1)}, u32[]{:S(2)}, u32[]{:S(2)}) collective-permute-start(bf16[2,8,128,256]{3,2,1,0:T(8,128)(2,1)S(1)} %pad_maximum_fusion.1.a_ref), channel_id=1, source_target_pairs={{0,8},{8,0},{16,24},{24,16},{1,9},{9,1},{17,25},{25,17},{2,10},{10... | collective-permute-start | bytes 3145736 | tf_op jit(solution)/shard_map/ppermute | solution.py:585
  199.7 17.6 %collective-permute-start.33 = (bf16[2,8,128,256]{3,2,1,0:T(8,128)(2,1)S(1)}, bf16[2,8,128,256]{3,2,1,0:T(8,128)(2,1)}, u32[]{:S(2)}, u32[]{:S(2)}) collective-permute-start(bf16[2,8,128,256]{3,2,1,0:T(8,128)(2,1)S(1)} %bitcast.90), channel_id=1, source_target_pairs={{0,8},{8,0},{16,24},{24,16},{1,9},{9,1},{17,25},{25,17},{2,10},{10... | collective-permute-start | bytes 3145736 | tf_op jit(solution)/shard_map/ppermute | solution.py:585
  (29 other events, 275.7 us)

commit v2 on v1

v2 whole, which is shorter than its diff:
```python
from functools import partial
import math

import jax
import jax.numpy as jnp
import numpy as np
from jax import lax
from jax.experimental import pallas as pl
from jax.experimental.pallas import tpu as pltpu
from jax.sharding import PartitionSpec as P

SG = 512
TS = 16
LANES = 128
GROUP = LANES // TS

kernel_width = 2.5
kernel_norm = 0.565

VMEM_LIMIT = 56 * 1024 * 1024
F32 = jnp.float32
BF16 = jnp.bfloat16


def column_order():
    lane = np.arange(SG)
    chunk, b, cl = lane // LANES, (lane % LANES) // GROUP, lane % GROUP
    return TS * (GROUP * chunk + cl) + b


def column_tables(full_width):
    turns = np.outer(np.arange(full_width, dtype=np.int64), column_order()) % full_width
    angles = turns * (2.0 * np.pi / full_width)
    return (
        jnp.asarray(np.cos(angles).astype(BF16)),
        jnp.asarray((-np.sin(angles)).astype(BF16)),
    )


def row_tables(length):
    q = np.arange(TS)[:, None] + TS * np.arange(SG // TS)[None, :]
    turns = (q[:, :, None] * np.arange(length // TS)[None, None, :]) % length
    angles = turns * (2.0 * np.pi / length)
    return (
        jnp.asarray(np.cos(angles).astype(np.float32)),
        jnp.asarray((-np.sin(angles)).astype(np.float32)),
    )


def radix4(x, direction):
    (r0, i0), (r1, i1), (r2, i2), (r3, i3) = x
    sr, si, dr, di = r0 + r2, i0 + i2, r0 - r2, i0 - i2
    tr, ti, er, ei = r1 + r3, i1 + i3, r1 - r3, i1 - i3
    if direction < 0:
        fr, fi = ei, -er
    else:
        fr, fi = -ei, er
    return [(sr + tr, si + ti), (dr + fr, di + fi), (sr - tr, si - ti), (dr - fr, di - fi)]


def turn(value, step, direction):
    r, i = value
    step = step % TS
    if step == 0:
        return value
    if step == 4:
        return (-i, r) if direction > 0 else (i, -r)
    angle = direction * 2.0 * math.pi * step / TS
    if step == 2:
        h = math.sqrt(0.5)
        return (h * (r - i), h * (r + i)) if direction > 0 else (h * (r + i), h * (i - r))
    if step == 6:
        h = math.sqrt(0.5)
        return (-h * (r + i), h * (r - i)) if direction > 0 else (h * (i - r), -h * (r + i))
    c, s = math.cos(angle), math.sin(angle)
    return (c * r - s * i, s * r + c * i)


def dft16(x, direction):
    inner = [radix4([x[4 * a + b] for a in range(4)], direction) for b in range(4)]
    out = [None] * 16
    for c in range(4):
        column = radix4([turn(inner[b][c], b * c, direction) for b in range(4)], direction)
        for d in range(4):
            out[c + 4 * d] = column[d]
    return out


def wave(turns, length):
    angles = turns.astype(F32) * (2.0 * math.pi / length)
    return jnp.cos(angles), -jnp.sin(angles)


def row_phase(ids, row_off, jr, quarter, facets):
    length = quarter * TS
    off = row_off[jnp.bitwise_xor(ids[0], jr)]
    theta = jnp.bitwise_and(ids[0] * off, facets - 1) * (length // facets)
    n2 = lax.broadcasted_iota(jnp.int32, (1, quarter), 1)
    return wave(jnp.bitwise_and(n2 * off + theta, length - 1), length)


def col_level(ids, col_off, jr, window, full_width, length):
    width = window.shape[1]
    off = col_off[jnp.bitwise_xor(ids[0], jr)]
    c = ids[1] * width + lax.broadcasted_iota(jnp.int32, (1, width), 1)
    cosine, sine = wave(jnp.bitwise_and(c * off, full_width - 1), full_width)
    level = window * (1.0 / math.sqrt(length * full_width))
    return level * cosine, level * sine


def spread_window(window_ref, spread):
    def one(i, carry):
        row = jnp.broadcast_to(window_ref[pl.ds(i, 1), :], (LANES, LANES))
        spread[pl.ds(pl.multiple_of(i * LANES, LANES), LANES), :] = row.T
        return carry

    lax.fori_loop(0, window_ref.shape[0], one, 0)


def place_of(jr, count):
    return (jr % 2) * (count // 2) + jr // 2


def fill_matrix(ids, row_off, tables, write, count):
    t_r, t_i = tables
    quarter = t_r.shape[2]
    phases = [row_phase(ids, row_off, jr, quarter, count) for jr in range(count)]

    def per_q1(q1, carry):
        a_r, a_i = t_r[q1], t_i[q1]
        for jr, (d_r, d_i) in enumerate(phases):
            m_r = a_r * d_r - a_i * d_i
            m_i = a_r * d_i + a_i * d_r
            upper = jnp.concatenate([m_r, -m_i], axis=1)
            lower = jnp.concatenate([m_i, m_r], axis=1)
            block = jnp.concatenate([upper, lower], axis=0).astype(BF16)
            off = row_off[jnp.bitwise_xor(ids[0], jr)]
            write(jnp.bitwise_and(off + q1, TS - 1), place_of(jr, count), block)
        return carry

    lax.fori_loop(0, TS, per_q1, 0)


def exchange(first, second):
    upper = lax.broadcasted_iota(jnp.int32, first.shape, 0) < 4
    return (
        jnp.where(upper, first, pltpu.roll(second, 4, 0)),
        jnp.where(upper, pltpu.roll(first, 4, 0), second),
    )


def columns_out(real, imag, f_r, f_i, full):
    for z, (u, v) in enumerate(((f_r, -f_i), (f_i, f_r))):
        sums = jnp.dot(real, u, preferred_element_type=F32)
        sums += jnp.dot(imag, v, preferred_element_type=F32)
        for chunk in range(SG // LANES):
            full[z, chunk] = sums[:, chunk * LANES : (chunk + 1) * LANES]


def send_blocks(full, me, subs, a_ref, b_ref, at):
    tile_rows = SG // TS // subs
    q2 = SG // TS
    chunks = SG // LANES

    def store(place, row, chunk, value):
        out_ref = a_ref if chunk < chunks // 2 else b_ref
        lane = (chunk % (chunks // 2)) * LANES
        out_ref[at, place, row : row + TS, lane : lane + LANES] = value.astype(BF16)

    if tile_rows == 4:

        def per_pair(m, carry):
            for z in range(2):
                for chunk in range(chunks):
                    for quad in range(0, TS, 4):
                        v = [
                            full[z, chunk, pl.ds(pl.multiple_of((quad + n) * q2 + m * 8, 8), 8), :]
                            for n in range(4)
                        ]
                        pairs = [exchange(v[0], v[1]), exchange(v[2], v[3])]
                        for n in range(2):
                            value = jnp.concatenate([pairs[0][n], pairs[1][n]], axis=0)
                            place = jnp.bitwise_xor(2 * m + n, me)
                            store(place, z * TS * tile_rows + quad * tile_rows, chunk, value)
            return carry

        lax.fori_loop(0, subs // 2, per_pair, 0)
    else:
        assert tile_rows == 1

        def per_block(s, carry):
            for z in range(2):
                for chunk in range(chunks):
                    value = full[z, chunk, pl.ds(s, TS, stride=q2), :]
                    store(jnp.bitwise_xor(s, me), z * TS, chunk, value)
            return carry

        lax.fori_loop(0, subs, per_block, 0)


def forward_kernel(
    ids,
    row_off,
    col_off,
    x_ref,
    rw_ref,
    cw_ref,
    tr_ref,
    ti_ref,
    fr_ref,
    fi_ref,
    kept_ref,
    a_ref,
    b_ref,
    mat,
    inner,
    spread,
    level,
    odd,
    full,
):
    count = level.shape[0]
    quarter = tr_ref.shape[2]
    length = quarter * TS
    block = x_ref.shape[2]
    width = fr_ref.shape[0]
    blocks = width // block
    subs = a_ref.shape[1]
    part = 2 * (SG // TS)
    step = pl.program_id(0)

    @pl.when(step == 0)
    def _():
        def write(k1, place, value):
            mat[k1, place * part : (place + 1) * part, :] = value

        fill_matrix(ids, row_off, (tr_ref, ti_ref), write, count)
        spread_window(rw_ref, spread)
        for jr in range(count):
            l_r, l_i = col_level(ids, col_off, jr, cw_ref[...], width * subs, length)
            level[jr, 0:1, :] = l_r
            level[jr, 1:2, :] = l_i

    @pl.when(step < blocks)
    def _():
        def butterfly(chunk, carry):
            n2 = pl.multiple_of(chunk * 16, 16)
            for lane in range(0, block, LANES):
                values = []
                for n1 in range(TS):
                    rows = pl.ds(pl.multiple_of(n1 * quarter + n2, 16), 16)
                    window = spread[rows, :]
                    values.append(
                        tuple(
                            x_ref[z, rows, lane : lane + LANES].astype(F32) * window
                            for z in range(2)
                        )
                    )
                for k1, pair in enumerate(dft16(values, -1)):
                    for z in range(2):
                        rows = pl.ds(pl.multiple_of(z * quarter + n2, 16), 16)
                        inner[k1, rows, lane : lane + LANES] = pair[z].astype(BF16)
            return carry

        lax.fori_loop(0, quarter // 16, butterfly, 0)
        lanes = pl.ds(pl.multiple_of(step * block, block), block)

        def per_k1(k1, carry):
            sums = jnp.dot(mat[k1], inner[k1], preferred_element_type=F32)
            for jr in range(count):
                off = row_off[jnp.bitwise_xor(ids[0], jr)]
                q1 = jnp.bitwise_and(k1 - off, TS - 1)
                at = place_of(jr, count) * part
                real = sums[at : at + part // 2]
                imag = sums[at + part // 2 : at + part]
                l_r, l_i = level[jr, 0:1, lanes], level[jr, 1:2, lanes]
                out_r = (real * l_r - imag * l_i).astype(BF16)
                out_i = (real * l_i + imag * l_r).astype(BF16)
                if jr % 2:
                    odd[jr // 2, 0, q1, :, lanes] = out_r
                    odd[jr // 2, 1, q1, :, lanes] = out_i
                else:
                    kept_ref[jr // 2, 0, q1] = out_r
                    kept_ref[jr // 2, 1, q1] = out_i
            return carry

        lax.fori_loop(0, TS, per_k1, 0, unroll=4)

    @pl.when(step >= blocks)
    def _():
        j = step - blocks
        columns_out(
            odd[j, 0].reshape(SG, width),
            odd[j, 1].reshape(SG, width),
            fr_ref[...],
            fi_ref[...],
            full,
        )
        send_blocks(full, ids[1], subs, a_ref, b_ref, 0)


def forward(ids, row_off, col_off, strips, row_window, col_window, row_consts, col_consts, subs):
    _, length, width = strips.shape
    count = row_off.shape[0]
    quarter = length // TS
    q2 = SG // TS
    block = min(2 * LANES, width)
    blocks = width // block
    half = SG // 2
    used = count // 2
    rows = 2 * SG // subs
    sent = jax.ShapeDtypeStruct((used, subs, rows, half), BF16)
    kept = jax.ShapeDtypeStruct((used, 2, TS, q2, width), BF16)

    def late(c, *_):
        return (jnp.maximum(c - blocks, 0), 0, 0, 0)

    return pl.pallas_call(
        forward_kernel,
        grid_spec=pltpu.PrefetchScalarGridSpec(
            num_scalar_prefetch=3,
            grid=(blocks + used,),
            in_specs=[
                pl.BlockSpec((2, length, block), lambda c, *_: (0, 0, jnp.minimum(c, blocks - 1))),
                pl.BlockSpec((length // LANES, LANES), lambda c, *_: (0, 0)),
                pl.BlockSpec((1, width), lambda c, *_: (0, 0)),
                pl.BlockSpec((TS, q2, quarter), lambda c, *_: (0, 0, 0)),
                pl.BlockSpec((TS, q2, quarter), lambda c, *_: (0, 0, 0)),
                pl.BlockSpec((width, SG), lambda c, m, *_: (m[1], 0)),
                pl.BlockSpec((width, SG), lambda c, m, *_: (m[1], 0)),
            ],
            out_specs=[
                pl.BlockSpec(
                    (used, 2, TS, q2, block),
                    lambda c, *_: (0, 0, 0, 0, jnp.minimum(c, blocks - 1)),
                ),
                pl.BlockSpec((1, subs, rows, half), late),
                pl.BlockSpec((1, subs, rows, half), late),
            ],
            scratch_shapes=[
                pltpu.VMEM((TS, count * 2 * q2, 2 * quarter), BF16),
                pltpu.VMEM((TS, 2 * quarter, block), BF16),
                pltpu.VMEM((length, LANES), F32),
                pltpu.VMEM((count, 2, width), F32),
                pltpu.VMEM((used, 2, TS, q2, width), BF16),
                pltpu.VMEM((2, SG // LANES, SG, LANES), F32),
            ],
        ),
        out_shape=[kept, sent, sent],
        compiler_params=pltpu.CompilerParams(vmem_limit_bytes=VMEM_LIMIT),
        cost_estimate=pl.CostEstimate(
            flops=12_000_000_000, bytes_accessed=16 << 20, transcendentals=0
        ),
        name="forward",
    )(ids, row_off, col_off, strips, row_window, col_window, *row_consts, *col_consts)


def cols_forward_kernel(ids, r_ref, fr_ref, fi_ref, a_ref, b_ref, full):
    columns_out(r_ref[0, 0], r_ref[0, 1], fr_ref[...], fi_ref[...], full)
    send_blocks(full, ids[1], a_ref.shape[1], a_ref, b_ref, 0)


def cols_forward(ids, rows, tables, subs):
    used, _, _, width = rows.shape
    block_rows = 2 * SG // subs
    half = SG // 2
    shape = jax.ShapeDtypeStruct((used, subs, block_rows, half), BF16)
    return pl.pallas_call(
        cols_forward_kernel,
        grid_spec=pltpu.PrefetchScalarGridSpec(
            num_scalar_prefetch=1,
            grid=(used,),
            in_specs=[
                pl.BlockSpec((1, 2, SG, width), lambda j, m: (j, 0, 0, 0)),
                pl.BlockSpec((width, SG), lambda j, m: (m[1], 0)),
                pl.BlockSpec((width, SG), lambda j, m: (m[1], 0)),
            ],
            out_specs=[pl.BlockSpec((1, subs, block_rows, half), lambda j, m: (j, 0, 0, 0))] * 2,
            scratch_shapes=[pltpu.VMEM((2, SG // LANES, SG, LANES), F32)],
        ),
        out_shape=[shape, shape],
        compiler_params=pltpu.CompilerParams(vmem_limit_bytes=VMEM_LIMIT),
        cost_estimate=pl.CostEstimate(
            flops=4_000_000_000, bytes_accessed=6 << 20, transcendentals=0
        ),
        name="cols_forward",
    )(ids, rows, *tables)


def route_kernel(ids, owner_ref, *refs):
    subs = len(refs) - 8
    parts, outs = refs[:4], refs[4 : 4 + subs]
    where_ref, held, slots, counts = refs[4 + subs :]
    chunks = SG // LANES
    tile_rows = held.shape[1] // (2 * TS)
    groups = outs[0].shape[0]
    me = ids[1]
    for h in range(2):
        total = parts[2 * h][...].astype(F32) + parts[2 * h + 1][...].astype(F32)
        for c in range(chunks // 2):
            held[h * (chunks // 2) + c] = total[:, c * LANES : (c + 1) * LANES]

    def clear(g, carry):
        slots[g] = jnp.zeros(slots.shape[1:], F32)
        return carry

    lax.fori_loop(0, slots.shape[0], clear, 0, unroll=8)
    for o in range(subs):
        counts[o] = 0
    lane = lax.broadcasted_iota(jnp.int32, (2 * TS, LANES), 1) % GROUP

    def per_chunk(n, carry):
        value = held[n % chunks, pl.ds(n // chunks, 2 * TS, stride=tile_rows), :]
        for cl in range(GROUP):
            t = n * GROUP + cl
            owner = owner_ref[t]
            rank = counts[owner]
            counts[owner] = rank + 1
            g = jnp.bitwise_xor(owner, me) * groups + rank // GROUP
            sl = rank % GROUP
            where_ref[t] = g * GROUP + sl
            moved = pltpu.roll(value, jnp.bitwise_and(sl - cl, LANES - 1), 1)
            slots[g] = jnp.where(lane == sl, moved, slots[g])
        return carry

    lax.fori_loop(0, tile_rows * chunks, per_chunk, 0)
    for o in range(subs):
        outs[o][...] = slots[o * groups : (o + 1) * groups].astype(BF16)


def route(ids, owners, parts, subs, groups):
    rows = parts[0].shape[0]
    smem = pl.BlockSpec(memory_space=pltpu.SMEM)
    vmem = pl.BlockSpec(memory_space=pltpu.VMEM)
    block = jax.ShapeDtypeStruct((groups, 2 * TS, LANES), BF16)
    return pl.pallas_call(
        route_kernel,
        in_specs=[smem, smem] + [vmem] * 4,
        out_specs=[vmem] * subs + [smem],
        out_shape=[block] * subs + [jax.ShapeDtypeStruct(owners.shape, jnp.int32)],
        scratch_shapes=[
            pltpu.VMEM((SG // LANES, rows, LANES), F32),
            pltpu.VMEM((subs * groups, 2 * TS, LANES), F32),
            pltpu.SMEM((subs,), jnp.int32),
        ],
        compiler_params=pltpu.CompilerParams(vmem_limit_bytes=VMEM_LIMIT),
        name="route",
    )(ids, owners, *parts)


def unroute_kernel(where_ref, *refs):
    subs = len(refs) - 4
    ins, (a_ref, b_ref, slots, held) = refs[:subs], refs[subs:]
    groups = ins[0].shape[0]
    chunks = SG // LANES
    tile_rows = held.shape[1] // (2 * TS)
    for o in range(subs):
        slots[o * groups : (o + 1) * groups] = ins[o][...].astype(F32)
    lane = lax.broadcasted_iota(jnp.int32, (2 * TS, LANES), 1) % GROUP

    def per_row(r2, carry):
        for chunk in range(chunks):
            total = jnp.zeros((2 * TS, LANES), F32)
            for cl in range(GROUP):
                slot = where_ref[(r2 * chunks + chunk) * GROUP + cl]
                moved = pltpu.roll(
                    slots[slot // GROUP], jnp.bitwise_and(cl - slot % GROUP, LANES - 1), 1
                )
                total = jnp.where(lane == cl, moved, total)
            held[chunk, pl.ds(r2, 2 * TS, stride=tile_rows), :] = total
        return carry

    lax.fori_loop(0, tile_rows, per_row, 0)
    for chunk in range(chunks):
        out_ref = a_ref if chunk < chunks // 2 else b_ref
        at = (chunk % (chunks // 2)) * LANES
        out_ref[:, at : at + LANES] = held[chunk].astype(BF16)


def unroute(where, blocks, rows):
    groups = blocks[0].shape[0]
    smem = pl.BlockSpec(memory_space=pltpu.SMEM)
    vmem = pl.BlockSpec(memory_space=pltpu.VMEM)
    half = jax.ShapeDtypeStruct((rows, SG // 2), BF16)
    return pl.pallas_call(
        unroute_kernel,
        in_specs=[smem] + [vmem] * len(blocks),
        out_specs=[vmem] * 2,
        out_shape=[half] * 2,
        scratch_shapes=[
            pltpu.VMEM((len(blocks) * groups, 2 * TS, LANES), F32),
            pltpu.VMEM((SG // LANES, rows, LANES), F32),
        ],
        compiler_params=pltpu.CompilerParams(vmem_limit_bytes=VMEM_LIMIT),
        name="unroute",
    )(where, *blocks)


def falloffs(centre):
    spread = kernel_width * kernel_width
    c = centre.astype(F32)
    value = kernel_norm * jnp.exp(c * c * (-1.0 / spread))
    ratio = jnp.exp((2.0 * c - 1.0) * (1.0 / spread))
    out = [value]
    for _ in range(1, TS):
        value = value * ratio
        ratio = ratio * math.exp(-2.0 / spread)
        out.append(value)
    return out


def plane_phases(plane):
    base_r, base_i = wave(plane, TS * TS)
    step_r, step_i = base_r * base_r - base_i * base_i, 2.0 * base_r * base_i
    value_r, value_i, turn_r, turn_i = base_r, base_i, base_r, base_i
    out = [(None, None), (value_r, value_i)]
    for _ in range(2, TS // 2 + 1):
        turn_r, turn_i = (
            turn_r * step_r - turn_i * step_i,
            turn_r * step_i + turn_i * step_r,
        )
        value_r, value_i = (
            value_r * turn_r - value_i * turn_i,
            value_r * turn_i + value_i * turn_r,
        )
        out.append((value_r, value_i))
    return out


def kernels_kernel(pixel_ref, row_ref, col_ref):
    def one(g, carry):
        at = pl.ds(pl.multiple_of(g * GROUP, GROUP), GROUP)
        across, along = falloffs(pixel_ref[0, at, :]), falloffs(pixel_ref[1, at, :])
        phases = plane_phases(pixel_ref[2, at, :])
        zero = jnp.zeros(across[0].shape, F32)

        def times(falls, a, z):
            if a == TS // 2:
                return zero if z else falls[a]
            return falls[a] * phases[abs(a - TS // 2)][z]

        for a in range(0, TS, 2):
            rows = pl.ds(a * GROUP, 2 * GROUP)
            for z in range(2):
                row = jnp.concatenate([times(across, a, z), times(across, a + 1, z)], axis=0)
                col = jnp.concatenate([times(along, a, z), times(along, a + 1, z)], axis=0)
                row_ref[g, z, rows, :] = row.astype(BF16)
                col_ref[g, rows, z * LANES : (z + 1) * LANES] = col.astype(BF16)
        return carry

    lax.fori_loop(0, row_ref.shape[0], one, 0, unroll=2)


def kernels(pixels, steps):
    slots = pixels.shape[1]
    groups = slots // GROUP
    rows = TS * GROUP
    return pl.pallas_call(
        kernels_kernel,
        grid=(steps,),
        in_specs=[pl.BlockSpec((3, slots // steps, LANES), lambda i: (0, i, 0))],
        out_specs=[
            pl.BlockSpec((groups // steps, 2, rows, LANES), lambda i: (i, 0, 0, 0)),
            pl.BlockSpec((groups // steps, rows, 2 * LANES), lambda i: (i, 0, 0)),
        ],
        out_shape=[
            jax.ShapeDtypeStruct((groups, 2, rows, LANES), BF16),
            jax.ShapeDtypeStruct((groups, rows, 2 * LANES), BF16),
        ],
        compiler_params=pltpu.CompilerParams(vmem_limit_bytes=VMEM_LIMIT),
        cost_estimate=pl.CostEstimate(
            flops=6_000_000_000, bytes_accessed=9 << 20, transcendentals=0
        ),
        name="kernels",
    )(pixels)


def visit_kernel(sources, *refs):
    n = (len(refs) - 7) // 2
    ins, outs = refs[:n], refs[n + 5 : 2 * n + 5]
    meas_ref, weight_ref, row_ref, col_ref, mask_ref = refs[n : n + 5]
    held, wide = refs[-2:]
    groups = held.shape[0]
    rows = TS * GROUP
    lane = lax.broadcasted_iota(jnp.int32, (2 * TS, LANES), 1) % GROUP

    def one(g, v):
        at = pl.ds(g * GROUP, GROUP)
        blocks = jnp.concatenate(
            [held[g, pl.ds(k, 1), :] * mask_ref[...] for k in range(2 * TS)], axis=0
        ).astype(BF16)
        col = col_ref[g]
        sums = jnp.dot(blocks, col, preferred_element_type=F32)
        part_r = sums[:rows, :LANES] - sums[rows:, LANES:]
        part_i = sums[:rows, LANES:] + sums[rows:, :LANES]
        row_r, row_i = row_ref[g, 0].astype(F32), row_ref[g, 1].astype(F32)
        pred_r = jnp.sum((row_r * part_r - row_i * part_i).reshape(TS, GROUP, LANES), axis=0)
        pred_i = jnp.sum((row_r * part_i + row_i * part_r).reshape(TS, GROUP, LANES), axis=0)
        weight = weight_ref[at, :]
        res_r = jnp.tile(weight * (meas_ref[0, at, :] - pred_r), (TS, 1))
        res_i = jnp.tile(weight * (meas_ref[1, at, :] - pred_i), (TS, 1))
        s_r = (row_r * res_r + row_i * res_i).astype(BF16)
        s_i = (row_r * res_i - row_i * res_r).astype(BF16)
        both = jnp.concatenate(
            [jnp.concatenate([s_r, s_i], axis=1), jnp.concatenate([s_i, -s_r], axis=1)], axis=0
        )
        wide[v] = lax.dot_general(both, col, (((1,), (1,)), ((), ())), preferred_element_type=F32)
        total = wide[v, pl.ds(0, 2 * TS, stride=GROUP), :]
        for slot in range(1, GROUP):
            total = jnp.where(lane == slot, wide[v, pl.ds(slot, 2 * TS, stride=GROUP), :], total)
        return total.astype(BF16)

    for i in range(n):

        @pl.when(pl.program_id(0) == i)
        def _(i=i):
            held[...] = ins[i][...].astype(F32)
            for g, value in enumerate([one(g, g) for g in range(groups)]):
                outs[i][g] = value


def visit(sources, blocks, measured, weight, row, col):
    n = len(blocks)
    shape = blocks[0].shape
    groups = shape[0]
    slots = groups * GROUP
    rows = TS * GROUP
    mask = np.arange(GROUP)[:, None] == np.arange(LANES)[None, :] % GROUP
    whole = pl.BlockSpec(shape, lambda i, m: (0, 0, 0))
    return pl.pallas_call(
        visit_kernel,
        grid_spec=pltpu.PrefetchScalarGridSpec(
            num_scalar_prefetch=1,
            grid=(n,),
            in_specs=[whole] * n
            + [
                pl.BlockSpec((2, slots, LANES), lambda i, m: (0, m[i], 0)),
                pl.BlockSpec((slots, LANES), lambda i, m: (m[i], 0)),
                pl.BlockSpec((groups, 2, rows, LANES), lambda i, m: (m[i], 0, 0, 0)),
                pl.BlockSpec((groups, rows, 2 * LANES), lambda i, m: (m[i], 0, 0)),
                pl.BlockSpec((GROUP, LANES), lambda i, m: (0, 0)),
            ],
            out_specs=[whole] * n,
            scratch_shapes=[
                pltpu.VMEM((groups, 2 * TS, LANES), F32),
                pltpu.VMEM((groups, 2 * rows, LANES), F32),
            ],
        ),
        out_shape=[jax.ShapeDtypeStruct(b.shape, b.dtype) for b in blocks],
        compiler_params=pltpu.CompilerParams(vmem_limit_bytes=VMEM_LIMIT),
        cost_estimate=pl.CostEstimate(
            flops=1_800_000_000 * n, bytes_accessed=(5 << 18) * n, transcendentals=0
        ),
        name="visit",
    )(sources, *blocks, measured, weight, row, col, jnp.asarray(mask.astype(np.float32)))


def columns_back(ids, jr, col_off, halves, fr_ref, fi_ref, cw_ref, image, length):
    subs, rows, half = halves[0].shape
    width = fr_ref.shape[0]
    block = rows // 2

    def times(left, right):
        return lax.dot_general(left, right, (((1,), (1,)), ((), ())), preferred_element_type=F32)

    real = imag = 0.0
    for h, ref in enumerate(halves):
        p_r = ref[:, :block, :].reshape(subs * block, half)
        p_i = ref[:, block:, :].reshape(subs * block, half)
        f_r = fr_ref[:, h * half : (h + 1) * half]
        f_i = fi_ref[:, h * half : (h + 1) * half]
        real += times(p_r, f_r) + times(p_i, f_i)
        imag += times(p_i, f_r) + times(p_r, -f_i)
    l_r, l_i = col_level(ids, col_off, jr, cw_ref[...], width * subs, length)
    for z, value in enumerate((real * l_r + imag * l_i, imag * l_r - real * l_i)):
        for s in range(subs):
            for chunk in range(width // LANES):
                image[z, chunk, jnp.bitwise_xor(s, ids[1])] = value[
                    s * block : (s + 1) * block, chunk * LANES : (chunk + 1) * LANES
                ]


def sort_rows(image, off, write):
    _, chunks, subs, block, _ = image.shape
    tile_rows = block // TS
    q2 = SG // TS

    def k1_of(q1):
        return jnp.bitwise_and(off + q1, TS - 1)

    if tile_rows == 4:

        def per_pair(pair, carry):
            rows = pl.ds(pl.multiple_of(pair * 8, 8), 8)
            for z in range(2):
                for chunk in range(chunks):
                    for s in range(0, subs, 4):
                        v = [image[z, chunk, s + n, rows, :] for n in range(4)]
                        pairs = [exchange(v[0], v[1]), exchange(v[2], v[3])]
                        for n in range(2):
                            value = jnp.concatenate([pairs[0][n], pairs[1][n]], axis=0)
                            write(k1_of(2 * pair + n), z * q2 + s * tile_rows, chunk, value)
            return carry

        lax.fori_loop(0, TS // 2, per_pair, 0)
    else:
        assert tile_rows == 1
        for q1 in range(TS):
            for z in range(2):
                for chunk in range(chunks):
                    value = jnp.concatenate(
                        [image[z, chunk, s, q1 : q1 + 1, :] for s in range(subs)], axis=0
                    )
                    write(k1_of(q1), z * q2, chunk, value)


def cols_backward_kernel(
    ids, row_off, col_off, a_ref, b_ref, fr_ref, fi_ref, cw_ref, out_ref, image, *, length
):
    jr = 2 * pl.program_id(0)
    columns_back(
        ids, jr, col_off, (a_ref.at[0], b_ref.at[0]), fr_ref, fi_ref, cw_ref, image, length
    )

    def write(k1, row, chunk, value):
        lanes = slice(chunk * LANES, (chunk + 1) * LANES)
        out_ref[k1, row : row + value.shape[0], lanes] = value.astype(BF16)

    sort_rows(image, row_off[jnp.bitwise_xor(ids[0], jr)], write)


def image_scratch(width, subs):
    return pltpu.VMEM((2, width // LANES, subs, SG // subs, LANES), F32)


def cols_backward(ids, row_off, col_off, halves, tables, col_window, length):
    used, subs, rows, half = halves[0].shape
    width = col_window.shape[1]
    part = 2 * (SG // TS)
    return pl.pallas_call(
        partial(cols_backward_kernel, length=length),
        grid_spec=pltpu.PrefetchScalarGridSpec(
            num_scalar_prefetch=3,
            grid=(used,),
            in_specs=[pl.BlockSpec((1, subs, rows, half), lambda j, *_: (j, 0, 0, 0))] * 2
            + [pl.BlockSpec((width, SG), lambda j, m, *_: (m[1], 0))] * 2
            + [pl.BlockSpec((1, width), lambda j, *_: (0, 0))],
            out_specs=pl.BlockSpec((TS, part, width), lambda j, *_: (0, j, 0)),
            scratch_shapes=[image_scratch(width, subs)],
        ),
        out_shape=jax.ShapeDtypeStruct((TS, used * part, width), BF16),
        compiler_params=pltpu.CompilerParams(vmem_limit_bytes=VMEM_LIMIT),
        cost_estimate=pl.CostEstimate(
            flops=5_000_000_000, bytes_accessed=6 << 20, transcendentals=0
        ),
        name="cols_backward",
    )(ids, row_off, col_off, *halves, *tables, col_window)


def transposed_kernel(ids, row_off, tr_ref, ti_ref, out_ref, mat):
    part = 2 * (SG // TS)

    def write(k1, place, block):
        mat[k1, place * part : (place + 1) * part, :] = block.astype(F32)

    fill_matrix(ids, row_off, (tr_ref, ti_ref), write, row_off.shape[0])

    def per_k1(k1, carry):
        out_ref[k1] = mat[k1].T.astype(BF16)
        return carry

    lax.fori_loop(0, TS, per_k1, 0)


def transposed_matrix(ids, row_off, tables):
    count = row_off.shape[0]
    quarter = tables[0].shape[2]
    part = 2 * (SG // TS)
    vmem = pl.BlockSpec(memory_space=pltpu.VMEM)
    smem = pl.BlockSpec(memory_space=pltpu.SMEM)
    return pl.pallas_call(
        transposed_kernel,
        in_specs=[smem] * 2 + [vmem] * 2,
        out_specs=vmem,
        out_shape=jax.ShapeDtypeStruct((TS, 2 * quarter, count * part), BF16),
        scratch_shapes=[pltpu.VMEM((TS, count * part, 2 * quarter), F32)],
        compiler_params=pltpu.CompilerParams(vmem_limit_bytes=VMEM_LIMIT),
        cost_estimate=pl.CostEstimate(
            flops=5_000_000_000, bytes_accessed=5 << 20, transcendentals=0
        ),
        name="transposed_matrix",
    )(ids, row_off, *tables)


def backward_kernel(
    ids,
    row_off,
    col_off,
    a_ref,
    b_ref,
    fr_ref,
    fi_ref,
    cw_ref,
    even_ref,
    mat_ref,
    rw_ref,
    out_ref,
    image,
    odd,
    middle,
    spread,
):
    used = row_off.shape[0] // 2
    quarter = mat_ref.shape[1] // 2
    block = even_ref.shape[2]
    part = 2 * (SG // TS)
    step = pl.program_id(0)

    @pl.when(step == 0)
    def _():
        spread_window(rw_ref, spread)

    @pl.when(step < used)
    def _():
        jr = 2 * step + 1
        columns_back(
            ids,
            jr,
            col_off,
            (a_ref.at[0], b_ref.at[0]),
            fr_ref,
            fi_ref,
            cw_ref,
            image,
            quarter * TS,
        )

        def write(k1, row, chunk, value):
            rows = pl.ds(pl.multiple_of(step * part + row, 16), value.shape[0])
            odd[k1, rows, chunk * LANES : (chunk + 1) * LANES] = value.astype(BF16)

        sort_rows(image, row_off[jnp.bitwise_xor(ids[0], jr)], write)

    @pl.when(step >= used)
    def _():
        lanes = pl.ds(pl.multiple_of((step - used) * block, block), block)

        def per_k1(k1, carry):
            rows = jnp.concatenate([even_ref[k1], odd[k1, :, lanes]], axis=0)
            middle[k1] = jnp.dot(mat_ref[k1], rows, preferred_element_type=F32)
            return carry

        lax.fori_loop(0, TS, per_k1, 0, unroll=4)

        def butterfly(chunk, carry):
            n2 = pl.multiple_of(chunk * 16, 16)
            for lane in range(0, block, LANES):
                values = [
                    tuple(
                        middle[
                            k1,
                            pl.ds(pl.multiple_of(z * quarter + n2, 16), 16),
                            lane : lane + LANES,
                        ]
                        for z in range(2)
                    )
                    for k1 in range(TS)
                ]
                for n1, pair in enumerate(dft16(values, 1)):
                    rows = pl.ds(pl.multiple_of(n1 * quarter + n2, 16), 16)
                    window = spread[rows, :]
                    for z in range(2):
                        out_ref[z, rows, lane : lane + LANES] = (pair[z] * window).astype(BF16)
            return carry

        lax.fori_loop(0, quarter // 16, butterfly, 0)


def backward(ids, row_off, col_off, halves, tables, col_window, even, matrix, row_window):
    used, subs, rows, half = halves[0].shape
    _, depth, width = even.shape
    length = row_window.size
    quarter = length // TS
    block = min(2 * LANES, width)

    def early(c, *_):
        return (jnp.minimum(c, used - 1), 0, 0, 0)

    def late(c, *_):
        return (0, 0, jnp.maximum(c - used, 0))

    return pl.pallas_call(
        backward_kernel,
        grid_spec=pltpu.PrefetchScalarGridSpec(
            num_scalar_prefetch=3,
            grid=(used + width // block,),
            in_specs=[pl.BlockSpec((1, subs, rows, half), early)] * 2
            + [pl.BlockSpec((width, SG), lambda c, m, *_: (m[1], 0))] * 2
            + [
                pl.BlockSpec((1, width), lambda c, *_: (0, 0)),
                pl.BlockSpec((TS, depth, block), late),
                pl.BlockSpec((TS, 2 * quarter, 2 * depth), lambda c, *_: (0, 0, 0)),
                pl.BlockSpec((length // LANES, LANES), lambda c, *_: (0, 0)),
            ],
            out_specs=pl.BlockSpec((2, length, block), late),
            scratch_shapes=[
                image_scratch(width, subs),
                pltpu.VMEM((TS, depth, width), BF16),
                pltpu.VMEM((TS, 2 * quarter, block), F32),
                pltpu.VMEM((length, LANES), F32),
            ],
        ),
        out_shape=jax.ShapeDtypeStruct((2, length, width), BF16),
        compiler_params=pltpu.CompilerParams(vmem_limit_bytes=VMEM_LIMIT),
        name="backward",
    )(ids, row_off, col_off, *halves, *tables, col_window, even, matrix, row_window)


def swap(value, axis, bit):
    return lax.ppermute(value, axis, [(i, i ^ bit) for i in range(lax.axis_size(axis))])


def bits_of(axis):
    return [(axis, 1 << n) for n in range(lax.axis_size(axis).bit_length() - 1)]


def orders():
    facet, sub = bits_of("facet")[1:], bits_of("sub")
    rest = facet[1:] + sub[1:]
    return facet[:1] + sub[:1] + rest, sub[:1] + facet[:1] + rest


def dimensions():
    return bits_of("facet")[:0:-1] + bits_of("sub")[::-1]


def sum_blocks(kept, sent):
    result = []
    for kept_half, sent_half, order in zip(kept, sent, orders()):
        value = kept_half + swap(sent_half, "facet", 1)
        dims = dimensions()
        value = value.reshape((2,) * len(dims) + value.shape[2:])
        for step in order:
            at = dims.index(step)
            dims.remove(step)
            mine = lax.index_in_dim(value, 0, at, keepdims=False)
            arrived = swap(lax.index_in_dim(value, 1, at, keepdims=False), *step)
            value = mine + arrived if dims else None
        result += [mine, arrived]
    return result


def gather_blocks(halves, facet_count, sub_count):
    result = []
    for value, order in zip(halves, orders()):
        shape = value.shape
        have = []
        every = dimensions()
        for step in order[::-1]:
            at = len([d for d in every if d in have and every.index(d) < every.index(step)])
            have.append(step)
            value = jnp.stack([value, swap(value, *step)], axis=at)
        value = value.reshape((facet_count // 2, sub_count) + shape)
        result.append((value, swap(value, "facet", 1)))
    return result


def per_device(
    facet_strips,
    row_window,
    col_window,
    row_offsets,
    col_offsets,
    tile_owner,
    measured,
    vis_weight,
    uvw_pixels,
    vis_count,
):
    sub_count = lax.axis_size("sub")
    facet_count = lax.axis_size("facet")
    _, length, strip_width = facet_strips.shape
    full_width = strip_width * sub_count
    ids = jnp.stack([lax.axis_index("facet"), lax.axis_index("sub")]).astype(jnp.int32)
    row_win = row_window.reshape(length // LANES, LANES)
    col_win = col_window.reshape(1, strip_width)
    row_consts = row_tables(length)
    col_consts = column_tables(full_width)

    spectrum, *sent = forward(
        ids,
        row_offsets,
        col_offsets,
        facet_strips,
        row_win,
        col_win,
        row_consts,
        col_consts,
        sub_count,
    )
    spectrum = spectrum.reshape(facet_count // 2, 2, SG, strip_width)
    kept = cols_forward(ids, spectrum, col_consts, sub_count)

    owners = tile_owner.reshape(-1)
    slots = measured.shape[2]
    capacity = slots // sub_count
    padded = -(-capacity // GROUP) * GROUP
    groups = padded // GROUP

    def per_slot(value):
        if padded == capacity:
            return value
        value = value.reshape((sub_count, capacity) + value.shape[1:])
        value = jnp.pad(value, ((0, 0), (0, padded - capacity)) + ((0, 0),) * (value.ndim - 2))
        return value.reshape((sub_count * padded,) + value.shape[2:])

    visits = vis_weight.shape[3]
    live = jnp.arange(visits, dtype=jnp.int32)[None, :] < vis_count[0, 0][:, None]
    weights = per_slot(jnp.where(live, vis_weight[0, 0], 0.0))
    values = jnp.transpose(per_slot(measured[0, 0]), (1, 0, 2))
    pixels = jnp.transpose(per_slot(uvw_pixels[0, 0]), (1, 0, 2))

    parts = sum_blocks(kept, sent)
    row_kernels, col_kernels = kernels(pixels, 4)
    matrix = transposed_matrix(ids, row_offsets, row_consts)
    routed = route(ids, owners, parts, sub_count, groups)
    outgoing, where = routed[:-1], routed[-1]
    arrived = [outgoing[0]] + [swap(outgoing[r], "sub", r) for r in range(1, sub_count)]
    returned = []
    for first in range(0, sub_count, 2):
        sources = jnp.stack([ids[1] ^ first, ids[1] ^ (first + 1)])
        answered = visit(
            sources, arrived[first : first + 2], values, weights, row_kernels, col_kernels
        )
        returned += [
            swap(value, "sub", first + n) if first + n else value
            for n, value in enumerate(answered)
        ]
    halves = unroute(where, returned, 2 * SG // sub_count)

    (a_own, a_other), (b_own, b_other) = gather_blocks(halves, facet_count, sub_count)
    even = cols_backward(
        ids, row_offsets, col_offsets, (a_own, b_own), col_consts, col_win, length
    )
    return backward(
        ids,
        row_offsets,
        col_offsets,
        (a_other, b_other),
        col_consts,
        col_win,
        even,
        matrix,
        row_win,
    )


def solution(mesh):
    in_specs = (
        P(None, "facet", "sub"),
        P(),
        P("sub"),
        P(),
        P(),
        P("sub", "facet", None, None),
        P("facet", "sub", None, None, None),
        P("facet", "sub", None, None),
        P("facet", "sub", None, None, None),
        P("facet", "sub", None),
    )
    out_specs = P(None, "facet", "sub")
    return jax.shard_map(
        per_device, mesh=mesh, in_specs=in_specs, out_specs=out_specs, check_vma=False
    )
```

time: 249 us -> 201 us (0.81)
  Pallas kernels: 131 us -> 95.5 us
  other arithmetic: 12.5 us -> 8.2 us
  waiting for transfers between devices: 47.5 us -> 43.7 us
    pallas_call x6 -> x9, Pallas kernels: 106 us -> 82.2 us  [the longest x1 22.4 us: forward(): pl.pallas_call(forward_kernel, grid_spec=pltpu.PrefetchScalarGridSpec(num...]
    pallas_call x2 -> x1, Pallas kernels: 17.4 us -> 6.33 us  [cols_forward(): pl.pallas_call(cols_forward_kernel, grid_spec=pltpu.PrefetchScalarGridSpe...]
    ppermute x34, waiting for transfers between devices: 47.5 us -> 43.7 us  [swap(): lax.ppermute(value, axis, [(i, i ^ bit) for i in range(lax.axis_size(axis...]
    broadcast_in_dim x1 -> x0, local copies, waits for them, and re-layouts: 2.62 us -> none  [per_device(): window = jnp.broadcast_to(row_window[:, None], (length, LANES))]
    another operation x3 -> x5, other arithmetic: 5.23 us -> 3.1 us  [the longest x4 2.43 us: per_device(): sources = jnp.stack([ids[1] ^ first, ids[1] ^ first + 1])]
    unnamed x56 -> x50, local copies, waits for them, and re-layouts: 3.79 us -> 5.29 us
  transfers between devices with their start and end apart: 34 -> 34, of which waited for: 16 -> 14; matrix products, arithmetic and copies ran while one was open for 4% -> 6% of each run, Pallas kernels for 10% -> 22%
where the time goes in v2:
time: 201 us
  Pallas kernels  95.5 us (48%)
  starting transfers between devices  45.2 us (22%)
  waiting for transfers between devices  43.7 us (22%)
  other arithmetic  8.2 us (4%)
  local copies, waits for them, and re-layouts  7.71 us (4%)
    ppermute x34, starting transfers between devices, swap(): lax.ppermute(value, axis, [(i, i ^ bit) for i in range(lax.axis_size(axis...  45.2 us
    ppermute x34, waiting for transfers between devices, swap(): lax.ppermute(value, axis, [(i, i ^ bit) for i in range(lax.axis_size(axis...  43.7 us
    pallas_call x1, Pallas kernels, forward(): pl.pallas_call(forward_kernel, grid_spec=pltpu.PrefetchScalarGridSpec(num...  22.4 us
    pallas_call x1, Pallas kernels, backward(): pl.pallas_call(backward_kernel, grid_spec=pltpu.PrefetchScalarGridSpec(nu...  21.4 us
    pallas_call x4, Pallas kernels, visit(): pl.pallas_call(visit_kernel, grid_spec=pltpu.PrefetchScalarGridSpec(num_s...  18.5 us
    pallas_call x1, Pallas kernels, cols_backward(): pl.pallas_call(partial(cols_backward_kernel, length=length), grid_spec=pl...  6.82 us
    pallas_call x1, Pallas kernels, transposed_matrix(): pl.pallas_call(transposed_kernel, in_specs=[smem] * 2 + [vmem] * 2, out_s...  6.65 us
    pallas_call x1, Pallas kernels, kernels(): pl.pallas_call(kernels_kernel, grid=(steps,), in_specs=[pl.BlockSpec((3,...  6.49 us
  transfers between devices with their start and end apart: 34, of which 14 were waited for; matrix products, arithmetic and copies ran while one was open for 6% of the time, Pallas kernels for 22%

profile of v2, /device:TPU:0, one launch (start us, length us, event | category | flops | bytes accessed | tf_op | source)
XLA Modules:
  0.0 200.7 jit_solution(8572248789646054175)
XLA Ops:
  0.7 22.4 %forward.1 = (bf16[2,2,16,32,512]{4,3,2,1,0:T(8,128)(2,1)}, bf16[2,8,128,256]{3,2,1,0:T(8,128)(2,1)}, bf16[2,8,128,256]{3,2,1,0:T(8,128)(2,1)}) custom-call(s32[2]{0:T(128)} %pad_add_fusion.ids, s32[4]{0:T(128)} %row_off.7, s32[4]{0:T(128)} %col_off.5, bf16[2,4096,512]{2,1,0:T(8,128)(2,1)} %x_ref.1, f32[32,128]{1,0:T(8,128)} %bitcast.109, ...), custom_call_target="tpu_custom_call" | custom-call | flops 12000000000 | bytes 16777216 | tf_op jit(solution)/shard_map/forward/pallas_call | solution.py:318
  23.6 6.5 %kernels.1 = (bf16[64,2,128,128]{3,2,1,0:T(8,128)(2,1)}, bf16[64,128,256]{2,1,0:T(8,128)(2,1)}) custom-call(s32[3,512,128]{2,1,0:T(8,128)} %bitcast.116), custom_call_target="tpu_custom_call" | custom-call | flops 6000000000 | bytes 9437184 | tf_op jit(solution)/shard_map/kernels/pallas_call | solution.py:558
  30.1 6.3 %cols_forward.1 = (bf16[2,8,128,256]{3,2,1,0:T(8,128)(2,1)}, bf16[2,8,128,256]{3,2,1,0:T(8,128)(2,1)}) custom-call(s32[2]{0:T(128)} %pad_add_fusion.ids, bf16[2,2,512,512]{3,2,1,0:T(8,128)(2,1)} %bitcast.117, bf16[4096,512]{1,0:T(8,128)(2,1)} %constant.36.clone.fr_ref, bf16[4096,512]{1,0:T(8,128)(2,1)} %constant.37.clone.fi_ref), custom_call_target="tpu_custom_call" | custom-call | flops 4000000000 | bytes 6291456 | tf_op jit(solution)/shard_map/cols_forward/pallas_call | solution.py:368
  39.0 3.0 %collective-permute-start.1 = (bf16[2,2,2,128,256]{4,3,0,1,2:T(8,128)(2,1)}, bf16[2,2,2,128,256]{4,3,0,1,2:T(8,128)(2,1)S(1)}, u32[]{:S(2)}, u32[]{:S(2)}) collective-permute-start(bf16[2,2,2,128,256]{4,3,0,1,2:T(8,128)(2,1)} %copy.23), channel_id=1, source_target_pairs={{0,16},{8,24},{16,0},{24,8},{1,17},{9,25},{17,1},{25,9},{2,18},{10... | collective-permute-start | bytes 1572872 | tf_op jit(solution)/shard_map/ppermute | solution.py:920
  46.0 1.9 copy.40
  47.9 6.4 %collective-permute-done.1 = bf16[2,2,2,128,256]{4,3,0,1,2:T(8,128)(2,1)S(1)} collective-permute-done((bf16[2,2,2,128,256]{4,3,0,1,2:T(8,128)(2,1)}, bf16[2,2,2,128,256]{4,3,0,1,2:T(8,128)(2,1)S(1)}, u32[]{:S(2)}, u32[]{:S(2)}) %collective-permute-start.1) | collective-permute-done | bytes 524320 | tf_op jit(solution)/shard_map/ppermute | solution.py:920
  56.1 2.1 %collective-permute-done.6 = bf16[2,2,2,128,256]{4,3,1,2,0:T(8,128)(2,1)S(1)} collective-permute-done((bf16[2,2,2,128,256]{4,3,1,2,0:T(8,128)(2,1)S(1)}, bf16[2,2,2,128,256]{4,3,1,2,0:T(8,128)(2,1)S(1)}, u32[]{:S(2)}, u32[]{:S(2)}) %collective-permute-start.6) | collective-permute-done | bytes 524320 | tf_op jit(solution)/shard_map/ppermute | solution.py:920
  58.4 4.6 %collective-permute-done.2 = bf16[2,2,128,256]{3,2,0,1:T(8,128)(2,1)S(1)} collective-permute-done((bf16[2,2,128,256]{3,2,0,1:T(8,128)(2,1)S(1)}, bf16[2,2,128,256]{3,2,0,1:T(8,128)(2,1)S(1)}, u32[]{:S(2)}, u32[]{:S(2)}) %collective-permute-start.2) | collective-permute-done | bytes 262176 | tf_op jit(solution)/shard_map/ppermute | solution.py:920
  66.6 2.7 %collective-permute-done.3 = bf16[2,128,256]{2,1,0:T(8,128)(2,1)S(1)} collective-permute-done((bf16[2,128,256]{2,1,0:T(8,128)(2,1)S(1)}, bf16[2,128,256]{2,1,0:T(8,128)(2,1)S(1)}, u32[]{:S(2)}, u32[]{:S(2)}) %collective-permute-start.3) | collective-permute-done | bytes 131104 | tf_op jit(solution)/shard_map/ppermute | solution.py:920
  69.9 2.5 %collective-permute-start.4 = (bf16[128,256]{1,0:T(8,128)(2,1)S(1)}, bf16[128,256]{1,0:T(8,128)(2,1)S(1)}, u32[]{:S(2)}, u32[]{:S(2)}) collective-permute-start(bf16[128,256]{1,0:T(8,128)(2,1)S(1)} %get-tuple-element.73), channel_id=1, source_target_pairs={{0,4},{1,5},{2,6},{3,7},{4,0},{5,1},{6,2},{7,3},{8,12},{9,13},{10,... | collective-permute-start | bytes 196616 | tf_op jit(solution)/shard_map/ppermute | solution.py:920
  76.4 1.8 collective-permute-done.9.refs_3_
  78.9 4.1 %route.1 = (bf16[8,32,128]{2,1,0:T(8,128)(2,1)}, bf16[8,32,128]{2,1,0:T(8,128)(2,1)}, bf16[8,32,128]{2,1,0:T(8,128)(2,1)}, bf16[8,32,128]{2,1,0:T(8,128)(2,1)}, ...) custom-call(s32[2]{0:T(128)} %pad_add_fusion.ids, ...), custom_call_target="tpu_custom_call" | custom-call | tf_op jit(solution)/shard_map/route/pallas_call | solution.py:436
  83.0 2.7 %collective-permute-start.20 = (bf16[8,32,128]{2,1,0:T(8,128)(2,1)}, bf16[8,32,128]{2,1,0:T(8,128)(2,1)S(1)}, u32[]{:S(2)}, u32[]{:S(2)}) collective-permute-start(bf16[8,32,128]{2,1,0:T(8,128)(2,1)} %get-tuple-element.51), channel_id=1, source_target_pairs={{0,6},{1,7},{2,4},{3,5},{4,2},{5,3},{6,0},{7,1},{8,14},{9,15},{10,... | collective-permute-start | bytes 196616 | tf_op jit(solution)/shard_map/ppermute | solution.py:920
  85.7 2.1 %collective-permute-start.21 = (bf16[8,32,128]{2,1,0:T(8,128)(2,1)}, bf16[8,32,128]{2,1,0:T(8,128)(2,1)S(1)}, u32[]{:S(2)}, u32[]{:S(2)}) collective-permute-start(bf16[8,32,128]{2,1,0:T(8,128)(2,1)} %get-tuple-element.52), channel_id=1, source_target_pairs={{0,7},{1,6},{2,5},{3,4},{4,3},{5,2},{6,1},{7,0},{8,15},{9,14},{10,... | collective-permute-start | bytes 196616 | tf_op jit(solution)/shard_map/ppermute | solution.py:920
  88.9 3.0 %collective-permute-start.13 = (bf16[8,32,128]{2,1,0:T(8,128)(2,1)}, bf16[8,32,128]{2,1,0:T(8,128)(2,1)S(1)}, u32[]{:S(2)}, u32[]{:S(2)}) collective-permute-start(bf16[8,32,128]{2,1,0:T(8,128)(2,1)} %get-tuple-element.44), channel_id=1, source_target_pairs={{0,3},{1,2},{2,1},{3,0},{4,7},{5,6},{6,5},{7,4},{8,11},{9,10},{10,... | collective-permute-start | bytes 196616 | tf_op jit(solution)/shard_map/ppermute | solution.py:920
  94.8 4.5 %visit.7 = (bf16[8,32,128]{2,1,0:T(8,128)(2,1)}, bf16[8,32,128]{2,1,0:T(8,128)(2,1)}) custom-call(s32[2]{0:T(128)} %pad_add_fusion.4.sources, bf16[8,32,128]{2,1,0:T(8,128)(2,1)} %copy-done.20, bf16[8,32,128]{2,1,0:T(8,128)(2,1)} %copy-done.21, f32[2,512,128]{2,1,0:T(8,128)} %bitcast.95, f32[512,128]{1,0:T(8,128)} %bitcast_select_fusion.refs_3_, ...), custom_call_target="tpu_custom_call" | custom-call | flops 3600000000 | bytes 2621440 | tf_op jit(solution)/shard_map/visit/pallas_call | solution.py:630
  99.3 2.7 %collective-permute-start.22 = (bf16[8,32,128]{2,1,0:T(8,128)(2,1)}, bf16[8,32,128]{2,1,0:T(8,128)(2,1)S(1)}, u32[]{:S(2)}, u32[]{:S(2)}) collective-permute-start(bf16[8,32,128]{2,1,0:T(8,128)(2,1)} %get-tuple-element.53), channel_id=1, source_target_pairs={{0,6},{1,7},{2,4},{3,5},{4,2},{5,3},{6,0},{7,1},{8,14},{9,15},{10,... | collective-permute-start | bytes 196616 | tf_op jit(solution)/shard_map/ppermute | solution.py:920
  102.0 2.1 %collective-permute-start.23 = (bf16[8,32,128]{2,1,0:T(8,128)(2,1)}, bf16[8,32,128]{2,1,0:T(8,128)(2,1)S(1)}, u32[]{:S(2)}, u32[]{:S(2)}) collective-permute-start(bf16[8,32,128]{2,1,0:T(8,128)(2,1)} %get-tuple-element.54), channel_id=1, source_target_pairs={{0,7},{1,6},{2,5},{3,4},{4,3},{5,2},{6,1},{7,0},{8,15},{9,14},{10,... | collective-permute-start | bytes 196616 | tf_op jit(solution)/shard_map/ppermute | solution.py:920
  104.2 4.5 %visit.6 = (bf16[8,32,128]{2,1,0:T(8,128)(2,1)}, bf16[8,32,128]{2,1,0:T(8,128)(2,1)}) custom-call(s32[2]{0:T(128)} %pad_add_fusion.3.sources, bf16[8,32,128]{2,1,0:T(8,128)(2,1)} %copy-done.22, bf16[8,32,128]{2,1,0:T(8,128)(2,1)} %copy-done.23, f32[2,512,128]{2,1,0:T(8,128)} %bitcast.96, f32[512,128]{1,0:T(8,128)} %bitcast_select_fusion.refs_3_, ...), custom_call_target="tpu_custom_call" | custom-call | flops 3600000000 | bytes 2621440 | tf_op jit(solution)/shard_map/visit/pallas_call | solution.py:630
  108.8 2.9 %collective-permute-start.19 = (bf16[8,32,128]{2,1,0:T(8,128)(2,1)}, bf16[8,32,128]{2,1,0:T(8,128)(2,1)S(1)}, u32[]{:S(2)}, u32[]{:S(2)}) collective-permute-start(bf16[8,32,128]{2,1,0:T(8,128)(2,1)} %get-tuple-element.50), channel_id=1, source_target_pairs={{0,5},{1,4},{2,7},{3,6},{4,1},{5,0},{6,3},{7,2},{8,13},{9,12},{10,... | collective-permute-start | bytes 196616 | tf_op jit(solution)/shard_map/ppermute | solution.py:920
  111.7 4.5 %visit.5 = (bf16[8,32,128]{2,1,0:T(8,128)(2,1)}, bf16[8,32,128]{2,1,0:T(8,128)(2,1)}) custom-call(s32[2]{0:T(128)} %pad_add_fusion.2.sources, bf16[8,32,128]{2,1,0:T(8,128)(2,1)} %copy-done.17, bf16[8,32,128]{2,1,0:T(8,128)(2,1)} %copy-done.18, f32[2,512,128]{2,1,0:T(8,128)} %bitcast.97, f32[512,128]{1,0:T(8,128)} %bitcast_select_fusion.refs_3_, ...), custom_call_target="tpu_custom_call" | custom-call | flops 3600000000 | bytes 2621440 | tf_op jit(solution)/shard_map/visit/pallas_call | solution.py:630
  117.2 4.9 %visit.4 = (bf16[8,32,128]{2,1,0:T(8,128)(2,1)}, bf16[8,32,128]{2,1,0:T(8,128)(2,1)}) custom-call(s32[2]{0:T(128)} %pad_add_fusion.1.sources, bf16[8,32,128]{2,1,0:T(8,128)(2,1)} %get-tuple-element.37.refs_0_, bf16[8,32,128]{2,1,0:T(8,128)(2,1)} %copy-done.16, f32[2,512,128]{2,1,0:T(8,128)} %bitcast.98, f32[512,128]{1,0:T(8,128)} %bitcast_select_fusion.refs_3_, ...), custom_call_target="tpu_custom_call" | custom-call | flops 3600000000 | bytes 2621440 | tf_op jit(solution)/shard_map/visit/pallas_call | solution.py:630
  122.1 2.1 %collective-permute-start.15 = (bf16[8,32,128]{2,1,0:T(8,128)(2,1)S(1)}, bf16[8,32,128]{2,1,0:T(8,128)(2,1)S(1)}, u32[]{:S(2)}, u32[]{:S(2)}) collective-permute-start(bf16[8,32,128]{2,1,0:T(8,128)(2,1)S(1)} %copy-done.19), channel_id=1, source_target_pairs={{0,3},{1,2},{2,1},{3,0},{4,7},{5,6},{6,5},{7,4},{8,11},{9,10},{10,... | collective-permute-start | bytes 196616 | tf_op jit(solution)/shard_map/ppermute | solution.py:920
  124.8 2.5 %collective-permute-done.15.refs_3_ = bf16[8,32,128]{2,1,0:T(8,128)(2,1)S(1)} collective-permute-done((bf16[8,32,128]{2,1,0:T(8,128)(2,1)S(1)}, bf16[8,32,128]{2,1,0:T(8,128)(2,1)S(1)}, u32[]{:S(2)}, u32[]{:S(2)}) %collective-permute-start.15) | collective-permute-done | bytes 65568 | tf_op jit(solution)/shard_map/ppermute | solution.py:920
  129.3 2.9 %unroute.1 = (bf16[128,256]{1,0:T(8,128)(2,1)}, bf16[128,256]{1,0:T(8,128)(2,1)}) custom-call(s32[128]{0:T(128)} %get-tuple-element.36.where_ref, bf16[8,32,128]{2,1,0:T(8,128)(2,1)} %get-tuple-element.41.refs_0_, bf16[8,32,128]{2,1,0:T(8,128)(2,1)} %copy-done.12, bf16[8,32,128]{2,1,0:T(8,128)(2,1)} %copy-done.10, bf16[8,32,128]{2,1,0:T(8,128)(2,1)} %copy-done.11, ...), custom_call_target="tpu_custom_call" | custom-call | tf_op jit(solution)/shard_map/unroute/pallas_call | solution.py:485
  135.2 3.2 %collective-permute-done.29 = bf16[128,256]{1,0:T(8,128)(2,1)S(1)} collective-permute-done((bf16[128,256]{1,0:T(8,128)(2,1)}, bf16[128,256]{1,0:T(8,128)(2,1)S(1)}, u32[]{:S(2)}, u32[]{:S(2)}) %collective-permute-start.29) | collective-permute-done | bytes 65568 | tf_op jit(solution)/shard_map/ppermute | solution.py:920
  142.2 2.0 %collective-permute-done.30 = bf16[2,128,256]{2,1,0:T(8,128)(2,1)S(1)} collective-permute-done((bf16[2,128,256]{2,1,0:T(8,128)(2,1)S(1)}, bf16[2,128,256]{2,1,0:T(8,128)(2,1)S(1)}, u32[]{:S(2)}, u32[]{:S(2)}) %collective-permute-start.30) | collective-permute-done | bytes 131104 | tf_op jit(solution)/shard_map/ppermute | solution.py:920
  147.2 6.3 %collective-permute-done.31 = bf16[2,2,128,256]{3,2,0,1:T(8,128)(2,1)S(1)} collective-permute-done((bf16[2,2,128,256]{3,2,0,1:T(8,128)(2,1)S(1)}, bf16[2,2,128,256]{3,2,0,1:T(8,128)(2,1)S(1)}, u32[]{:S(2)}, u32[]{:S(2)}) %collective-permute-start.31) | collective-permute-done | bytes 262176 | tf_op jit(solution)/shard_map/ppermute | solution.py:920
  154.6 8.2 %collective-permute-done.32 = bf16[2,2,2,128,256]{4,3,1,2,0:T(8,128)(2,1)S(1)} collective-permute-done((bf16[2,2,2,128,256]{4,3,1,2,0:T(8,128)(2,1)S(1)}, bf16[2,2,2,128,256]{4,3,1,2,0:T(8,128)(2,1)S(1)}, u32[]{:S(2)}, u32[]{:S(2)}) %collective-permute-start.32) | collective-permute-done | bytes 524320 | tf_op jit(solution)/shard_map/ppermute | solution.py:920
  163.8 6.7 %transposed_matrix.1.mat_ref = bf16[16,512,256]{2,1,0:T(8,128)(2,1)} custom-call(s32[2]{0:T(128)} %pad_add_fusion.ids, s32[4]{0:T(128)} %row_off.7, f32[16,32,256]{2,1,0:T(8,128)} %constant.34.clone.tr_ref, f32[16,32,256]{2,1,0:T(8,128)} %constant.35.clone.ti_ref), custom_call_target="tpu_custom_call" | custom-call | flops 5000000000 | bytes 5242880 | tf_op jit(solution)/shard_map/transposed_matrix/pallas_call | solution.py:781
  170.5 6.8 %cols_backward.1.even_ref = bf16[16,128,512]{2,1,0:T(8,128)(2,1)} custom-call(s32[2]{0:T(128)} %pad_add_fusion.ids, s32[4]{0:T(128)} %row_off.7, s32[4]{0:T(128)} %col_off.5, bf16[2,8,128,256]{3,2,1,0:T(8,128)(2,1)} %copy-done.4, bf16[2,8,128,256]{3,2,1,0:T(8,128)(2,1)} %bitcast.94, bf16[4096,512]{1,0:T(8,128)(2,1)} %constant.36.clone.fr_ref, ...), custom_call_target="tpu_custom_call" | custom-call | flops 5000000000 | bytes 6291456 | tf_op jit(solution)/shard_map/cols_backward/pallas_call | solution.py:740
  179.4 21.4 %backward.1 = bf16[2,4096,512]{2,1,0:T(8,128)(2,1)} custom-call(s32[2]{0:T(128)} %pad_add_fusion.ids, s32[4]{0:T(128)} %row_off.7, s32[4]{0:T(128)} %col_off.5, bf16[2,8,128,256]{3,2,1,0:T(8,128)(2,1)} %copy-done.1, bf16[2,8,128,256]{3,2,1,0:T(8,128)(2,1)} %copy-done.2, bf16[4096,512]{1,0:T(8,128)(2,1)} %constant.36.clone.fr_ref, ...), custom_call_target="tpu_custom_call" | custom-call | tf_op jit(solution)/shard_map/backward/pallas_call | solution.py:892
  (132 shorter events, 39.9 us)
Async XLA Ops:
  23.0 13.4 %collective-permute-start = (bf16[2,8,128,256]{3,2,1,0:T(8,128)(2,1)}, bf16[2,8,128,256]{3,2,1,0:T(8,128)(2,1)S(1)}, u32[]{:S(2)}, u32[]{:S(2)}) collective-permute-start(bf16[2,8,128,256]{3,2,1,0:T(8,128)(2,1)} %get-tuple-element.33), channel_id=1, source_target_pairs={{0,8},{8,0},{16,24},{24,16},{1,9},{9,1},{17,25},{25,17},{2,10},{10... | collective-permute-start | bytes 3145736 | tf_op jit(solution)/shard_map/ppermute | solution.py:920
  23.5 19.8 %collective-permute-start.5 = (bf16[2,8,128,256]{3,2,1,0:T(8,128)(2,1)}, bf16[2,8,128,256]{3,2,1,0:T(8,128)(2,1)S(1)}, u32[]{:S(2)}, u32[]{:S(2)}) collective-permute-start(bf16[2,8,128,256]{3,2,1,0:T(8,128)(2,1)} %get-tuple-element.35), channel_id=1, source_target_pairs={{0,8},{8,0},{16,24},{24,16},{1,9},{9,1},{17,25},{25,17},{2,10},{10... | collective-permute-start | bytes 3145736 | tf_op jit(solution)/shard_map/ppermute | solution.py:920
  39.0 15.3 %collective-permute-start.1 = (bf16[2,2,2,128,256]{4,3,0,1,2:T(8,128)(2,1)}, bf16[2,2,2,128,256]{4,3,0,1,2:T(8,128)(2,1)S(1)}, u32[]{:S(2)}, u32[]{:S(2)}) collective-permute-start(bf16[2,2,2,128,256]{4,3,0,1,2:T(8,128)(2,1)} %copy.23), channel_id=1, source_target_pairs={{0,16},{8,24},{16,0},{24,8},{1,17},{9,25},{17,1},{25,9},{2,18},{10... | collective-permute-start | bytes 1572872 | tf_op jit(solution)/shard_map/ppermute | solution.py:920
  43.8 14.5 %collective-permute-start.6 = (bf16[2,2,2,128,256]{4,3,1,2,0:T(8,128)(2,1)S(1)}, bf16[2,2,2,128,256]{4,3,1,2,0:T(8,128)(2,1)S(1)}, u32[]{:S(2)}, u32[]{:S(2)}) collective-permute-start(bf16[2,2,2,128,256]{4,3,1,2,0:T(8,128)(2,1)S(1)} %bitcast.99), channel_id=1, source_target_pairs={{0,1},{1,0},{2,3},{3,2},{4,5},{5,4},{6,7},{7,6},{8,9},{9,8},{10,11... | collective-permute-start | bytes 1572872 | tf_op jit(solution)/shard_map/ppermute | solution.py:920
  54.4 8.7 %collective-permute-start.2 = (bf16[2,2,128,256]{3,2,0,1:T(8,128)(2,1)S(1)}, bf16[2,2,128,256]{3,2,0,1:T(8,128)(2,1)S(1)}, u32[]{:S(2)}, u32[]{:S(2)}) collective-permute-start(bf16[2,2,128,256]{3,2,0,1:T(8,128)(2,1)S(1)} %slice_bitcast_fusion.2), channel_id=1, source_target_pairs={{0,1},{1,0},{2,3},{3,2},{4,5},{5,4},{6,7},{7,6},{8,9},{9,8},{10,11... | collective-permute-start | bytes 786440 | tf_op jit(solution)/shard_map/ppermute | solution.py:920
  58.3 6.4 %collective-permute-start.7 = (bf16[2,2,128,256]{3,2,0,1:T(8,128)(2,1)S(1)}, bf16[2,2,128,256]{3,2,0,1:T(8,128)(2,1)S(1)}, u32[]{:S(2)}, u32[]{:S(2)}) collective-permute-start(bf16[2,2,128,256]{3,2,0,1:T(8,128)(2,1)S(1)} %slice_bitcast_fusion), channel_id=1, source_target_pairs={{0,16},{8,24},{16,0},{24,8},{1,17},{9,25},{17,1},{25,9},{2,18},{10... | collective-permute-start | bytes 786440 | tf_op jit(solution)/shard_map/ppermute | solution.py:920
  63.1 6.2 %collective-permute-start.3 = (bf16[2,128,256]{2,1,0:T(8,128)(2,1)S(1)}, bf16[2,128,256]{2,1,0:T(8,128)(2,1)S(1)}, u32[]{:S(2)}, u32[]{:S(2)}) collective-permute-start(bf16[2,128,256]{2,1,0:T(8,128)(2,1)S(1)} %slice_bitcast_fusion.6), channel_id=1, source_target_pairs={{0,2},{1,3},{2,0},{3,1},{4,6},{5,7},{6,4},{7,5},{8,10},{9,11},{10,... | collective-permute-start | bytes 393224 | tf_op jit(solution)/shard_map/ppermute | solution.py:920
  64.8 7.6 %collective-permute-start.8 = (bf16[2,128,256]{2,1,0:T(8,128)(2,1)S(1)}, bf16[2,128,256]{2,1,0:T(8,128)(2,1)S(1)}, u32[]{:S(2)}, u32[]{:S(2)}) collective-permute-start(bf16[2,128,256]{2,1,0:T(8,128)(2,1)S(1)} %slice_bitcast_fusion.4), channel_id=1, source_target_pairs={{0,2},{1,3},{2,0},{3,1},{4,6},{5,7},{6,4},{7,5},{8,10},{9,11},{10,... | collective-permute-start | bytes 393224 | tf_op jit(solution)/shard_map/ppermute | solution.py:920
  69.9 6.5 %collective-permute-start.4 = (bf16[128,256]{1,0:T(8,128)(2,1)S(1)}, bf16[128,256]{1,0:T(8,128)(2,1)S(1)}, u32[]{:S(2)}, u32[]{:S(2)}) collective-permute-start(bf16[128,256]{1,0:T(8,128)(2,1)S(1)} %get-tuple-element.73), channel_id=1, source_target_pairs={{0,4},{1,5},{2,6},{3,7},{4,0},{5,1},{6,2},{7,3},{8,12},{9,13},{10,... | collective-permute-start | bytes 196616 | tf_op jit(solution)/shard_map/ppermute | solution.py:920
  73.1 5.2 %collective-permute-start.9 = (bf16[128,256]{1,0:T(8,128)(2,1)S(1)}, bf16[128,256]{1,0:T(8,128)(2,1)S(1)}, u32[]{:S(2)}, u32[]{:S(2)}) collective-permute-start(bf16[128,256]{1,0:T(8,128)(2,1)S(1)} %get-tuple-element.71), channel_id=1, source_target_pairs={{0,4},{1,5},{2,6},{3,7},{4,0},{5,1},{6,2},{7,3},{8,12},{9,13},{10,... | collective-permute-start | bytes 196616 | tf_op jit(solution)/shard_map/ppermute | solution.py:920
  83.0 8.9 %collective-permute-start.20 = (bf16[8,32,128]{2,1,0:T(8,128)(2,1)}, bf16[8,32,128]{2,1,0:T(8,128)(2,1)S(1)}, u32[]{:S(2)}, u32[]{:S(2)}) collective-permute-start(bf16[8,32,128]{2,1,0:T(8,128)(2,1)} %get-tuple-element.51), channel_id=1, source_target_pairs={{0,6},{1,7},{2,4},{3,5},{4,2},{5,3},{6,0},{7,1},{8,14},{9,15},{10,... | collective-permute-start | bytes 196616 | tf_op jit(solution)/shard_map/ppermute | solution.py:920
  85.7 7.8 %collective-permute-start.21 = (bf16[8,32,128]{2,1,0:T(8,128)(2,1)}, bf16[8,32,128]{2,1,0:T(8,128)(2,1)S(1)}, u32[]{:S(2)}, u32[]{:S(2)}) collective-permute-start(bf16[8,32,128]{2,1,0:T(8,128)(2,1)} %get-tuple-element.52), channel_id=1, source_target_pairs={{0,7},{1,6},{2,5},{3,4},{4,3},{5,2},{6,1},{7,0},{8,15},{9,14},{10,... | collective-permute-start | bytes 196616 | tf_op jit(solution)/shard_map/ppermute | solution.py:920
  88.4 27.9 %collective-permute-start.10 = (bf16[8,32,128]{2,1,0:T(8,128)(2,1)}, bf16[8,32,128]{2,1,0:T(8,128)(2,1)S(1)}, u32[]{:S(2)}, u32[]{:S(2)}) collective-permute-start(bf16[8,32,128]{2,1,0:T(8,128)(2,1)} %get-tuple-element.38), channel_id=1, source_target_pairs={{0,1},{1,0},{2,3},{3,2},{4,5},{5,4},{6,7},{7,6},{8,9},{9,8},{10,11... | collective-permute-start | bytes 196616 | tf_op jit(solution)/shard_map/ppermute | solution.py:920
  88.9 19.8 %collective-permute-start.12 = (bf16[8,32,128]{2,1,0:T(8,128)(2,1)}, bf16[8,32,128]{2,1,0:T(8,128)(2,1)S(1)}, u32[]{:S(2)}, u32[]{:S(2)}) collective-permute-start(bf16[8,32,128]{2,1,0:T(8,128)(2,1)} %get-tuple-element.43), channel_id=1, source_target_pairs={{0,2},{1,3},{2,0},{3,1},{4,6},{5,7},{6,4},{7,5},{8,10},{9,11},{10,... | collective-permute-start | bytes 196616 | tf_op jit(solution)/shard_map/ppermute | solution.py:920
  88.9 19.9 %collective-permute-start.13 = (bf16[8,32,128]{2,1,0:T(8,128)(2,1)}, bf16[8,32,128]{2,1,0:T(8,128)(2,1)S(1)}, u32[]{:S(2)}, u32[]{:S(2)}) collective-permute-start(bf16[8,32,128]{2,1,0:T(8,128)(2,1)} %get-tuple-element.44), channel_id=1, source_target_pairs={{0,3},{1,2},{2,1},{3,0},{4,7},{5,6},{6,5},{7,4},{8,11},{9,10},{10,... | collective-permute-start | bytes 196616 | tf_op jit(solution)/shard_map/ppermute | solution.py:920
  91.9 7.5 %collective-permute-start.16 = (bf16[8,32,128]{2,1,0:T(8,128)(2,1)}, bf16[8,32,128]{2,1,0:T(8,128)(2,1)S(1)}, u32[]{:S(2)}, u32[]{:S(2)}) collective-permute-start(bf16[8,32,128]{2,1,0:T(8,128)(2,1)} %get-tuple-element.47), channel_id=1, source_target_pairs={{0,4},{1,5},{2,6},{3,7},{4,0},{5,1},{6,2},{7,3},{8,12},{9,13},{10,... | collective-permute-start | bytes 196616 | tf_op jit(solution)/shard_map/ppermute | solution.py:920
  93.4 8.6 %collective-permute-start.17 = (bf16[8,32,128]{2,1,0:T(8,128)(2,1)}, bf16[8,32,128]{2,1,0:T(8,128)(2,1)S(1)}, u32[]{:S(2)}, u32[]{:S(2)}) collective-permute-start(bf16[8,32,128]{2,1,0:T(8,128)(2,1)} %get-tuple-element.48), channel_id=1, source_target_pairs={{0,5},{1,4},{2,7},{3,6},{4,1},{5,0},{6,3},{7,2},{8,13},{9,12},{10,... | collective-permute-start | bytes 196616 | tf_op jit(solution)/shard_map/ppermute | solution.py:920
  99.3 22.7 %collective-permute-start.22 = (bf16[8,32,128]{2,1,0:T(8,128)(2,1)}, bf16[8,32,128]{2,1,0:T(8,128)(2,1)S(1)}, u32[]{:S(2)}, u32[]{:S(2)}) collective-permute-start(bf16[8,32,128]{2,1,0:T(8,128)(2,1)} %get-tuple-element.53), channel_id=1, source_target_pairs={{0,6},{1,7},{2,4},{3,5},{4,2},{5,3},{6,0},{7,1},{8,14},{9,15},{10,... | collective-permute-start | bytes 196616 | tf_op jit(solution)/shard_map/ppermute | solution.py:920
  102.0 22.2 %collective-permute-start.23 = (bf16[8,32,128]{2,1,0:T(8,128)(2,1)}, bf16[8,32,128]{2,1,0:T(8,128)(2,1)S(1)}, u32[]{:S(2)}, u32[]{:S(2)}) collective-permute-start(bf16[8,32,128]{2,1,0:T(8,128)(2,1)} %get-tuple-element.54), channel_id=1, source_target_pairs={{0,7},{1,6},{2,5},{3,4},{4,3},{5,2},{6,1},{7,0},{8,15},{9,14},{10,... | collective-permute-start | bytes 196616 | tf_op jit(solution)/shard_map/ppermute | solution.py:920
  108.7 16.0 %collective-permute-start.18 = (bf16[8,32,128]{2,1,0:T(8,128)(2,1)}, bf16[8,32,128]{2,1,0:T(8,128)(2,1)S(1)}, u32[]{:S(2)}, u32[]{:S(2)}) collective-permute-start(bf16[8,32,128]{2,1,0:T(8,128)(2,1)} %get-tuple-element.49), channel_id=1, source_target_pairs={{0,4},{1,5},{2,6},{3,7},{4,0},{5,1},{6,2},{7,3},{8,12},{9,13},{10,... | collective-permute-start | bytes 196616 | tf_op jit(solution)/shard_map/ppermute | solution.py:920
  108.8 16.0 %collective-permute-start.19 = (bf16[8,32,128]{2,1,0:T(8,128)(2,1)}, bf16[8,32,128]{2,1,0:T(8,128)(2,1)S(1)}, u32[]{:S(2)}, u32[]{:S(2)}) collective-permute-start(bf16[8,32,128]{2,1,0:T(8,128)(2,1)} %get-tuple-element.50), channel_id=1, source_target_pairs={{0,5},{1,4},{2,7},{3,6},{4,1},{5,0},{6,3},{7,2},{8,13},{9,12},{10,... | collective-permute-start | bytes 196616 | tf_op jit(solution)/shard_map/ppermute | solution.py:920
  116.3 8.5 %collective-permute-start.14 = (bf16[8,32,128]{2,1,0:T(8,128)(2,1)}, bf16[8,32,128]{2,1,0:T(8,128)(2,1)S(1)}, u32[]{:S(2)}, u32[]{:S(2)}) collective-permute-start(bf16[8,32,128]{2,1,0:T(8,128)(2,1)} %get-tuple-element.45), channel_id=1, source_target_pairs={{0,2},{1,3},{2,0},{3,1},{4,6},{5,7},{6,4},{7,5},{8,10},{9,11},{10,... | collective-permute-start | bytes 196616 | tf_op jit(solution)/shard_map/ppermute | solution.py:920
  122.1 5.2 %collective-permute-start.15 = (bf16[8,32,128]{2,1,0:T(8,128)(2,1)S(1)}, bf16[8,32,128]{2,1,0:T(8,128)(2,1)S(1)}, u32[]{:S(2)}, u32[]{:S(2)}) collective-permute-start(bf16[8,32,128]{2,1,0:T(8,128)(2,1)S(1)} %copy-done.19), channel_id=1, source_target_pairs={{0,3},{1,2},{2,1},{3,0},{4,7},{5,6},{6,5},{7,4},{8,11},{9,10},{10,... | collective-permute-start | bytes 196616 | tf_op jit(solution)/shard_map/ppermute | solution.py:920
  132.2 6.1 %collective-permute-start.29 = (bf16[128,256]{1,0:T(8,128)(2,1)}, bf16[128,256]{1,0:T(8,128)(2,1)S(1)}, u32[]{:S(2)}, u32[]{:S(2)}) collective-permute-start(bf16[128,256]{1,0:T(8,128)(2,1)} %get-tuple-element.56), channel_id=1, source_target_pairs={{0,4},{1,5},{2,6},{3,7},{4,0},{5,1},{6,2},{7,3},{8,12},{9,13},{10,... | collective-permute-start | bytes 196616 | tf_op jit(solution)/shard_map/ppermute | solution.py:920
  133.9 5.9 %collective-permute-start.24 = (bf16[128,256]{1,0:T(8,128)(2,1)}, bf16[128,256]{1,0:T(8,128)(2,1)S(1)}, u32[]{:S(2)}, u32[]{:S(2)}) collective-permute-start(bf16[128,256]{1,0:T(8,128)(2,1)} %get-tuple-element.55), channel_id=1, source_target_pairs={{0,4},{1,5},{2,6},{3,7},{4,0},{5,1},{6,2},{7,3},{8,12},{9,13},{10,... | collective-permute-start | bytes 196616 | tf_op jit(solution)/shard_map/ppermute | solution.py:920
  139.2 5.0 %collective-permute-start.30 = (bf16[2,128,256]{2,1,0:T(8,128)(2,1)S(1)}, bf16[2,128,256]{2,1,0:T(8,128)(2,1)S(1)}, u32[]{:S(2)}, u32[]{:S(2)}) collective-permute-start(bf16[2,128,256]{2,1,0:T(8,128)(2,1)S(1)} %get-tuple-element.68), channel_id=1, source_target_pairs={{0,2},{1,3},{2,0},{3,1},{4,6},{5,7},{6,4},{7,5},{8,10},{9,11},{10,... | collective-permute-start | bytes 393224 | tf_op jit(solution)/shard_map/ppermute | solution.py:920
  144.2 9.3 %collective-permute-start.31 = (bf16[2,2,128,256]{3,2,0,1:T(8,128)(2,1)S(1)}, bf16[2,2,128,256]{3,2,0,1:T(8,128)(2,1)S(1)}, u32[]{:S(2)}, u32[]{:S(2)}) collective-permute-start(bf16[2,2,128,256]{3,2,0,1:T(8,128)(2,1)S(1)} %get-tuple-element.64), channel_id=1, source_target_pairs={{0,16},{8,24},{16,0},{24,8},{1,17},{9,25},{17,1},{25,9},{2,18},{10... | collective-permute-start | bytes 786440 | tf_op jit(solution)/shard_map/ppermute | solution.py:920
  145.8 7.9 %collective-permute-start.26 = (bf16[2,2,128,256]{3,2,0,1:T(8,128)(2,1)S(1)}, bf16[2,2,128,256]{3,2,0,1:T(8,128)(2,1)S(1)}, u32[]{:S(2)}, u32[]{:S(2)}) collective-permute-start(bf16[2,2,128,256]{3,2,0,1:T(8,128)(2,1)S(1)} %get-tuple-element.66), channel_id=1, source_target_pairs={{0,1},{1,0},{2,3},{3,2},{4,5},{5,4},{6,7},{7,6},{8,9},{9,8},{10,11... | collective-permute-start | bytes 786440 | tf_op jit(solution)/shard_map/ppermute | solution.py:920
  153.6 9.2 %collective-permute-start.32 = (bf16[2,2,2,128,256]{4,3,1,2,0:T(8,128)(2,1)S(1)}, bf16[2,2,2,128,256]{4,3,1,2,0:T(8,128)(2,1)S(1)}, u32[]{:S(2)}, u32[]{:S(2)}) collective-permute-start(bf16[2,2,2,128,256]{4,3,1,2,0:T(8,128)(2,1)S(1)} %get-tuple-element.62), channel_id=1, source_target_pairs={{0,1},{1,0},{2,3},{3,2},{4,5},{5,4},{6,7},{7,6},{8,9},{9,8},{10,11... | collective-permute-start | bytes 1572872 | tf_op jit(solution)/shard_map/ppermute | solution.py:920
  153.8 9.3 %collective-permute-start.27 = (bf16[2,2,2,128,256]{4,3,0,1,2:T(8,128)(2,1)S(1)}, bf16[2,2,2,128,256]{4,3,0,1,2:T(8,128)(2,1)S(1)}, u32[]{:S(2)}, u32[]{:S(2)}) collective-permute-start(bf16[2,2,2,128,256]{4,3,0,1,2:T(8,128)(2,1)S(1)} %pad_maximum_fusion.2), channel_id=1, source_target_pairs={{0,16},{8,24},{16,0},{24,8},{1,17},{9,25},{17,1},{25,9},{2,18},{10... | collective-permute-start | bytes 1572872 | tf_op jit(solution)/shard_map/ppermute | solution.py:920
  163.2 14.1 %collective-permute-start.28 = (bf16[2,8,128,256]{3,2,1,0:T(8,128)(2,1)S(1)}, bf16[2,8,128,256]{3,2,1,0:T(8,128)(2,1)S(1)}, u32[]{:S(2)}, u32[]{:S(2)}) collective-permute-start(bf16[2,8,128,256]{3,2,1,0:T(8,128)(2,1)S(1)} %pad_maximum_fusion.a_ref), channel_id=1, source_target_pairs={{0,8},{8,0},{16,24},{24,16},{1,9},{9,1},{17,25},{25,17},{2,10},{10... | collective-permute-start | bytes 3145736 | tf_op jit(solution)/shard_map/ppermute | solution.py:920
  163.3 14.0 %collective-permute-start.33 = (bf16[2,8,128,256]{3,2,1,0:T(8,128)(2,1)S(1)}, bf16[2,8,128,256]{3,2,1,0:T(8,128)(2,1)S(1)}, u32[]{:S(2)}, u32[]{:S(2)}) collective-permute-start(bf16[2,8,128,256]{3,2,1,0:T(8,128)(2,1)S(1)} %bitcast.93), channel_id=1, source_target_pairs={{0,8},{8,0},{16,24},{24,16},{1,9},{9,1},{17,25},{25,17},{2,10},{10... | collective-permute-start | bytes 3145736 | tf_op jit(solution)/shard_map/ppermute | solution.py:920
  (26 other events, 94.6 us)

commit v3 on v2

--- a/solution.py
+++ b/solution.py
@@ -114,7 +114,7 @@
         spread[pl.ds(pl.multiple_of(i * LANES, LANES), LANES), :] = row.T
         return carry
 
-    lax.fori_loop(0, window_ref.shape[0], one, 0)
+    lax.fori_loop(0, window_ref.shape[0], one, 0, unroll=8)
 
 
 def place_of(jr, count):
@@ -212,6 +212,8 @@
     kept_ref,
     a_ref,
     b_ref,
+    strips,
+    arrived,
     mat,
     inner,
     spread,
@@ -222,15 +224,21 @@
     count = level.shape[0]
     quarter = tr_ref.shape[2]
     length = quarter * TS
-    block = x_ref.shape[2]
+    blocks, _, _, block = strips.shape
     width = fr_ref.shape[0]
-    blocks = width // block
     subs = a_ref.shape[1]
     part = 2 * (SG // TS)
     step = pl.program_id(0)
 
+    def fetch(b):
+        lanes = pl.ds(pl.multiple_of(b * block, block), block)
+        return pltpu.make_async_copy(x_ref.at[:, :, lanes], strips.at[b], arrived.at[b])
+
     @pl.when(step == 0)
     def _():
+        for b in range(blocks):
+            fetch(b).start()
+
         def write(k1, place, value):
             mat[k1, place * part : (place + 1) * part, :] = value
 
@@ -243,6 +251,8 @@
 
     @pl.when(step < blocks)
     def _():
+        fetch(step).wait()
+
         def butterfly(chunk, carry):
             n2 = pl.multiple_of(chunk * 16, 16)
             for lane in range(0, block, LANES):
@@ -252,7 +262,7 @@
                     window = spread[rows, :]
                     values.append(
                         tuple(
-                            x_ref[z, rows, lane : lane + LANES].astype(F32) * window
+                            strips[step, z, rows, lane : lane + LANES].astype(F32) * window
                             for z in range(2)
                         )
                     )
@@ -321,7 +331,7 @@
             num_scalar_prefetch=3,
             grid=(blocks + used,),
             in_specs=[
-                pl.BlockSpec((2, length, block), lambda c, *_: (0, 0, jnp.minimum(c, blocks - 1))),
+                pl.BlockSpec(memory_space=pl.ANY),
                 pl.BlockSpec((length // LANES, LANES), lambda c, *_: (0, 0)),
                 pl.BlockSpec((1, width), lambda c, *_: (0, 0)),
                 pl.BlockSpec((TS, q2, quarter), lambda c, *_: (0, 0, 0)),
@@ -338,6 +348,8 @@
                 pl.BlockSpec((1, subs, rows, half), late),
             ],
             scratch_shapes=[
+                pltpu.VMEM((blocks, 2, length, block), BF16),
+                pltpu.SemaphoreType.DMA((blocks,)),
                 pltpu.VMEM((TS, count * 2 * q2, 2 * quarter), BF16),
                 pltpu.VMEM((TS, 2 * quarter, block), BF16),
                 pltpu.VMEM((length, LANES), F32),
@@ -575,7 +587,7 @@
     )(pixels)
 
 
-def visit_kernel(sources, *refs):
+def visit_kernel(ids, *refs):
     n = (len(refs) - 7) // 2
     ins, outs = refs[:n], refs[n + 5 : 2 * n + 5]
     meas_ref, weight_ref, row_ref, col_ref, mask_ref = refs[n : n + 5]
@@ -619,7 +631,7 @@
                 outs[i][g] = value
 
 
-def visit(sources, blocks, measured, weight, row, col):
+def visit(ids, first, blocks, measured, weight, row, col):
     n = len(blocks)
     shape = blocks[0].shape
     groups = shape[0]
@@ -627,6 +639,10 @@
     rows = TS * GROUP
     mask = np.arange(GROUP)[:, None] == np.arange(LANES)[None, :] % GROUP
     whole = pl.BlockSpec(shape, lambda i, m: (0, 0, 0))
+
+    def source(i, m):
+        return jnp.bitwise_xor(m[1], first + i)
+
     return pl.pallas_call(
         visit_kernel,
         grid_spec=pltpu.PrefetchScalarGridSpec(
@@ -634,10 +650,10 @@
             grid=(n,),
             in_specs=[whole] * n
             + [
-                pl.BlockSpec((2, slots, LANES), lambda i, m: (0, m[i], 0)),
-                pl.BlockSpec((slots, LANES), lambda i, m: (m[i], 0)),
-                pl.BlockSpec((groups, 2, rows, LANES), lambda i, m: (m[i], 0, 0, 0)),
-                pl.BlockSpec((groups, rows, 2 * LANES), lambda i, m: (m[i], 0, 0)),
+                pl.BlockSpec((2, slots, LANES), lambda i, m: (0, source(i, m), 0)),
+                pl.BlockSpec((slots, LANES), lambda i, m: (source(i, m), 0)),
+                pl.BlockSpec((groups, 2, rows, LANES), lambda i, m: (source(i, m), 0, 0, 0)),
+                pl.BlockSpec((groups, rows, 2 * LANES), lambda i, m: (source(i, m), 0, 0)),
                 pl.BlockSpec((GROUP, LANES), lambda i, m: (0, 0)),
             ],
             out_specs=[whole] * n,
@@ -652,7 +668,7 @@
             flops=1_800_000_000 * n, bytes_accessed=(5 << 18) * n, transcendentals=0
         ),
         name="visit",
-    )(sources, *blocks, measured, weight, row, col, jnp.asarray(mask.astype(np.float32)))
+    )(ids, *blocks, measured, weight, row, col, jnp.asarray(mask.astype(np.float32)))
 
 
 def columns_back(ids, jr, col_off, halves, fr_ref, fi_ref, cw_ref, image, length):
@@ -757,7 +773,7 @@
     )(ids, row_off, col_off, *halves, *tables, col_window)
 
 
-def transposed_kernel(ids, row_off, tr_ref, ti_ref, out_ref, mat):
+def adjoint_tables_kernel(ids, row_off, tr_ref, ti_ref, rw_ref, out_ref, spread_ref, mat):
     part = 2 * (SG // TS)
 
     def write(k1, place, block):
@@ -770,26 +786,30 @@
         return carry
 
     lax.fori_loop(0, TS, per_k1, 0)
-
-
-def transposed_matrix(ids, row_off, tables):
+    spread_window(rw_ref, spread_ref)
+
+
+def adjoint_tables(ids, row_off, tables, row_window):
     count = row_off.shape[0]
     quarter = tables[0].shape[2]
     part = 2 * (SG // TS)
     vmem = pl.BlockSpec(memory_space=pltpu.VMEM)
     smem = pl.BlockSpec(memory_space=pltpu.SMEM)
     return pl.pallas_call(
-        transposed_kernel,
-        in_specs=[smem] * 2 + [vmem] * 2,
-        out_specs=vmem,
-        out_shape=jax.ShapeDtypeStruct((TS, 2 * quarter, count * part), BF16),
+        adjoint_tables_kernel,
+        in_specs=[smem] * 2 + [vmem] * 3,
+        out_specs=[vmem] * 2,
+        out_shape=[
+            jax.ShapeDtypeStruct((TS, 2 * quarter, count * part), BF16),
+            jax.ShapeDtypeStruct((row_window.size, LANES), F32),
+        ],
         scratch_shapes=[pltpu.VMEM((TS, count * part, 2 * quarter), F32)],
         compiler_params=pltpu.CompilerParams(vmem_limit_bytes=VMEM_LIMIT),
         cost_estimate=pl.CostEstimate(
-            flops=5_000_000_000, bytes_accessed=5 << 20, transcendentals=0
+            flops=7_000_000_000, bytes_accessed=7 << 20, transcendentals=0
         ),
-        name="transposed_matrix",
-    )(ids, row_off, *tables)
+        name="adjoint_tables",
+    )(ids, row_off, *tables, row_window)
 
 
 def backward_kernel(
@@ -803,22 +823,42 @@
     cw_ref,
     even_ref,
     mat_ref,
-    rw_ref,
+    spread_ref,
     out_ref,
     image,
     odd,
     middle,
+    mat,
     spread,
+    update,
+    arrived,
+    left,
 ):
     used = row_off.shape[0] // 2
-    quarter = mat_ref.shape[1] // 2
-    block = even_ref.shape[2]
+    quarter = mat.shape[1] // 2
+    blocks, _, _, _, block = update.shape
+    pieces = left.shape[1]
+    piece = quarter // pieces
     part = 2 * (SG // TS)
     step = pl.program_id(0)
 
+    def fetches():
+        return (
+            pltpu.make_async_copy(mat_ref, mat, arrived.at[0]),
+            pltpu.make_async_copy(spread_ref, spread, arrived.at[1]),
+        )
+
+    def leave(b, n):
+        rows = pl.ds(pl.multiple_of(n * piece, piece), piece)
+        lanes = pl.ds(pl.multiple_of(b * block, block), block)
+        return pltpu.make_async_copy(
+            update.at[b, :, :, rows, :], out_ref.at[:, :, rows, lanes], left.at[b, n]
+        )
+
     @pl.when(step == 0)
     def _():
-        spread_window(rw_ref, spread)
+        for copy in fetches():
+            copy.start()
 
     @pl.when(step < used)
     def _():
@@ -841,13 +881,19 @@
 
         sort_rows(image, row_off[jnp.bitwise_xor(ids[0], jr)], write)
 
+    @pl.when(step == used)
+    def _():
+        for copy in fetches():
+            copy.wait()
+
     @pl.when(step >= used)
     def _():
-        lanes = pl.ds(pl.multiple_of((step - used) * block, block), block)
+        b = step - used
+        lanes = pl.ds(pl.multiple_of(b * block, block), block)
 
         def per_k1(k1, carry):
             rows = jnp.concatenate([even_ref[k1], odd[k1, :, lanes]], axis=0)
-            middle[k1] = jnp.dot(mat_ref[k1], rows, preferred_element_type=F32)
+            middle[k1] = jnp.dot(mat[k1], rows, preferred_element_type=F32)
             return carry
 
         lax.fori_loop(0, TS, per_k1, 0, unroll=4)
@@ -867,53 +913,70 @@
                     for k1 in range(TS)
                 ]
                 for n1, pair in enumerate(dft16(values, 1)):
-                    rows = pl.ds(pl.multiple_of(n1 * quarter + n2, 16), 16)
-                    window = spread[rows, :]
+                    window = spread[pl.ds(pl.multiple_of(n1 * quarter + n2, 16), 16), :]
                     for z in range(2):
-                        out_ref[z, rows, lane : lane + LANES] = (pair[z] * window).astype(BF16)
+                        update[b, z, n1, pl.ds(n2, 16), lane : lane + LANES] = (
+                            pair[z] * window
+                        ).astype(BF16)
             return carry
 
-        lax.fori_loop(0, quarter // 16, butterfly, 0)
-
-
-def backward(ids, row_off, col_off, halves, tables, col_window, even, matrix, row_window):
+        def per_piece(n, carry):
+            chunks = piece // 16
+            lax.fori_loop(n * chunks, (n + 1) * chunks, butterfly, 0)
+            leave(b, n).start()
+            return carry
+
+        lax.fori_loop(0, pieces, per_piece, 0)
+
+    @pl.when(step == used + blocks - 1)
+    def _():
+        for b in range(blocks):
+            for n in range(pieces):
+                leave(b, n).wait()
+
+
+def backward(ids, row_off, col_off, halves, tables, col_window, even, matrix, spread):
     used, subs, rows, half = halves[0].shape
     _, depth, width = even.shape
-    length = row_window.size
+    length = spread.shape[0]
     quarter = length // TS
     block = min(2 * LANES, width)
+    blocks = width // block
+    pieces = 4
 
     def early(c, *_):
         return (jnp.minimum(c, used - 1), 0, 0, 0)
 
-    def late(c, *_):
-        return (0, 0, jnp.maximum(c - used, 0))
-
-    return pl.pallas_call(
+    update = pl.pallas_call(
         backward_kernel,
         grid_spec=pltpu.PrefetchScalarGridSpec(
             num_scalar_prefetch=3,
-            grid=(used + width // block,),
+            grid=(used + blocks,),
             in_specs=[pl.BlockSpec((1, subs, rows, half), early)] * 2
             + [pl.BlockSpec((width, SG), lambda c, m, *_: (m[1], 0))] * 2
             + [
                 pl.BlockSpec((1, width), lambda c, *_: (0, 0)),
-                pl.BlockSpec((TS, depth, block), late),
-                pl.BlockSpec((TS, 2 * quarter, 2 * depth), lambda c, *_: (0, 0, 0)),
-                pl.BlockSpec((length // LANES, LANES), lambda c, *_: (0, 0)),
+                pl.BlockSpec((TS, depth, block), lambda c, *_: (0, 0, jnp.maximum(c - used, 0))),
+                pl.BlockSpec(memory_space=pl.ANY),
+                pl.BlockSpec(memory_space=pl.ANY),
             ],
-            out_specs=pl.BlockSpec((2, length, block), late),
+            out_specs=pl.BlockSpec(memory_space=pl.ANY),
             scratch_shapes=[
                 image_scratch(width, subs),
                 pltpu.VMEM((TS, depth, width), BF16),
                 pltpu.VMEM((TS, 2 * quarter, block), F32),
-                pltpu.VMEM((length, LANES), F32),
+                pltpu.VMEM(matrix.shape, BF16),
+                pltpu.VMEM(spread.shape, F32),
+                pltpu.VMEM((blocks, 2, TS, quarter, block), BF16),
+                pltpu.SemaphoreType.DMA((2,)),
+                pltpu.SemaphoreType.DMA((blocks, pieces)),
             ],
         ),
-        out_shape=jax.ShapeDtypeStruct((2, length, width), BF16),
+        out_shape=jax.ShapeDtypeStruct((2, TS, quarter, width), BF16),
         compiler_params=pltpu.CompilerParams(vmem_limit_bytes=VMEM_LIMIT),
         name="backward",
-    )(ids, row_off, col_off, *halves, *tables, col_window, even, matrix, row_window)
+    )(ids, row_off, col_off, *halves, *tables, col_window, even, matrix, spread)
+    return update.reshape(2, length, width)
 
 
 def swap(value, axis, bit):
@@ -934,35 +997,54 @@
     return bits_of("facet")[:0:-1] + bits_of("sub")[::-1]
 
 
-def sum_blocks(kept, sent):
+def sum_blocks(kept, sent, beside, operand):
+    values = [k + swap(s, "facet", 1) for k, s in zip(kept, sent)]
+    values, operand = lax.optimization_barrier((values, operand))
+    extra = beside(operand)
+    left = [dimensions(), dimensions()]
+    values = [value.reshape((2,) * len(left[0]) + value.shape[2:]) for value in values]
+
+    def halve(n, step):
+        at = left[n].index(step)
+        left[n].remove(step)
+        mine = lax.index_in_dim(values[n], 0, at, keepdims=False)
+        return mine, swap(lax.index_in_dim(values[n], 1, at, keepdims=False), *step)
+
+    steps = list(zip(*orders()))
+    for pair in steps[:-1]:
+        halved = [halve(n, step) for n, step in enumerate(pair)]
+        if pair is steps[0]:
+            halved, extra = lax.optimization_barrier((halved, extra))
+        values = [mine + arrived for mine, arrived in halved]
+    last = [halve(n, step) for n, step in enumerate(steps[-1])]
+    return last[0] + last[1], extra
+
+
+def gather_blocks(halves, facet_count, sub_count, beside, operand):
+    shape = halves[0].shape
+    every = dimensions()
+    have = [[], []]
+    values = list(halves)
+
+    def grow(n, step):
+        at = len([d for d in every if d in have[n] and every.index(d) < every.index(step)])
+        have[n].append(step)
+        values[n] = jnp.stack([values[n], swap(values[n], *step)], axis=at)
+
+    steps = list(zip(*[order[::-1] for order in orders()]))
+    for pair in steps[:-1]:
+        for n, step in enumerate(pair):
+            grow(n, step)
+    values, operand = lax.optimization_barrier((values, operand))
+    extra = beside(operand)
+    for n, step in enumerate(steps[-1]):
+        grow(n, step)
+    values, extra = lax.optimization_barrier((values, extra))
     result = []
-    for kept_half, sent_half, order in zip(kept, sent, orders()):
-        value = kept_half + swap(sent_half, "facet", 1)
-        dims = dimensions()
-        value = value.reshape((2,) * len(dims) + value.shape[2:])
-        for step in order:
-            at = dims.index(step)
-            dims.remove(step)
-            mine = lax.index_in_dim(value, 0, at, keepdims=False)
-            arrived = swap(lax.index_in_dim(value, 1, at, keepdims=False), *step)
-            value = mine + arrived if dims else None
-        result += [mine, arrived]
-    return result
-
-
-def gather_blocks(halves, facet_count, sub_count):
-    result = []
-    for value, order in zip(halves, orders()):
-        shape = value.shape
-        have = []
-        every = dimensions()
-        for step in order[::-1]:
-            at = len([d for d in every if d in have and every.index(d) < every.index(step)])
-            have.append(step)
-            value = jnp.stack([value, swap(value, *step)], axis=at)
+    for value in values:
         value = value.reshape((facet_count // 2, sub_count) + shape)
         result.append((value, swap(value, "facet", 1)))
-    return result
+    return result, extra
 
 
 def per_device(
@@ -1020,25 +1102,27 @@
     values = jnp.transpose(per_slot(measured[0, 0]), (1, 0, 2))
     pixels = jnp.transpose(per_slot(uvw_pixels[0, 0]), (1, 0, 2))
 
-    parts = sum_blocks(kept, sent)
-    row_kernels, col_kernels = kernels(pixels, 4)
-    matrix = transposed_matrix(ids, row_offsets, row_consts)
+    parts, (row_kernels, col_kernels) = sum_blocks(kept, sent, partial(kernels, steps=4), pixels)
     routed = route(ids, owners, parts, sub_count, groups)
     outgoing, where = routed[:-1], routed[-1]
     arrived = [outgoing[0]] + [swap(outgoing[r], "sub", r) for r in range(1, sub_count)]
     returned = []
-    for first in range(0, sub_count, 2):
-        sources = jnp.stack([ids[1] ^ first, ids[1] ^ (first + 1)])
-        answered = visit(
-            sources, arrived[first : first + 2], values, weights, row_kernels, col_kernels
-        )
+    for first in range(0, sub_count, sub_count // 2):
+        chosen = arrived[first : first + sub_count // 2]
+        answered = visit(ids, first, chosen, values, weights, row_kernels, col_kernels)
         returned += [
             swap(value, "sub", first + n) if first + n else value
             for n, value in enumerate(answered)
         ]
     halves = unroute(where, returned, 2 * SG // sub_count)
 
-    (a_own, a_other), (b_own, b_other) = gather_blocks(halves, facet_count, sub_count)
+    ((a_own, a_other), (b_own, b_other)), (matrix, spread) = gather_blocks(
+        halves,
+        facet_count,
+        sub_count,
+        lambda window: adjoint_tables(ids, row_offsets, row_consts, window),
+        row_win,
+    )
     even = cols_backward(
         ids, row_offsets, col_offsets, (a_own, b_own), col_consts, col_win, length
     )
@@ -1051,7 +1135,7 @@
         col_win,
         even,
         matrix,
-        row_win,
+        spread,
     )
 
 

time: 201 us -> 179 us (0.89)
  Pallas kernels: 95.5 us -> 83.9 us
  waiting for transfers between devices: 43.7 us -> 33.6 us
    ppermute x34, waiting for transfers between devices: 43.7 us -> 33.6 us  [swap(): lax.ppermute(value, axis, [(i, i ^ bit) for i in range(lax.axis_size(axis...]
    pallas_call x1, Pallas kernels: 21.4 us -> 16.4 us  [backward(): pl.pallas_call(backward_kernel, grid_spec=pltpu.PrefetchScalarGridSpec(nu...]
    pallas_call x4 -> x2, Pallas kernels: 18.5 us -> 14.1 us  [visit(): pl.pallas_call(visit_kernel, grid_spec=pltpu.PrefetchScalarGridSpec(num_s...]
    pallas_call x1, Pallas kernels: 22.4 us -> 18.8 us  [forward(): pl.pallas_call(forward_kernel, grid_spec=pltpu.PrefetchScalarGridSpec(num...]
    another operation x12 -> x8, other arithmetic: 4.54 us -> 2.08 us  [grow(): values[n] = jnp.stack([values[n], swap(values[n], *step)], axis=at)]
    unnamed x50 -> x49, local copies, waits for them, and re-layouts: 5.29 us -> 6.62 us
  transfers between devices with their start and end apart: 34 -> 34, of which waited for: 14 -> 15; matrix products, arithmetic and copies ran while one was open for 6% -> 4% of each run, Pallas kernels for 22% -> 23%
where the time goes in v3:
time: 179 us
  Pallas kernels  83.9 us (47%)
  starting transfers between devices  45.3 us (25%)
  waiting for transfers between devices  33.6 us (19%)
  local copies, waits for them, and re-layouts  8.3 us (5%)
  other arithmetic  6.93 us (4%)
    ppermute x34, starting transfers between devices, swap(): lax.ppermute(value, axis, [(i, i ^ bit) for i in range(lax.axis_size(axis...  45.3 us
    ppermute x34, waiting for transfers between devices, swap(): lax.ppermute(value, axis, [(i, i ^ bit) for i in range(lax.axis_size(axis...  33.6 us
    pallas_call x1, Pallas kernels, forward(): pl.pallas_call(forward_kernel, grid_spec=pltpu.PrefetchScalarGridSpec(num...  18.8 us
    pallas_call x1, Pallas kernels, backward(): pl.pallas_call(backward_kernel, grid_spec=pltpu.PrefetchScalarGridSpec(nu...  16.4 us
    pallas_call x2, Pallas kernels, visit(): pl.pallas_call(visit_kernel, grid_spec=pltpu.PrefetchScalarGridSpec(num_s...  14.1 us
    pallas_call x1, Pallas kernels, adjoint_tables(): pl.pallas_call(adjoint_tables_kernel, in_specs=[smem] * 2 + [vmem] * 3, o...  7.91 us
    pallas_call x1, Pallas kernels, cols_backward(): pl.pallas_call(partial(cols_backward_kernel, length=length), grid_spec=pl...  6.88 us
    unnamed x49, local copies, waits for them, and re-layouts  6.62 us
  transfers between devices with their start and end apart: 34, of which 15 were waited for; matrix products, arithmetic and copies ran while one was open for 4% of the time, Pallas kernels for 23%

profile of v3, /device:TPU:0, one launch (start us, length us, event | category | flops | bytes accessed | tf_op | source)
XLA Modules:
  0.0 178.6 jit_solution(17975160414379647847)
XLA Ops:
  0.7 18.8 %forward.1 = (bf16[2,2,16,32,512]{4,3,2,1,0:T(8,128)(2,1)}, bf16[2,8,128,256]{3,2,1,0:T(8,128)(2,1)}, bf16[2,8,128,256]{3,2,1,0:T(8,128)(2,1)}) custom-call(s32[2]{0:T(128)} %pad_add_fusion.ids, s32[4]{0:T(128)} %row_off.7, s32[4]{0:T(128)} %col_off.5, bf16[2,4096,512]{2,1,0:T(8,128)(2,1)} %x_ref.1, f32[32,128]{1,0:T(8,128)} %bitcast.110, ...), custom_call_target="tpu_custom_call" | custom-call | flops 12000000000 | bytes 16777216 | tf_op jit(solution)/shard_map/forward/pallas_call | solution.py:328
  20.1 6.3 %cols_forward.1 = (bf16[2,8,128,256]{3,2,1,0:T(8,128)(2,1)}, bf16[2,8,128,256]{3,2,1,0:T(8,128)(2,1)}) custom-call(s32[2]{0:T(128)} %pad_add_fusion.ids, bf16[2,2,512,512]{3,2,1,0:T(8,128)(2,1)} %bitcast.112, bf16[4096,512]{1,0:T(8,128)(2,1)} %constant.22.clone.fr_ref, bf16[4096,512]{1,0:T(8,128)(2,1)} %constant.23.clone.fi_ref), custom_call_target="tpu_custom_call" | custom-call | flops 4000000000 | bytes 6291456 | tf_op jit(solution)/shard_map/cols_forward/pallas_call | solution.py:380
  29.8 3.0 %collective-permute-start.2 = (bf16[2,2,2,128,256]{4,3,0,1,2:T(8,128)(2,1)S(1)}, bf16[2,2,2,128,256]{4,3,0,1,2:T(8,128)(2,1)S(1)}, u32[]{:S(2)}, u32[]{:S(2)}) collective-permute-start(bf16[2,2,2,128,256]{4,3,0,1,2:T(8,128)(2,1)S(1)} %copy.20), channel_id=1, source_target_pairs={{0,16},{8,24},{16,0},{24,8},{1,17},{9,25},{17,1},{25,9},{2,18},{10... | collective-permute-start | bytes 1572872 | tf_op jit(solution)/shard_map/ppermute | solution.py:983
  34.3 6.5 %kernels.1 = (bf16[64,2,128,128]{3,2,1,0:T(8,128)(2,1)}, bf16[64,128,256]{2,1,0:T(8,128)(2,1)}) custom-call(s32[3,512,128]{2,1,0:T(8,128)} %bitcast.109), custom_call_target="tpu_custom_call" | custom-call | flops 6000000000 | bytes 9437184 | tf_op jit(solution)/shard_map/kernels/pallas_call | solution.py:570
  40.8 4.1 %collective-permute-done.2 = bf16[2,2,2,128,256]{4,3,0,1,2:T(8,128)(2,1)S(1)} collective-permute-done((bf16[2,2,2,128,256]{4,3,0,1,2:T(8,128)(2,1)S(1)}, bf16[2,2,2,128,256]{4,3,0,1,2:T(8,128)(2,1)S(1)}, u32[]{:S(2)}, u32[]{:S(2)}) %collective-permute-start.2) | collective-permute-done | bytes 524320 | tf_op jit(solution)/shard_map/ppermute | solution.py:983
  46.5 1.6 collective-permute-start.4
  48.8 4.9 %collective-permute-done.4 = bf16[2,2,128,256]{3,2,0,1:T(8,128)(2,1)S(1)} collective-permute-done((bf16[2,2,128,256]{3,2,0,1:T(8,128)(2,1)S(1)}, bf16[2,2,128,256]{3,2,0,1:T(8,128)(2,1)S(1)}, u32[]{:S(2)}, u32[]{:S(2)}) %collective-permute-start.4) | collective-permute-done | bytes 262176 | tf_op jit(solution)/shard_map/ppermute | solution.py:983
  53.8 1.6 collective-permute-start.5
  56.9 1.9 %collective-permute-done.5 = bf16[2,128,256]{2,1,0:T(8,128)(2,1)S(1)} collective-permute-done((bf16[2,128,256]{2,1,0:T(8,128)(2,1)S(1)}, bf16[2,128,256]{2,1,0:T(8,128)(2,1)S(1)}, u32[]{:S(2)}, u32[]{:S(2)}) %collective-permute-start.5) | collective-permute-done | bytes 131104 | tf_op jit(solution)/shard_map/ppermute | solution.py:983
  59.5 2.6 %collective-permute-start.6 = (bf16[128,256]{1,0:T(8,128)(2,1)S(1)}, bf16[128,256]{1,0:T(8,128)(2,1)S(1)}, u32[]{:S(2)}, u32[]{:S(2)}) collective-permute-start(bf16[128,256]{1,0:T(8,128)(2,1)S(1)} %get-tuple-element.107), channel_id=1, source_target_pairs={{0,4},{1,5},{2,6},{3,7},{4,0},{5,1},{6,2},{7,3},{8,12},{9,13},{10,... | collective-permute-start | bytes 196616 | tf_op jit(solution)/shard_map/ppermute | solution.py:983
  64.2 1.7 collective-permute-done.6.refs_1_
  65.9 2.0 %collective-permute-done.9.refs_3_ = bf16[128,256]{1,0:T(8,128)(2,1)S(1)} collective-permute-done((bf16[128,256]{1,0:T(8,128)(2,1)S(1)}, bf16[128,256]{1,0:T(8,128)(2,1)S(1)}, u32[]{:S(2)}, u32[]{:S(2)}) %collective-permute-start.9) | collective-permute-done | bytes 65568 | tf_op jit(solution)/shard_map/ppermute | solution.py:983
  68.5 4.1 %route.1 = (bf16[8,32,128]{2,1,0:T(8,128)(2,1)}, bf16[8,32,128]{2,1,0:T(8,128)(2,1)}, bf16[8,32,128]{2,1,0:T(8,128)(2,1)}, bf16[8,32,128]{2,1,0:T(8,128)(2,1)}, ...) custom-call(s32[2]{0:T(128)} %pad_add_fusion.ids, ...), custom_call_target="tpu_custom_call" | custom-call | tf_op jit(solution)/shard_map/route/pallas_call | solution.py:448
  74.1 1.6 collective-permute-start.11
  79.4 2.3 %collective-permute-start.17 = (bf16[8,32,128]{2,1,0:T(8,128)(2,1)}, bf16[8,32,128]{2,1,0:T(8,128)(2,1)S(1)}, u32[]{:S(2)}, u32[]{:S(2)}) collective-permute-start(bf16[8,32,128]{2,1,0:T(8,128)(2,1)} %get-tuple-element.75), channel_id=1, source_target_pairs={{0,5},{1,4},{2,7},{3,6},{4,1},{5,0},{6,3},{7,2},{8,13},{9,12},{10,... | collective-permute-start | bytes 196616 | tf_op jit(solution)/shard_map/ppermute | solution.py:983
  81.7 2.8 %collective-permute-start.18 = (bf16[8,32,128]{2,1,0:T(8,128)(2,1)}, bf16[8,32,128]{2,1,0:T(8,128)(2,1)S(1)}, u32[]{:S(2)}, u32[]{:S(2)}) collective-permute-start(bf16[8,32,128]{2,1,0:T(8,128)(2,1)} %get-tuple-element.76), channel_id=1, source_target_pairs={{0,6},{1,7},{2,4},{3,5},{4,2},{5,3},{6,0},{7,1},{8,14},{9,15},{10,... | collective-permute-start | bytes 196616 | tf_op jit(solution)/shard_map/ppermute | solution.py:983
  86.1 7.0 %visit.2 = (bf16[8,32,128]{2,1,0:T(8,128)(2,1)}, bf16[8,32,128]{2,1,0:T(8,128)(2,1)}, bf16[8,32,128]{2,1,0:T(8,128)(2,1)}, bf16[8,32,128]{2,1,0:T(8,128)(2,1)}) custom-call(s32[2]{0:T(128)} %pad_add_fusion.ids, bf16[8,32,128]{2,1,0:T(8,128)(2,1)} %get-tuple-element.64.refs_0_, bf16[8,32,128]{2,1,0:T(8,128)(2,1)} %copy-done.20, ...), custom_call_target="tpu_custom_call" | custom-call | flops 7200000000 | bytes 5242880 | tf_op jit(solution)/shard_map/visit/pallas_call | solution.py:646
  94.7 2.0 %collective-permute-start.15 = (bf16[8,32,128]{2,1,0:T(8,128)(2,1)}, bf16[8,32,128]{2,1,0:T(8,128)(2,1)S(1)}, u32[]{:S(2)}, u32[]{:S(2)}) collective-permute-start(bf16[8,32,128]{2,1,0:T(8,128)(2,1)} %get-tuple-element.73), channel_id=1, source_target_pairs={{0,3},{1,2},{2,1},{3,0},{4,7},{5,6},{6,5},{7,4},{8,11},{9,10},{10,... | collective-permute-start | bytes 196616 | tf_op jit(solution)/shard_map/ppermute | solution.py:983
  97.9 7.1 %visit.3 = (bf16[8,32,128]{2,1,0:T(8,128)(2,1)}, bf16[8,32,128]{2,1,0:T(8,128)(2,1)}, bf16[8,32,128]{2,1,0:T(8,128)(2,1)}, bf16[8,32,128]{2,1,0:T(8,128)(2,1)}) custom-call(s32[2]{0:T(128)} %pad_add_fusion.ids, bf16[8,32,128]{2,1,0:T(8,128)(2,1)} %copy-done.16, bf16[8,32,128]{2,1,0:T(8,128)(2,1)} %copy-done.17, bf16[8,32,128]{2,1,0:T(8,128)(2,1)} %copy-done.18, ...), custom_call_target="tpu_custom_call" | custom-call | flops 7200000000 | bytes 5242880 | tf_op jit(solution)/shard_map/visit/pallas_call | solution.py:646
  106.5 2.4 %collective-permute-start.21 = (bf16[8,32,128]{2,1,0:T(8,128)(2,1)}, bf16[8,32,128]{2,1,0:T(8,128)(2,1)S(1)}, u32[]{:S(2)}, u32[]{:S(2)}) collective-permute-start(bf16[8,32,128]{2,1,0:T(8,128)(2,1)} %get-tuple-element.79), channel_id=1, source_target_pairs={{0,5},{1,4},{2,7},{3,6},{4,1},{5,0},{6,3},{7,2},{8,13},{9,12},{10,... | collective-permute-start | bytes 196616 | tf_op jit(solution)/shard_map/ppermute | solution.py:983
  108.9 2.8 %collective-permute-start.22 = (bf16[8,32,128]{2,1,0:T(8,128)(2,1)}, bf16[8,32,128]{2,1,0:T(8,128)(2,1)S(1)}, u32[]{:S(2)}, u32[]{:S(2)}) collective-permute-start(bf16[8,32,128]{2,1,0:T(8,128)(2,1)} %get-tuple-element.80), channel_id=1, source_target_pairs={{0,6},{1,7},{2,4},{3,5},{4,2},{5,3},{6,0},{7,1},{8,14},{9,15},{10,... | collective-permute-start | bytes 196616 | tf_op jit(solution)/shard_map/ppermute | solution.py:983
  112.8 2.5 %collective-permute-done.22.refs_6_ = bf16[8,32,128]{2,1,0:T(8,128)(2,1)S(1)} collective-permute-done((bf16[8,32,128]{2,1,0:T(8,128)(2,1)}, bf16[8,32,128]{2,1,0:T(8,128)(2,1)S(1)}, u32[]{:S(2)}, u32[]{:S(2)}) %collective-permute-start.22) | collective-permute-done | bytes 65568 | tf_op jit(solution)/shard_map/ppermute | solution.py:983
  115.3 3.7 %collective-permute-done.23.refs_7_ = bf16[8,32,128]{2,1,0:T(8,128)(2,1)S(1)} collective-permute-done((bf16[8,32,128]{2,1,0:T(8,128)(2,1)}, bf16[8,32,128]{2,1,0:T(8,128)(2,1)S(1)}, u32[]{:S(2)}, u32[]{:S(2)}) %collective-permute-start.23) | collective-permute-done | bytes 65568 | tf_op jit(solution)/shard_map/ppermute | solution.py:983
  119.6 2.9 %unroute.1 = (bf16[128,256]{1,0:T(8,128)(2,1)}, bf16[128,256]{1,0:T(8,128)(2,1)}) custom-call(s32[128]{0:T(128)} %get-tuple-element.63.where_ref, bf16[8,32,128]{2,1,0:T(8,128)(2,1)} %get-tuple-element.70.refs_0_, bf16[8,32,128]{2,1,0:T(8,128)(2,1)} %copy-done.6, bf16[8,32,128]{2,1,0:T(8,128)(2,1)} %copy-done.7, bf16[8,32,128]{2,1,0:T(8,128)(2,1)} %copy-done.8, ...), custom_call_target="tpu_custom_call" | custom-call | tf_op jit(solution)/shard_map/unroute/pallas_call | solution.py:497
  122.5 2.9 %collective-permute-start.27 = (bf16[128,256]{1,0:T(8,128)(2,1)}, bf16[128,256]{1,0:T(8,128)(2,1)S(1)}, u32[]{:S(2)}, u32[]{:S(2)}) collective-permute-start(bf16[128,256]{1,0:T(8,128)(2,1)} %get-tuple-element.83), channel_id=1, source_target_pairs={{0,4},{1,5},{2,6},{3,7},{4,0},{5,1},{6,2},{7,3},{8,12},{9,13},{10,... | collective-permute-start | bytes 196616 | tf_op jit(solution)/shard_map/ppermute | solution.py:983
  125.4 2.4 %collective-permute-done.24 = bf16[128,256]{1,0:T(8,128)(2,1)S(1)} collective-permute-done((bf16[128,256]{1,0:T(8,128)(2,1)}, bf16[128,256]{1,0:T(8,128)(2,1)S(1)}, u32[]{:S(2)}, u32[]{:S(2)}) %collective-permute-start.24) | collective-permute-done | bytes 65568 | tf_op jit(solution)/shard_map/ppermute | solution.py:983
  130.1 1.6 collective-permute-start.28
  131.8 2.0 %collective-permute-done.25 = bf16[2,128,256]{2,1,0:T(8,128)(2,1)S(1)} collective-permute-done((bf16[2,128,256]{2,1,0:T(8,128)(2,1)S(1)}, bf16[2,128,256]{2,1,0:T(8,128)(2,1)S(1)}, u32[]{:S(2)}, u32[]{:S(2)}) %collective-permute-start.25) | collective-permute-done | bytes 131104 | tf_op jit(solution)/shard_map/ppermute | solution.py:983
  136.0 5.9 %collective-permute-done.26 = bf16[2,2,128,256]{3,2,0,1:T(8,128)(2,1)S(1)} collective-permute-done((bf16[2,2,128,256]{3,2,0,1:T(8,128)(2,1)S(1)}, bf16[2,2,128,256]{3,2,0,1:T(8,128)(2,1)S(1)}, u32[]{:S(2)}, u32[]{:S(2)}) %collective-permute-start.26) | collective-permute-done | bytes 262176 | tf_op jit(solution)/shard_map/ppermute | solution.py:983
  143.5 7.9 %adjoint_tables.1 = (bf16[16,512,256]{2,1,0:T(8,128)(2,1)}, f32[4096,128]{1,0:T(8,128)}) custom-call(s32[2]{0:T(128)} %pad_add_fusion.ids, s32[4]{0:T(128)} %row_off.7, f32[16,32,256]{2,1,0:T(8,128)} %constant.20.clone.tr_ref, f32[16,32,256]{2,1,0:T(8,128)} %constant.21.clone.ti_ref, f32[32,128]{1,0:T(8,128)} %bitcast.111), custom_call_target="tpu_custom_call" | custom-call | flops 7000000000 | bytes 7340032 | tf_op jit(solution)/shard_map/adjoint_tables/pallas_call | solution.py:798
  153.1 6.9 %cols_backward.1.even_ref = bf16[16,128,512]{2,1,0:T(8,128)(2,1)} custom-call(s32[2]{0:T(128)} %pad_add_fusion.ids, s32[4]{0:T(128)} %row_off.7, s32[4]{0:T(128)} %col_off.5, bf16[2,8,128,256]{3,2,1,0:T(8,128)(2,1)} %bitcast.88, bf16[2,8,128,256]{3,2,1,0:T(8,128)(2,1)} %bitcast.90, bf16[4096,512]{1,0:T(8,128)(2,1)} %constant.22.clone.fr_ref, ...), custom_call_target="tpu_custom_call" | custom-call | flops 5000000000 | bytes 6291456 | tf_op jit(solution)/shard_map/cols_backward/pallas_call | solution.py:756
  162.0 16.4 %backward.1 = bf16[2,16,256,512]{3,2,1,0:T(8,128)(2,1)} custom-call(s32[2]{0:T(128)} %pad_add_fusion.ids, s32[4]{0:T(128)} %row_off.7, s32[4]{0:T(128)} %col_off.5, bf16[2,8,128,256]{3,2,1,0:T(8,128)(2,1)} %copy-done.1, bf16[2,8,128,256]{3,2,1,0:T(8,128)(2,1)} %copy-done, bf16[4096,512]{1,0:T(8,128)(2,1)} %constant.22.clone.fr_ref, ...), custom_call_target="tpu_custom_call" | custom-call | tf_op jit(solution)/shard_map/backward/pallas_call | solution.py:950
  (124 shorter events, 35.7 us)
Async XLA Ops:
  19.5 6.9 %collective-permute-start = (bf16[2,8,128,256]{3,2,1,0:T(8,128)(2,1)}, bf16[2,8,128,256]{3,2,1,0:T(8,128)(2,1)S(1)}, u32[]{:S(2)}, u32[]{:S(2)}) collective-permute-start(bf16[2,8,128,256]{3,2,1,0:T(8,128)(2,1)} %get-tuple-element.51), channel_id=1, source_target_pairs={{0,8},{8,0},{16,24},{24,16},{1,9},{9,1},{17,25},{25,17},{2,10},{10... | collective-permute-start | bytes 3145736 | tf_op jit(solution)/shard_map/ppermute | solution.py:983
  20.0 7.9 %collective-permute-start.1 = (bf16[2,8,128,256]{3,2,1,0:T(8,128)(2,1)}, bf16[2,8,128,256]{3,2,1,0:T(8,128)(2,1)S(1)}, u32[]{:S(2)}, u32[]{:S(2)}) collective-permute-start(bf16[2,8,128,256]{3,2,1,0:T(8,128)(2,1)} %get-tuple-element.53), channel_id=1, source_target_pairs={{0,8},{8,0},{16,24},{24,16},{1,9},{9,1},{17,25},{25,17},{2,10},{10... | collective-permute-start | bytes 3145736 | tf_op jit(solution)/shard_map/ppermute | solution.py:983
  29.8 15.2 %collective-permute-start.2 = (bf16[2,2,2,128,256]{4,3,0,1,2:T(8,128)(2,1)S(1)}, bf16[2,2,2,128,256]{4,3,0,1,2:T(8,128)(2,1)S(1)}, u32[]{:S(2)}, u32[]{:S(2)}) collective-permute-start(bf16[2,2,2,128,256]{4,3,0,1,2:T(8,128)(2,1)S(1)} %copy.20), channel_id=1, source_target_pairs={{0,16},{8,24},{16,0},{24,8},{1,17},{9,25},{17,1},{25,9},{2,18},{10... | collective-permute-start | bytes 1572872 | tf_op jit(solution)/shard_map/ppermute | solution.py:983
  32.8 13.6 %collective-permute-start.3 = (bf16[2,2,2,128,256]{4,3,1,2,0:T(8,128)(2,1)S(1)}, bf16[2,2,2,128,256]{4,3,1,2,0:T(8,128)(2,1)S(1)}, u32[]{:S(2)}, u32[]{:S(2)}) collective-permute-start(bf16[2,2,2,128,256]{4,3,1,2,0:T(8,128)(2,1)S(1)} %bitcast.93), channel_id=1, source_target_pairs={{0,1},{1,0},{2,3},{3,2},{4,5},{5,4},{6,7},{7,6},{8,9},{9,8},{10,11... | collective-permute-start | bytes 1572872 | tf_op jit(solution)/shard_map/ppermute | solution.py:983
  46.5 7.2 %collective-permute-start.4 = (bf16[2,2,128,256]{3,2,0,1:T(8,128)(2,1)S(1)}, bf16[2,2,128,256]{3,2,0,1:T(8,128)(2,1)S(1)}, u32[]{:S(2)}, u32[]{:S(2)}) collective-permute-start(bf16[2,2,128,256]{3,2,0,1:T(8,128)(2,1)S(1)} %slice_bitcast_fusion.2), channel_id=1, source_target_pairs={{0,1},{1,0},{2,3},{3,2},{4,5},{5,4},{6,7},{7,6},{8,9},{9,8},{10,11... | collective-permute-start | bytes 786440 | tf_op jit(solution)/shard_map/ppermute | solution.py:983
  48.2 7.2 %collective-permute-start.7 = (bf16[2,2,128,256]{3,2,0,1:T(8,128)(2,1)S(1)}, bf16[2,2,128,256]{3,2,0,1:T(8,128)(2,1)S(1)}, u32[]{:S(2)}, u32[]{:S(2)}) collective-permute-start(bf16[2,2,128,256]{3,2,0,1:T(8,128)(2,1)S(1)} %slice_bitcast_fusion), channel_id=1, source_target_pairs={{0,16},{8,24},{16,0},{24,8},{1,17},{9,25},{17,1},{25,9},{2,18},{10... | collective-permute-start | bytes 786440 | tf_op jit(solution)/shard_map/ppermute | solution.py:983
  53.8 5.0 %collective-permute-start.5 = (bf16[2,128,256]{2,1,0:T(8,128)(2,1)S(1)}, bf16[2,128,256]{2,1,0:T(8,128)(2,1)S(1)}, u32[]{:S(2)}, u32[]{:S(2)}) collective-permute-start(bf16[2,128,256]{2,1,0:T(8,128)(2,1)S(1)} %slice_bitcast_fusion.6), channel_id=1, source_target_pairs={{0,2},{1,3},{2,0},{3,1},{4,6},{5,7},{6,4},{7,5},{8,10},{9,11},{10,... | collective-permute-start | bytes 393224 | tf_op jit(solution)/shard_map/ppermute | solution.py:983
  55.5 6.6 %collective-permute-start.8 = (bf16[2,128,256]{2,1,0:T(8,128)(2,1)S(1)}, bf16[2,128,256]{2,1,0:T(8,128)(2,1)S(1)}, u32[]{:S(2)}, u32[]{:S(2)}) collective-permute-start(bf16[2,128,256]{2,1,0:T(8,128)(2,1)S(1)} %slice_bitcast_fusion.4), channel_id=1, source_target_pairs={{0,2},{1,3},{2,0},{3,1},{4,6},{5,7},{6,4},{7,5},{8,10},{9,11},{10,... | collective-permute-start | bytes 393224 | tf_op jit(solution)/shard_map/ppermute | solution.py:983
  59.5 6.4 %collective-permute-start.6 = (bf16[128,256]{1,0:T(8,128)(2,1)S(1)}, bf16[128,256]{1,0:T(8,128)(2,1)S(1)}, u32[]{:S(2)}, u32[]{:S(2)}) collective-permute-start(bf16[128,256]{1,0:T(8,128)(2,1)S(1)} %get-tuple-element.107), channel_id=1, source_target_pairs={{0,4},{1,5},{2,6},{3,7},{4,0},{5,1},{6,2},{7,3},{8,12},{9,13},{10,... | collective-permute-start | bytes 196616 | tf_op jit(solution)/shard_map/ppermute | solution.py:983
  62.7 5.2 %collective-permute-start.9 = (bf16[128,256]{1,0:T(8,128)(2,1)S(1)}, bf16[128,256]{1,0:T(8,128)(2,1)S(1)}, u32[]{:S(2)}, u32[]{:S(2)}) collective-permute-start(bf16[128,256]{1,0:T(8,128)(2,1)S(1)} %get-tuple-element.105), channel_id=1, source_target_pairs={{0,4},{1,5},{2,6},{3,7},{4,0},{5,1},{6,2},{7,3},{8,12},{9,13},{10,... | collective-permute-start | bytes 196616 | tf_op jit(solution)/shard_map/ppermute | solution.py:983
  72.6 9.1 %collective-permute-start.10 = (bf16[8,32,128]{2,1,0:T(8,128)(2,1)}, bf16[8,32,128]{2,1,0:T(8,128)(2,1)S(1)}, u32[]{:S(2)}, u32[]{:S(2)}) collective-permute-start(bf16[8,32,128]{2,1,0:T(8,128)(2,1)} %get-tuple-element.65), channel_id=1, source_target_pairs={{0,1},{1,0},{2,3},{3,2},{4,5},{5,4},{6,7},{7,6},{8,9},{9,8},{10,11... | collective-permute-start | bytes 196616 | tf_op jit(solution)/shard_map/ppermute | solution.py:983
  74.1 10.3 %collective-permute-start.11 = (bf16[8,32,128]{2,1,0:T(8,128)(2,1)}, bf16[8,32,128]{2,1,0:T(8,128)(2,1)S(1)}, u32[]{:S(2)}, u32[]{:S(2)}) collective-permute-start(bf16[8,32,128]{2,1,0:T(8,128)(2,1)} %get-tuple-element.66), channel_id=1, source_target_pairs={{0,2},{1,3},{2,0},{3,1},{4,6},{5,7},{6,4},{7,5},{8,10},{9,11},{10,... | collective-permute-start | bytes 196616 | tf_op jit(solution)/shard_map/ppermute | solution.py:983
  75.7 9.8 %collective-permute-start.12 = (bf16[8,32,128]{2,1,0:T(8,128)(2,1)}, bf16[8,32,128]{2,1,0:T(8,128)(2,1)S(1)}, u32[]{:S(2)}, u32[]{:S(2)}) collective-permute-start(bf16[8,32,128]{2,1,0:T(8,128)(2,1)} %get-tuple-element.67), channel_id=1, source_target_pairs={{0,3},{1,2},{2,1},{3,0},{4,7},{5,6},{6,5},{7,4},{8,11},{9,10},{10,... | collective-permute-start | bytes 196616 | tf_op jit(solution)/shard_map/ppermute | solution.py:983
  77.8 16.8 %collective-permute-start.16 = (bf16[8,32,128]{2,1,0:T(8,128)(2,1)}, bf16[8,32,128]{2,1,0:T(8,128)(2,1)S(1)}, u32[]{:S(2)}, u32[]{:S(2)}) collective-permute-start(bf16[8,32,128]{2,1,0:T(8,128)(2,1)} %get-tuple-element.74), channel_id=1, source_target_pairs={{0,4},{1,5},{2,6},{3,7},{4,0},{5,1},{6,2},{7,3},{8,12},{9,13},{10,... | collective-permute-start | bytes 196616 | tf_op jit(solution)/shard_map/ppermute | solution.py:983
  79.4 15.2 %collective-permute-start.17 = (bf16[8,32,128]{2,1,0:T(8,128)(2,1)}, bf16[8,32,128]{2,1,0:T(8,128)(2,1)S(1)}, u32[]{:S(2)}, u32[]{:S(2)}) collective-permute-start(bf16[8,32,128]{2,1,0:T(8,128)(2,1)} %get-tuple-element.75), channel_id=1, source_target_pairs={{0,5},{1,4},{2,7},{3,6},{4,1},{5,0},{6,3},{7,2},{8,13},{9,12},{10,... | collective-permute-start | bytes 196616 | tf_op jit(solution)/shard_map/ppermute | solution.py:983
  81.7 14.9 %collective-permute-start.18 = (bf16[8,32,128]{2,1,0:T(8,128)(2,1)}, bf16[8,32,128]{2,1,0:T(8,128)(2,1)S(1)}, u32[]{:S(2)}, u32[]{:S(2)}) collective-permute-start(bf16[8,32,128]{2,1,0:T(8,128)(2,1)} %get-tuple-element.76), channel_id=1, source_target_pairs={{0,6},{1,7},{2,4},{3,5},{4,2},{5,3},{6,0},{7,1},{8,14},{9,15},{10,... | collective-permute-start | bytes 196616 | tf_op jit(solution)/shard_map/ppermute | solution.py:983
  84.5 12.2 %collective-permute-start.19 = (bf16[8,32,128]{2,1,0:T(8,128)(2,1)}, bf16[8,32,128]{2,1,0:T(8,128)(2,1)S(1)}, u32[]{:S(2)}, u32[]{:S(2)}) collective-permute-start(bf16[8,32,128]{2,1,0:T(8,128)(2,1)} %get-tuple-element.77), channel_id=1, source_target_pairs={{0,7},{1,6},{2,5},{3,4},{4,3},{5,2},{6,1},{7,0},{8,15},{9,14},{10,... | collective-permute-start | bytes 196616 | tf_op jit(solution)/shard_map/ppermute | solution.py:983
  93.1 15.8 %collective-permute-start.13 = (bf16[8,32,128]{2,1,0:T(8,128)(2,1)}, bf16[8,32,128]{2,1,0:T(8,128)(2,1)S(1)}, u32[]{:S(2)}, u32[]{:S(2)}) collective-permute-start(bf16[8,32,128]{2,1,0:T(8,128)(2,1)} %get-tuple-element.71), channel_id=1, source_target_pairs={{0,1},{1,0},{2,3},{3,2},{4,5},{5,4},{6,7},{7,6},{8,9},{9,8},{10,11... | collective-permute-start | bytes 196616 | tf_op jit(solution)/shard_map/ppermute | solution.py:983
  94.6 17.0 %collective-permute-start.14 = (bf16[8,32,128]{2,1,0:T(8,128)(2,1)}, bf16[8,32,128]{2,1,0:T(8,128)(2,1)S(1)}, u32[]{:S(2)}, u32[]{:S(2)}) collective-permute-start(bf16[8,32,128]{2,1,0:T(8,128)(2,1)} %get-tuple-element.72), channel_id=1, source_target_pairs={{0,2},{1,3},{2,0},{3,1},{4,6},{5,7},{6,4},{7,5},{8,10},{9,11},{10,... | collective-permute-start | bytes 196616 | tf_op jit(solution)/shard_map/ppermute | solution.py:983
  94.7 18.1 %collective-permute-start.15 = (bf16[8,32,128]{2,1,0:T(8,128)(2,1)}, bf16[8,32,128]{2,1,0:T(8,128)(2,1)S(1)}, u32[]{:S(2)}, u32[]{:S(2)}) collective-permute-start(bf16[8,32,128]{2,1,0:T(8,128)(2,1)} %get-tuple-element.73), channel_id=1, source_target_pairs={{0,3},{1,2},{2,1},{3,0},{4,7},{5,6},{6,5},{7,4},{8,11},{9,10},{10,... | collective-permute-start | bytes 196616 | tf_op jit(solution)/shard_map/ppermute | solution.py:983
  105.0 7.7 %collective-permute-start.20 = (bf16[8,32,128]{2,1,0:T(8,128)(2,1)}, bf16[8,32,128]{2,1,0:T(8,128)(2,1)S(1)}, u32[]{:S(2)}, u32[]{:S(2)}) collective-permute-start(bf16[8,32,128]{2,1,0:T(8,128)(2,1)} %get-tuple-element.78), channel_id=1, source_target_pairs={{0,4},{1,5},{2,6},{3,7},{4,0},{5,1},{6,2},{7,3},{8,12},{9,13},{10,... | collective-permute-start | bytes 196616 | tf_op jit(solution)/shard_map/ppermute | solution.py:983
  106.5 6.3 %collective-permute-start.21 = (bf16[8,32,128]{2,1,0:T(8,128)(2,1)}, bf16[8,32,128]{2,1,0:T(8,128)(2,1)S(1)}, u32[]{:S(2)}, u32[]{:S(2)}) collective-permute-start(bf16[8,32,128]{2,1,0:T(8,128)(2,1)} %get-tuple-element.79), channel_id=1, source_target_pairs={{0,5},{1,4},{2,7},{3,6},{4,1},{5,0},{6,3},{7,2},{8,13},{9,12},{10,... | collective-permute-start | bytes 196616 | tf_op jit(solution)/shard_map/ppermute | solution.py:983
  108.9 6.4 %collective-permute-start.22 = (bf16[8,32,128]{2,1,0:T(8,128)(2,1)}, bf16[8,32,128]{2,1,0:T(8,128)(2,1)S(1)}, u32[]{:S(2)}, u32[]{:S(2)}) collective-permute-start(bf16[8,32,128]{2,1,0:T(8,128)(2,1)} %get-tuple-element.80), channel_id=1, source_target_pairs={{0,6},{1,7},{2,4},{3,5},{4,2},{5,3},{6,0},{7,1},{8,14},{9,15},{10,... | collective-permute-start | bytes 196616 | tf_op jit(solution)/shard_map/ppermute | solution.py:983
  111.7 7.3 %collective-permute-start.23 = (bf16[8,32,128]{2,1,0:T(8,128)(2,1)}, bf16[8,32,128]{2,1,0:T(8,128)(2,1)S(1)}, u32[]{:S(2)}, u32[]{:S(2)}) collective-permute-start(bf16[8,32,128]{2,1,0:T(8,128)(2,1)} %get-tuple-element.81), channel_id=1, source_target_pairs={{0,7},{1,6},{2,5},{3,4},{4,3},{5,2},{6,1},{7,0},{8,15},{9,14},{10,... | collective-permute-start | bytes 196616 | tf_op jit(solution)/shard_map/ppermute | solution.py:983
  122.5 5.4 %collective-permute-start.24 = (bf16[128,256]{1,0:T(8,128)(2,1)}, bf16[128,256]{1,0:T(8,128)(2,1)S(1)}, u32[]{:S(2)}, u32[]{:S(2)}) collective-permute-start(bf16[128,256]{1,0:T(8,128)(2,1)} %get-tuple-element.82), channel_id=1, source_target_pairs={{0,4},{1,5},{2,6},{3,7},{4,0},{5,1},{6,2},{7,3},{8,12},{9,13},{10,... | collective-permute-start | bytes 196616 | tf_op jit(solution)/shard_map/ppermute | solution.py:983
  122.5 6.8 %collective-permute-start.27 = (bf16[128,256]{1,0:T(8,128)(2,1)}, bf16[128,256]{1,0:T(8,128)(2,1)S(1)}, u32[]{:S(2)}, u32[]{:S(2)}) collective-permute-start(bf16[128,256]{1,0:T(8,128)(2,1)} %get-tuple-element.83), channel_id=1, source_target_pairs={{0,4},{1,5},{2,6},{3,7},{4,0},{5,1},{6,2},{7,3},{8,12},{9,13},{10,... | collective-permute-start | bytes 196616 | tf_op jit(solution)/shard_map/ppermute | solution.py:983
  133.8 8.1 %collective-permute-start.26 = (bf16[2,2,128,256]{3,2,0,1:T(8,128)(2,1)S(1)}, bf16[2,2,128,256]{3,2,0,1:T(8,128)(2,1)S(1)}, u32[]{:S(2)}, u32[]{:S(2)}) collective-permute-start(bf16[2,2,128,256]{3,2,0,1:T(8,128)(2,1)S(1)} %get-tuple-element.100), channel_id=1, source_target_pairs={{0,1},{1,0},{2,3},{3,2},{4,5},{5,4},{6,7},{7,6},{8,9},{9,8},{10,11... | collective-permute-start | bytes 786440 | tf_op jit(solution)/shard_map/ppermute | solution.py:983
  135.2 6.8 %collective-permute-start.29 = (bf16[2,2,128,256]{3,2,0,1:T(8,128)(2,1)S(1)}, bf16[2,2,128,256]{3,2,0,1:T(8,128)(2,1)S(1)}, u32[]{:S(2)}, u32[]{:S(2)}) collective-permute-start(bf16[2,2,128,256]{3,2,0,1:T(8,128)(2,1)S(1)} %get-tuple-element.98), channel_id=1, source_target_pairs={{0,16},{8,24},{16,0},{24,8},{1,17},{9,25},{17,1},{25,9},{2,18},{10... | collective-permute-start | bytes 786440 | tf_op jit(solution)/shard_map/ppermute | solution.py:983
  142.0 9.4 %collective-permute-start.30 = (bf16[2,2,2,128,256]{4,3,0,1,2:T(8,128)(2,1)S(1)}, bf16[2,2,2,128,256]{4,3,0,1,2:T(8,128)(2,1)S(1)}, u32[]{:S(2)}, u32[]{:S(2)}) collective-permute-start(bf16[2,2,2,128,256]{4,3,0,1,2:T(8,128)(2,1)S(1)} %pad_maximum_fusion.2), channel_id=1, source_target_pairs={{0,16},{8,24},{16,0},{24,8},{1,17},{9,25},{17,1},{25,9},{2,18},{10... | collective-permute-start | bytes 1572872 | tf_op jit(solution)/shard_map/ppermute | solution.py:983
  142.5 9.2 %collective-permute-start.31 = (bf16[2,2,2,128,256]{4,3,1,2,0:T(8,128)(2,1)S(1)}, bf16[2,2,2,128,256]{4,3,1,2,0:T(8,128)(2,1)S(1)}, u32[]{:S(2)}, u32[]{:S(2)}) collective-permute-start(bf16[2,2,2,128,256]{4,3,1,2,0:T(8,128)(2,1)S(1)} %pad_maximum_fusion.3), channel_id=1, source_target_pairs={{0,1},{1,0},{2,3},{3,2},{4,5},{5,4},{6,7},{7,6},{8,9},{9,8},{10,11... | collective-permute-start | bytes 1572872 | tf_op jit(solution)/shard_map/ppermute | solution.py:983
  151.9 8.1 %collective-permute-start.33 = (bf16[2,8,128,256]{3,2,1,0:T(8,128)(2,1)S(1)}, bf16[2,8,128,256]{3,2,1,0:T(8,128)(2,1)S(1)}, u32[]{:S(2)}, u32[]{:S(2)}) collective-permute-start(bf16[2,8,128,256]{3,2,1,0:T(8,128)(2,1)S(1)} %bitcast.89), channel_id=1, source_target_pairs={{0,8},{8,0},{16,24},{24,16},{1,9},{9,1},{17,25},{25,17},{2,10},{10... | collective-permute-start | bytes 3145736 | tf_op jit(solution)/shard_map/ppermute | solution.py:983
  152.0 8.0 %collective-permute-start.32 = (bf16[2,8,128,256]{3,2,1,0:T(8,128)(2,1)S(1)}, bf16[2,8,128,256]{3,2,1,0:T(8,128)(2,1)S(1)}, u32[]{:S(2)}, u32[]{:S(2)}) collective-permute-start(bf16[2,8,128,256]{3,2,1,0:T(8,128)(2,1)S(1)} %bitcast.87), channel_id=1, source_target_pairs={{0,8},{8,0},{16,24},{24,16},{1,9},{9,1},{17,25},{25,17},{2,10},{10... | collective-permute-start | bytes 3145736 | tf_op jit(solution)/shard_map/ppermute | solution.py:983
  (25 other events, 169.2 us)

commit v4 on v3

--- a/solution.py
+++ b/solution.py
@@ -435,7 +435,7 @@
             slots[g] = jnp.where(lane == sl, moved, slots[g])
         return carry
 
-    lax.fori_loop(0, tile_rows * chunks, per_chunk, 0)
+    lax.fori_loop(0, tile_rows * chunks, per_chunk, 0, unroll=4)
     for o in range(subs):
         outs[o][...] = slots[o * groups : (o + 1) * groups].astype(BF16)
 
@@ -482,7 +482,7 @@
             held[chunk, pl.ds(r2, 2 * TS, stride=tile_rows), :] = total
         return carry
 
-    lax.fori_loop(0, tile_rows, per_row, 0)
+    lax.fori_loop(0, tile_rows, per_row, 0, unroll=2 if tile_rows > 1 else 1)
     for chunk in range(chunks):
         out_ref = a_ref if chunk < chunks // 2 else b_ref
         at = (chunk % (chunks // 2)) * LANES
@@ -999,7 +999,7 @@
 
 def sum_blocks(kept, sent, beside, operand):
     values = [k + swap(s, "facet", 1) for k, s in zip(kept, sent)]
-    values, operand = lax.optimization_barrier((values, operand))
+    values[0], operand = lax.optimization_barrier((values[0], operand))
     extra = beside(operand)
     left = [dimensions(), dimensions()]
     values = [value.reshape((2,) * len(left[0]) + value.shape[2:]) for value in values]
@@ -1096,13 +1096,20 @@
         value = jnp.pad(value, ((0, 0), (0, padded - capacity)) + ((0, 0),) * (value.ndim - 2))
         return value.reshape((sub_count * padded,) + value.shape[2:])
 
-    visits = vis_weight.shape[3]
-    live = jnp.arange(visits, dtype=jnp.int32)[None, :] < vis_count[0, 0][:, None]
-    weights = per_slot(jnp.where(live, vis_weight[0, 0], 0.0))
-    values = jnp.transpose(per_slot(measured[0, 0]), (1, 0, 2))
-    pixels = jnp.transpose(per_slot(uvw_pixels[0, 0]), (1, 0, 2))
-
-    parts, (row_kernels, col_kernels) = sum_blocks(kept, sent, partial(kernels, steps=4), pixels)
+    def prepare(operand):
+        pixels, values, weights, counts = operand
+        live = jnp.arange(weights.shape[1], dtype=jnp.int32)[None, :] < counts[:, None]
+        weights = per_slot(jnp.where(live, weights, 0.0))
+        values = jnp.transpose(per_slot(values), (1, 0, 2))
+        pixels = jnp.transpose(per_slot(pixels), (1, 0, 2))
+        return values, weights, kernels(pixels, 4)
+
+    parts, (values, weights, (row_kernels, col_kernels)) = sum_blocks(
+        kept,
+        sent,
+        prepare,
+        (uvw_pixels[0, 0], measured[0, 0], vis_weight[0, 0], vis_count[0, 0]),
+    )
     routed = route(ids, owners, parts, sub_count, groups)
     outgoing, where = routed[:-1], routed[-1]
     arrived = [outgoing[0]] + [swap(outgoing[r], "sub", r) for r in range(1, sub_count)]

time: 179 us -> 177 us (0.989)
    unnamed x49 -> x51, local copies, waits for them, and re-layouts: 6.62 us -> 6.6 us
  transfers between devices with their start and end apart: 34 -> 34, of which waited for: 15 -> 14; matrix products, arithmetic and copies ran while one was open for 4% -> 4% of each run, Pallas kernels for 23% -> 24%
where the time goes in v4:
time: 177 us; the launch traced here: 176 us
  Pallas kernels  83.3 us (47%)
  starting transfers between devices  45.8 us (26%)
  waiting for transfers between devices  32.3 us (18%)
  local copies, waits for them, and re-layouts  8.26 us (5%)
  other arithmetic  5.72 us (3%)
    ppermute x34, starting transfers between devices, swap(): lax.ppermute(value, axis, [(i, i ^ bit) for i in range(lax.axis_size(axis...  45.8 us
    ppermute x34, waiting for transfers between devices, swap(): lax.ppermute(value, axis, [(i, i ^ bit) for i in range(lax.axis_size(axis...  32.3 us
    pallas_call x1, Pallas kernels, forward(): pl.pallas_call(forward_kernel, grid_spec=pltpu.PrefetchScalarGridSpec(num...  19 us
    pallas_call x1, Pallas kernels, backward(): pl.pallas_call(backward_kernel, grid_spec=pltpu.PrefetchScalarGridSpec(nu...  16.4 us
    pallas_call x2, Pallas kernels, visit(): pl.pallas_call(visit_kernel, grid_spec=pltpu.PrefetchScalarGridSpec(num_s...  14.1 us
    pallas_call x1, Pallas kernels, adjoint_tables(): pl.pallas_call(adjoint_tables_kernel, in_specs=[smem] * 2 + [vmem] * 3, o...  7.91 us
    pallas_call x1, Pallas kernels, cols_backward(): pl.pallas_call(partial(cols_backward_kernel, length=length), grid_spec=pl...  6.87 us
    unnamed x51, local copies, waits for them, and re-layouts  6.6 us
  transfers between devices with their start and end apart: 34, of which 14 were waited for; matrix products, arithmetic and copies ran while one was open for 4% of the time, Pallas kernels for 24%

profile of v4, /device:TPU:0, one launch (start us, length us, event | category | flops | bytes accessed | tf_op | source)
XLA Modules:
  0.0 175.9 jit_solution(10816941560021162566)
XLA Ops:
  0.6 19.0 %forward.1 = (bf16[2,2,16,32,512]{4,3,2,1,0:T(8,128)(2,1)}, bf16[2,8,128,256]{3,2,1,0:T(8,128)(2,1)}, bf16[2,8,128,256]{3,2,1,0:T(8,128)(2,1)}) custom-call(s32[2]{0:T(128)} %pad_add_fusion.ids, s32[4]{0:T(128)} %row_off.7, s32[4]{0:T(128)} %col_off.5, bf16[2,4096,512]{2,1,0:T(8,128)(2,1)} %x_ref.1, f32[32,128]{1,0:T(8,128)} %bitcast.108, ...), custom_call_target="tpu_custom_call" | custom-call | flops 12000000000 | bytes 16777216 | tf_op jit(solution)/shard_map/forward/pallas_call | solution.py:328
  21.0 6.3 %cols_forward.1 = (bf16[2,8,128,256]{3,2,1,0:T(8,128)(2,1)}, bf16[2,8,128,256]{3,2,1,0:T(8,128)(2,1)}) custom-call(s32[2]{0:T(128)} %pad_add_fusion.ids, bf16[2,2,512,512]{3,2,1,0:T(8,128)(2,1)} %bitcast.110, bf16[4096,512]{1,0:T(8,128)(2,1)} %constant.22.clone.fr_ref, bf16[4096,512]{1,0:T(8,128)(2,1)} %constant.23.clone.fi_ref), custom_call_target="tpu_custom_call" | custom-call | flops 4000000000 | bytes 6291456 | tf_op jit(solution)/shard_map/cols_forward/pallas_call | solution.py:380
  27.3 1.6 add.24
  29.1 3.0 %collective-permute-start.1 = (bf16[2,2,2,128,256]{4,3,0,1,2:T(8,128)(2,1)S(1)}, bf16[2,2,2,128,256]{4,3,0,1,2:T(8,128)(2,1)S(1)}, u32[]{:S(2)}, u32[]{:S(2)}) collective-permute-start(bf16[2,2,2,128,256]{4,3,0,1,2:T(8,128)(2,1)S(1)} %copy.21), channel_id=1, source_target_pairs={{0,16},{8,24},{16,0},{24,8},{1,17},{9,25},{17,1},{25,9},{2,18},{10... | collective-permute-start | bytes 1572872 | tf_op jit(solution)/shard_map/ppermute | solution.py:983
  35.0 6.5 %kernels.1 = (bf16[64,2,128,128]{3,2,1,0:T(8,128)(2,1)}, bf16[64,128,256]{2,1,0:T(8,128)(2,1)}) custom-call(s32[3,512,128]{2,1,0:T(8,128)} %bitcast.107), custom_call_target="tpu_custom_call" | custom-call | flops 6000000000 | bytes 9437184 | tf_op jit(solution)/shard_map/kernels/pallas_call | solution.py:570
  41.6 2.7 %collective-permute-done.1 = bf16[2,2,2,128,256]{4,3,0,1,2:T(8,128)(2,1)S(1)} collective-permute-done((bf16[2,2,2,128,256]{4,3,0,1,2:T(8,128)(2,1)S(1)}, bf16[2,2,2,128,256]{4,3,0,1,2:T(8,128)(2,1)S(1)}, u32[]{:S(2)}, u32[]{:S(2)}) %collective-permute-start.1) | collective-permute-done | bytes 524320 | tf_op jit(solution)/shard_map/ppermute | solution.py:983
  44.3 2.0 %collective-permute-done.3 = bf16[2,2,2,128,256]{4,3,1,2,0:T(8,128)(2,1)S(1)} collective-permute-done((bf16[2,2,2,128,256]{4,3,1,2,0:T(8,128)(2,1)S(1)}, bf16[2,2,2,128,256]{4,3,1,2,0:T(8,128)(2,1)S(1)}, u32[]{:S(2)}, u32[]{:S(2)}) %collective-permute-start.3) | collective-permute-done | bytes 524320 | tf_op jit(solution)/shard_map/ppermute | solution.py:983
  48.7 4.9 %collective-permute-done.4 = bf16[2,2,128,256]{3,2,0,1:T(8,128)(2,1)S(1)} collective-permute-done((bf16[2,2,128,256]{3,2,0,1:T(8,128)(2,1)S(1)}, bf16[2,2,128,256]{3,2,0,1:T(8,128)(2,1)S(1)}, u32[]{:S(2)}, u32[]{:S(2)}) %collective-permute-start.4) | collective-permute-done | bytes 262176 | tf_op jit(solution)/shard_map/ppermute | solution.py:983
  53.7 1.6 collective-permute-start.5
  56.7 2.0 %collective-permute-done.5 = bf16[2,128,256]{2,1,0:T(8,128)(2,1)S(1)} collective-permute-done((bf16[2,128,256]{2,1,0:T(8,128)(2,1)S(1)}, bf16[2,128,256]{2,1,0:T(8,128)(2,1)S(1)}, u32[]{:S(2)}, u32[]{:S(2)}) %collective-permute-start.5) | collective-permute-done | bytes 131104 | tf_op jit(solution)/shard_map/ppermute | solution.py:983
  59.3 2.6 %collective-permute-start.6 = (bf16[128,256]{1,0:T(8,128)(2,1)S(1)}, bf16[128,256]{1,0:T(8,128)(2,1)S(1)}, u32[]{:S(2)}, u32[]{:S(2)}) collective-permute-start(bf16[128,256]{1,0:T(8,128)(2,1)S(1)} %get-tuple-element.115), channel_id=1, source_target_pairs={{0,4},{1,5},{2,6},{3,7},{4,0},{5,1},{6,2},{7,3},{8,12},{9,13},{10,... | collective-permute-start | bytes 196616 | tf_op jit(solution)/shard_map/ppermute | solution.py:983
  64.0 1.7 collective-permute-done.6.refs_1_
  65.8 2.0 %collective-permute-done.9.refs_3_ = bf16[128,256]{1,0:T(8,128)(2,1)S(1)} collective-permute-done((bf16[128,256]{1,0:T(8,128)(2,1)S(1)}, bf16[128,256]{1,0:T(8,128)(2,1)S(1)}, u32[]{:S(2)}, u32[]{:S(2)}) %collective-permute-start.9) | collective-permute-done | bytes 65568 | tf_op jit(solution)/shard_map/ppermute | solution.py:983
  68.4 3.5 %route.1 = (bf16[8,32,128]{2,1,0:T(8,128)(2,1)}, bf16[8,32,128]{2,1,0:T(8,128)(2,1)}, bf16[8,32,128]{2,1,0:T(8,128)(2,1)}, bf16[8,32,128]{2,1,0:T(8,128)(2,1)}, ...) custom-call(s32[2]{0:T(128)} %pad_add_fusion.ids, ...), custom_call_target="tpu_custom_call" | custom-call | tf_op jit(solution)/shard_map/route/pallas_call | solution.py:448
  77.0 2.3 %collective-permute-start.17 = (bf16[8,32,128]{2,1,0:T(8,128)(2,1)}, bf16[8,32,128]{2,1,0:T(8,128)(2,1)S(1)}, u32[]{:S(2)}, u32[]{:S(2)}) collective-permute-start(bf16[8,32,128]{2,1,0:T(8,128)(2,1)} %get-tuple-element.83), channel_id=1, source_target_pairs={{0,5},{1,4},{2,7},{3,6},{4,1},{5,0},{6,3},{7,2},{8,13},{9,12},{10,... | collective-permute-start | bytes 196616 | tf_op jit(solution)/shard_map/ppermute | solution.py:983
  79.3 2.8 %collective-permute-start.18 = (bf16[8,32,128]{2,1,0:T(8,128)(2,1)}, bf16[8,32,128]{2,1,0:T(8,128)(2,1)S(1)}, u32[]{:S(2)}, u32[]{:S(2)}) collective-permute-start(bf16[8,32,128]{2,1,0:T(8,128)(2,1)} %get-tuple-element.84), channel_id=1, source_target_pairs={{0,6},{1,7},{2,4},{3,5},{4,2},{5,3},{6,0},{7,1},{8,14},{9,15},{10,... | collective-permute-start | bytes 196616 | tf_op jit(solution)/shard_map/ppermute | solution.py:983
  83.7 6.9 %visit.2 = (bf16[8,32,128]{2,1,0:T(8,128)(2,1)}, bf16[8,32,128]{2,1,0:T(8,128)(2,1)}, bf16[8,32,128]{2,1,0:T(8,128)(2,1)}, bf16[8,32,128]{2,1,0:T(8,128)(2,1)}) custom-call(s32[2]{0:T(128)} %pad_add_fusion.ids, bf16[8,32,128]{2,1,0:T(8,128)(2,1)} %get-tuple-element.70.refs_0_, bf16[8,32,128]{2,1,0:T(8,128)(2,1)} %copy-done.21, ...), custom_call_target="tpu_custom_call" | custom-call | flops 7200000000 | bytes 5242880 | tf_op jit(solution)/shard_map/visit/pallas_call | solution.py:646
  92.2 2.0 %collective-permute-start.15 = (bf16[8,32,128]{2,1,0:T(8,128)(2,1)}, bf16[8,32,128]{2,1,0:T(8,128)(2,1)S(1)}, u32[]{:S(2)}, u32[]{:S(2)}) collective-permute-start(bf16[8,32,128]{2,1,0:T(8,128)(2,1)} %get-tuple-element.81), channel_id=1, source_target_pairs={{0,3},{1,2},{2,1},{3,0},{4,7},{5,6},{6,5},{7,4},{8,11},{9,10},{10,... | collective-permute-start | bytes 196616 | tf_op jit(solution)/shard_map/ppermute | solution.py:983
  95.4 7.1 %visit.3 = (bf16[8,32,128]{2,1,0:T(8,128)(2,1)}, bf16[8,32,128]{2,1,0:T(8,128)(2,1)}, bf16[8,32,128]{2,1,0:T(8,128)(2,1)}, bf16[8,32,128]{2,1,0:T(8,128)(2,1)}) custom-call(s32[2]{0:T(128)} %pad_add_fusion.ids, bf16[8,32,128]{2,1,0:T(8,128)(2,1)} %copy-done.17, bf16[8,32,128]{2,1,0:T(8,128)(2,1)} %copy-done.18, bf16[8,32,128]{2,1,0:T(8,128)(2,1)} %copy-done.19, ...), custom_call_target="tpu_custom_call" | custom-call | flops 7200000000 | bytes 5242880 | tf_op jit(solution)/shard_map/visit/pallas_call | solution.py:646
  104.1 2.3 %collective-permute-start.21 = (bf16[8,32,128]{2,1,0:T(8,128)(2,1)}, bf16[8,32,128]{2,1,0:T(8,128)(2,1)S(1)}, u32[]{:S(2)}, u32[]{:S(2)}) collective-permute-start(bf16[8,32,128]{2,1,0:T(8,128)(2,1)} %get-tuple-element.87), channel_id=1, source_target_pairs={{0,5},{1,4},{2,7},{3,6},{4,1},{5,0},{6,3},{7,2},{8,13},{9,12},{10,... | collective-permute-start | bytes 196616 | tf_op jit(solution)/shard_map/ppermute | solution.py:983
  106.4 2.8 %collective-permute-start.22 = (bf16[8,32,128]{2,1,0:T(8,128)(2,1)}, bf16[8,32,128]{2,1,0:T(8,128)(2,1)S(1)}, u32[]{:S(2)}, u32[]{:S(2)}) collective-permute-start(bf16[8,32,128]{2,1,0:T(8,128)(2,1)} %get-tuple-element.88), channel_id=1, source_target_pairs={{0,6},{1,7},{2,4},{3,5},{4,2},{5,3},{6,0},{7,1},{8,14},{9,15},{10,... | collective-permute-start | bytes 196616 | tf_op jit(solution)/shard_map/ppermute | solution.py:983
  110.4 2.6 %collective-permute-done.22.refs_6_ = bf16[8,32,128]{2,1,0:T(8,128)(2,1)S(1)} collective-permute-done((bf16[8,32,128]{2,1,0:T(8,128)(2,1)}, bf16[8,32,128]{2,1,0:T(8,128)(2,1)S(1)}, u32[]{:S(2)}, u32[]{:S(2)}) %collective-permute-start.22) | collective-permute-done | bytes 65568 | tf_op jit(solution)/shard_map/ppermute | solution.py:983
  113.0 3.4 %collective-permute-done.23.refs_7_ = bf16[8,32,128]{2,1,0:T(8,128)(2,1)S(1)} collective-permute-done((bf16[8,32,128]{2,1,0:T(8,128)(2,1)}, bf16[8,32,128]{2,1,0:T(8,128)(2,1)S(1)}, u32[]{:S(2)}, u32[]{:S(2)}) %collective-permute-start.23) | collective-permute-done | bytes 65568 | tf_op jit(solution)/shard_map/ppermute | solution.py:983
  117.0 2.8 %unroute.1 = (bf16[128,256]{1,0:T(8,128)(2,1)}, bf16[128,256]{1,0:T(8,128)(2,1)}) custom-call(s32[128]{0:T(128)} %get-tuple-element.69.where_ref, bf16[8,32,128]{2,1,0:T(8,128)(2,1)} %get-tuple-element.78.refs_0_, bf16[8,32,128]{2,1,0:T(8,128)(2,1)} %copy-done.7, bf16[8,32,128]{2,1,0:T(8,128)(2,1)} %copy-done.8, bf16[8,32,128]{2,1,0:T(8,128)(2,1)} %copy-done.9, ...), custom_call_target="tpu_custom_call" | custom-call | tf_op jit(solution)/shard_map/unroute/pallas_call | solution.py:497
  119.8 2.9 %collective-permute-start.27 = (bf16[128,256]{1,0:T(8,128)(2,1)}, bf16[128,256]{1,0:T(8,128)(2,1)S(1)}, u32[]{:S(2)}, u32[]{:S(2)}) collective-permute-start(bf16[128,256]{1,0:T(8,128)(2,1)} %get-tuple-element.91), channel_id=1, source_target_pairs={{0,4},{1,5},{2,6},{3,7},{4,0},{5,1},{6,2},{7,3},{8,12},{9,13},{10,... | collective-permute-start | bytes 196616 | tf_op jit(solution)/shard_map/ppermute | solution.py:983
  122.7 2.4 %collective-permute-done.24 = bf16[128,256]{1,0:T(8,128)(2,1)S(1)} collective-permute-done((bf16[128,256]{1,0:T(8,128)(2,1)}, bf16[128,256]{1,0:T(8,128)(2,1)S(1)}, u32[]{:S(2)}, u32[]{:S(2)}) %collective-permute-start.24) | collective-permute-done | bytes 65568 | tf_op jit(solution)/shard_map/ppermute | solution.py:983
  127.4 1.6 collective-permute-start.28
  129.1 2.0 %collective-permute-done.25 = bf16[2,128,256]{2,1,0:T(8,128)(2,1)S(1)} collective-permute-done((bf16[2,128,256]{2,1,0:T(8,128)(2,1)S(1)}, bf16[2,128,256]{2,1,0:T(8,128)(2,1)S(1)}, u32[]{:S(2)}, u32[]{:S(2)}) %collective-permute-start.25) | collective-permute-done | bytes 131104 | tf_op jit(solution)/shard_map/ppermute | solution.py:983
  133.2 4.9 %collective-permute-done.26 = bf16[2,2,128,256]{3,2,0,1:T(8,128)(2,1)S(1)} collective-permute-done((bf16[2,2,128,256]{3,2,0,1:T(8,128)(2,1)S(1)}, bf16[2,2,128,256]{3,2,0,1:T(8,128)(2,1)S(1)}, u32[]{:S(2)}, u32[]{:S(2)}) %collective-permute-start.26) | collective-permute-done | bytes 262176 | tf_op jit(solution)/shard_map/ppermute | solution.py:983
  141.0 7.9 %adjoint_tables.1 = (bf16[16,512,256]{2,1,0:T(8,128)(2,1)}, f32[4096,128]{1,0:T(8,128)}) custom-call(s32[2]{0:T(128)} %pad_add_fusion.ids, s32[4]{0:T(128)} %row_off.7, f32[16,32,256]{2,1,0:T(8,128)} %constant.20.clone.tr_ref, f32[16,32,256]{2,1,0:T(8,128)} %constant.21.clone.ti_ref, f32[32,128]{1,0:T(8,128)} %bitcast.109), custom_call_target="tpu_custom_call" | custom-call | flops 7000000000 | bytes 7340032 | tf_op jit(solution)/shard_map/adjoint_tables/pallas_call | solution.py:798
  150.5 6.9 %cols_backward.1.even_ref = bf16[16,128,512]{2,1,0:T(8,128)(2,1)} custom-call(s32[2]{0:T(128)} %pad_add_fusion.ids, s32[4]{0:T(128)} %row_off.7, s32[4]{0:T(128)} %col_off.5, bf16[2,8,128,256]{3,2,1,0:T(8,128)(2,1)} %bitcast.85, bf16[2,8,128,256]{3,2,1,0:T(8,128)(2,1)} %bitcast.87, bf16[4096,512]{1,0:T(8,128)(2,1)} %constant.22.clone.fr_ref, ...), custom_call_target="tpu_custom_call" | custom-call | flops 5000000000 | bytes 6291456 | tf_op jit(solution)/shard_map/cols_backward/pallas_call | solution.py:756
  159.3 16.4 %backward.1 = bf16[2,16,256,512]{3,2,1,0:T(8,128)(2,1)} custom-call(s32[2]{0:T(128)} %pad_add_fusion.ids, s32[4]{0:T(128)} %row_off.7, s32[4]{0:T(128)} %col_off.5, bf16[2,8,128,256]{3,2,1,0:T(8,128)(2,1)} %copy-done.2, bf16[2,8,128,256]{3,2,1,0:T(8,128)(2,1)} %copy-done.1, bf16[4096,512]{1,0:T(8,128)(2,1)} %constant.22.clone.fr_ref, ...), custom_call_target="tpu_custom_call" | custom-call | tf_op jit(solution)/shard_map/backward/pallas_call | solution.py:950
  (126 shorter events, 35.8 us)
Async XLA Ops:
  19.5 7.8 %collective-permute-start = (bf16[2,8,128,256]{3,2,1,0:T(8,128)(2,1)}, bf16[2,8,128,256]{3,2,1,0:T(8,128)(2,1)S(1)}, u32[]{:S(2)}, u32[]{:S(2)}) collective-permute-start(bf16[2,8,128,256]{3,2,1,0:T(8,128)(2,1)} %get-tuple-element.55), channel_id=1, source_target_pairs={{0,8},{8,0},{16,24},{24,16},{1,9},{9,1},{17,25},{25,17},{2,10},{10... | collective-permute-start | bytes 3145736 | tf_op jit(solution)/shard_map/ppermute | solution.py:983
  20.1 12.0 %collective-permute-start.2 = (bf16[2,8,128,256]{3,2,1,0:T(8,128)(2,1)}, bf16[2,8,128,256]{3,2,1,0:T(8,128)(2,1)S(1)}, u32[]{:S(2)}, u32[]{:S(2)}) collective-permute-start(bf16[2,8,128,256]{3,2,1,0:T(8,128)(2,1)} %get-tuple-element.58), channel_id=1, source_target_pairs={{0,8},{8,0},{16,24},{24,16},{1,9},{9,1},{17,25},{25,17},{2,10},{10... | collective-permute-start | bytes 3145736 | tf_op jit(solution)/shard_map/ppermute | solution.py:983
  29.1 15.2 %collective-permute-start.1 = (bf16[2,2,2,128,256]{4,3,0,1,2:T(8,128)(2,1)S(1)}, bf16[2,2,2,128,256]{4,3,0,1,2:T(8,128)(2,1)S(1)}, u32[]{:S(2)}, u32[]{:S(2)}) collective-permute-start(bf16[2,2,2,128,256]{4,3,0,1,2:T(8,128)(2,1)S(1)} %copy.21), channel_id=1, source_target_pairs={{0,16},{8,24},{16,0},{24,8},{1,17},{9,25},{17,1},{25,9},{2,18},{10... | collective-permute-start | bytes 1572872 | tf_op jit(solution)/shard_map/ppermute | solution.py:983
  32.6 13.7 %collective-permute-start.3 = (bf16[2,2,2,128,256]{4,3,1,2,0:T(8,128)(2,1)S(1)}, bf16[2,2,2,128,256]{4,3,1,2,0:T(8,128)(2,1)S(1)}, u32[]{:S(2)}, u32[]{:S(2)}) collective-permute-start(bf16[2,2,2,128,256]{4,3,1,2,0:T(8,128)(2,1)S(1)} %bitcast.90), channel_id=1, source_target_pairs={{0,1},{1,0},{2,3},{3,2},{4,5},{5,4},{6,7},{7,6},{8,9},{9,8},{10,11... | collective-permute-start | bytes 1572872 | tf_op jit(solution)/shard_map/ppermute | solution.py:983
  46.4 7.2 %collective-permute-start.4 = (bf16[2,2,128,256]{3,2,0,1:T(8,128)(2,1)S(1)}, bf16[2,2,128,256]{3,2,0,1:T(8,128)(2,1)S(1)}, u32[]{:S(2)}, u32[]{:S(2)}) collective-permute-start(bf16[2,2,128,256]{3,2,0,1:T(8,128)(2,1)S(1)} %slice_bitcast_fusion.2), channel_id=1, source_target_pairs={{0,1},{1,0},{2,3},{3,2},{4,5},{5,4},{6,7},{7,6},{8,9},{9,8},{10,11... | collective-permute-start | bytes 786440 | tf_op jit(solution)/shard_map/ppermute | solution.py:983
  48.1 7.2 %collective-permute-start.7 = (bf16[2,2,128,256]{3,2,0,1:T(8,128)(2,1)S(1)}, bf16[2,2,128,256]{3,2,0,1:T(8,128)(2,1)S(1)}, u32[]{:S(2)}, u32[]{:S(2)}) collective-permute-start(bf16[2,2,128,256]{3,2,0,1:T(8,128)(2,1)S(1)} %slice_bitcast_fusion), channel_id=1, source_target_pairs={{0,16},{8,24},{16,0},{24,8},{1,17},{9,25},{17,1},{25,9},{2,18},{10... | collective-permute-start | bytes 786440 | tf_op jit(solution)/shard_map/ppermute | solution.py:983
  55.4 6.6 %collective-permute-start.8 = (bf16[2,128,256]{2,1,0:T(8,128)(2,1)S(1)}, bf16[2,128,256]{2,1,0:T(8,128)(2,1)S(1)}, u32[]{:S(2)}, u32[]{:S(2)}) collective-permute-start(bf16[2,128,256]{2,1,0:T(8,128)(2,1)S(1)} %slice_bitcast_fusion.4), channel_id=1, source_target_pairs={{0,2},{1,3},{2,0},{3,1},{4,6},{5,7},{6,4},{7,5},{8,10},{9,11},{10,... | collective-permute-start | bytes 393224 | tf_op jit(solution)/shard_map/ppermute | solution.py:983
  59.3 6.4 %collective-permute-start.6 = (bf16[128,256]{1,0:T(8,128)(2,1)S(1)}, bf16[128,256]{1,0:T(8,128)(2,1)S(1)}, u32[]{:S(2)}, u32[]{:S(2)}) collective-permute-start(bf16[128,256]{1,0:T(8,128)(2,1)S(1)} %get-tuple-element.115), channel_id=1, source_target_pairs={{0,4},{1,5},{2,6},{3,7},{4,0},{5,1},{6,2},{7,3},{8,12},{9,13},{10,... | collective-permute-start | bytes 196616 | tf_op jit(solution)/shard_map/ppermute | solution.py:983
  62.6 5.2 %collective-permute-start.9 = (bf16[128,256]{1,0:T(8,128)(2,1)S(1)}, bf16[128,256]{1,0:T(8,128)(2,1)S(1)}, u32[]{:S(2)}, u32[]{:S(2)}) collective-permute-start(bf16[128,256]{1,0:T(8,128)(2,1)S(1)} %get-tuple-element.113), channel_id=1, source_target_pairs={{0,4},{1,5},{2,6},{3,7},{4,0},{5,1},{6,2},{7,3},{8,12},{9,13},{10,... | collective-permute-start | bytes 196616 | tf_op jit(solution)/shard_map/ppermute | solution.py:983
  71.8 7.4 %collective-permute-start.10 = (bf16[8,32,128]{2,1,0:T(8,128)(2,1)}, bf16[8,32,128]{2,1,0:T(8,128)(2,1)S(1)}, u32[]{:S(2)}, u32[]{:S(2)}) collective-permute-start(bf16[8,32,128]{2,1,0:T(8,128)(2,1)} %get-tuple-element.71), channel_id=1, source_target_pairs={{0,1},{1,0},{2,3},{3,2},{4,5},{5,4},{6,7},{7,6},{8,9},{9,8},{10,11... | collective-permute-start | bytes 196616 | tf_op jit(solution)/shard_map/ppermute | solution.py:983
  73.4 8.6 %collective-permute-start.11 = (bf16[8,32,128]{2,1,0:T(8,128)(2,1)}, bf16[8,32,128]{2,1,0:T(8,128)(2,1)S(1)}, u32[]{:S(2)}, u32[]{:S(2)}) collective-permute-start(bf16[8,32,128]{2,1,0:T(8,128)(2,1)} %get-tuple-element.72), channel_id=1, source_target_pairs={{0,2},{1,3},{2,0},{3,1},{4,6},{5,7},{6,4},{7,5},{8,10},{9,11},{10,... | collective-permute-start | bytes 196616 | tf_op jit(solution)/shard_map/ppermute | solution.py:983
  75.0 8.1 %collective-permute-start.12 = (bf16[8,32,128]{2,1,0:T(8,128)(2,1)}, bf16[8,32,128]{2,1,0:T(8,128)(2,1)S(1)}, u32[]{:S(2)}, u32[]{:S(2)}) collective-permute-start(bf16[8,32,128]{2,1,0:T(8,128)(2,1)} %get-tuple-element.73), channel_id=1, source_target_pairs={{0,3},{1,2},{2,1},{3,0},{4,7},{5,6},{6,5},{7,4},{8,11},{9,10},{10,... | collective-permute-start | bytes 196616 | tf_op jit(solution)/shard_map/ppermute | solution.py:983
  75.4 16.8 %collective-permute-start.16 = (bf16[8,32,128]{2,1,0:T(8,128)(2,1)}, bf16[8,32,128]{2,1,0:T(8,128)(2,1)S(1)}, u32[]{:S(2)}, u32[]{:S(2)}) collective-permute-start(bf16[8,32,128]{2,1,0:T(8,128)(2,1)} %get-tuple-element.82), channel_id=1, source_target_pairs={{0,4},{1,5},{2,6},{3,7},{4,0},{5,1},{6,2},{7,3},{8,12},{9,13},{10,... | collective-permute-start | bytes 196616 | tf_op jit(solution)/shard_map/ppermute | solution.py:983
  77.0 15.2 %collective-permute-start.17 = (bf16[8,32,128]{2,1,0:T(8,128)(2,1)}, bf16[8,32,128]{2,1,0:T(8,128)(2,1)S(1)}, u32[]{:S(2)}, u32[]{:S(2)}) collective-permute-start(bf16[8,32,128]{2,1,0:T(8,128)(2,1)} %get-tuple-element.83), channel_id=1, source_target_pairs={{0,5},{1,4},{2,7},{3,6},{4,1},{5,0},{6,3},{7,2},{8,13},{9,12},{10,... | collective-permute-start | bytes 196616 | tf_op jit(solution)/shard_map/ppermute | solution.py:983
  79.3 14.9 %collective-permute-start.18 = (bf16[8,32,128]{2,1,0:T(8,128)(2,1)}, bf16[8,32,128]{2,1,0:T(8,128)(2,1)S(1)}, u32[]{:S(2)}, u32[]{:S(2)}) collective-permute-start(bf16[8,32,128]{2,1,0:T(8,128)(2,1)} %get-tuple-element.84), channel_id=1, source_target_pairs={{0,6},{1,7},{2,4},{3,5},{4,2},{5,3},{6,0},{7,1},{8,14},{9,15},{10,... | collective-permute-start | bytes 196616 | tf_op jit(solution)/shard_map/ppermute | solution.py:983
  82.0 12.1 %collective-permute-start.19 = (bf16[8,32,128]{2,1,0:T(8,128)(2,1)}, bf16[8,32,128]{2,1,0:T(8,128)(2,1)S(1)}, u32[]{:S(2)}, u32[]{:S(2)}) collective-permute-start(bf16[8,32,128]{2,1,0:T(8,128)(2,1)} %get-tuple-element.85), channel_id=1, source_target_pairs={{0,7},{1,6},{2,5},{3,4},{4,3},{5,2},{6,1},{7,0},{8,15},{9,14},{10,... | collective-permute-start | bytes 196616 | tf_op jit(solution)/shard_map/ppermute | solution.py:983
  90.6 15.8 %collective-permute-start.13 = (bf16[8,32,128]{2,1,0:T(8,128)(2,1)}, bf16[8,32,128]{2,1,0:T(8,128)(2,1)S(1)}, u32[]{:S(2)}, u32[]{:S(2)}) collective-permute-start(bf16[8,32,128]{2,1,0:T(8,128)(2,1)} %get-tuple-element.79), channel_id=1, source_target_pairs={{0,1},{1,0},{2,3},{3,2},{4,5},{5,4},{6,7},{7,6},{8,9},{9,8},{10,11... | collective-permute-start | bytes 196616 | tf_op jit(solution)/shard_map/ppermute | solution.py:983
  92.2 17.1 %collective-permute-start.14 = (bf16[8,32,128]{2,1,0:T(8,128)(2,1)}, bf16[8,32,128]{2,1,0:T(8,128)(2,1)S(1)}, u32[]{:S(2)}, u32[]{:S(2)}) collective-permute-start(bf16[8,32,128]{2,1,0:T(8,128)(2,1)} %get-tuple-element.80), channel_id=1, source_target_pairs={{0,2},{1,3},{2,0},{3,1},{4,6},{5,7},{6,4},{7,5},{8,10},{9,11},{10,... | collective-permute-start | bytes 196616 | tf_op jit(solution)/shard_map/ppermute | solution.py:983
  92.2 18.1 %collective-permute-start.15 = (bf16[8,32,128]{2,1,0:T(8,128)(2,1)}, bf16[8,32,128]{2,1,0:T(8,128)(2,1)S(1)}, u32[]{:S(2)}, u32[]{:S(2)}) collective-permute-start(bf16[8,32,128]{2,1,0:T(8,128)(2,1)} %get-tuple-element.81), channel_id=1, source_target_pairs={{0,3},{1,2},{2,1},{3,0},{4,7},{5,6},{6,5},{7,4},{8,11},{9,10},{10,... | collective-permute-start | bytes 196616 | tf_op jit(solution)/shard_map/ppermute | solution.py:983
  102.6 7.7 %collective-permute-start.20 = (bf16[8,32,128]{2,1,0:T(8,128)(2,1)}, bf16[8,32,128]{2,1,0:T(8,128)(2,1)S(1)}, u32[]{:S(2)}, u32[]{:S(2)}) collective-permute-start(bf16[8,32,128]{2,1,0:T(8,128)(2,1)} %get-tuple-element.86), channel_id=1, source_target_pairs={{0,4},{1,5},{2,6},{3,7},{4,0},{5,1},{6,2},{7,3},{8,12},{9,13},{10,... | collective-permute-start | bytes 196616 | tf_op jit(solution)/shard_map/ppermute | solution.py:983
  104.1 6.3 %collective-permute-start.21 = (bf16[8,32,128]{2,1,0:T(8,128)(2,1)}, bf16[8,32,128]{2,1,0:T(8,128)(2,1)S(1)}, u32[]{:S(2)}, u32[]{:S(2)}) collective-permute-start(bf16[8,32,128]{2,1,0:T(8,128)(2,1)} %get-tuple-element.87), channel_id=1, source_target_pairs={{0,5},{1,4},{2,7},{3,6},{4,1},{5,0},{6,3},{7,2},{8,13},{9,12},{10,... | collective-permute-start | bytes 196616 | tf_op jit(solution)/shard_map/ppermute | solution.py:983
  106.4 6.5 %collective-permute-start.22 = (bf16[8,32,128]{2,1,0:T(8,128)(2,1)}, bf16[8,32,128]{2,1,0:T(8,128)(2,1)S(1)}, u32[]{:S(2)}, u32[]{:S(2)}) collective-permute-start(bf16[8,32,128]{2,1,0:T(8,128)(2,1)} %get-tuple-element.88), channel_id=1, source_target_pairs={{0,6},{1,7},{2,4},{3,5},{4,2},{5,3},{6,0},{7,1},{8,14},{9,15},{10,... | collective-permute-start | bytes 196616 | tf_op jit(solution)/shard_map/ppermute | solution.py:983
  109.2 7.2 %collective-permute-start.23 = (bf16[8,32,128]{2,1,0:T(8,128)(2,1)}, bf16[8,32,128]{2,1,0:T(8,128)(2,1)S(1)}, u32[]{:S(2)}, u32[]{:S(2)}) collective-permute-start(bf16[8,32,128]{2,1,0:T(8,128)(2,1)} %get-tuple-element.89), channel_id=1, source_target_pairs={{0,7},{1,6},{2,5},{3,4},{4,3},{5,2},{6,1},{7,0},{8,15},{9,14},{10,... | collective-permute-start | bytes 196616 | tf_op jit(solution)/shard_map/ppermute | solution.py:983
  119.8 5.4 %collective-permute-start.24 = (bf16[128,256]{1,0:T(8,128)(2,1)}, bf16[128,256]{1,0:T(8,128)(2,1)S(1)}, u32[]{:S(2)}, u32[]{:S(2)}) collective-permute-start(bf16[128,256]{1,0:T(8,128)(2,1)} %get-tuple-element.90), channel_id=1, source_target_pairs={{0,4},{1,5},{2,6},{3,7},{4,0},{5,1},{6,2},{7,3},{8,12},{9,13},{10,... | collective-permute-start | bytes 196616 | tf_op jit(solution)/shard_map/ppermute | solution.py:983
  119.8 6.8 %collective-permute-start.27 = (bf16[128,256]{1,0:T(8,128)(2,1)}, bf16[128,256]{1,0:T(8,128)(2,1)S(1)}, u32[]{:S(2)}, u32[]{:S(2)}) collective-permute-start(bf16[128,256]{1,0:T(8,128)(2,1)} %get-tuple-element.91), channel_id=1, source_target_pairs={{0,4},{1,5},{2,6},{3,7},{4,0},{5,1},{6,2},{7,3},{8,12},{9,13},{10,... | collective-permute-start | bytes 196616 | tf_op jit(solution)/shard_map/ppermute | solution.py:983
  127.4 5.2 %collective-permute-start.28 = (bf16[2,128,256]{2,1,0:T(8,128)(2,1)S(1)}, bf16[2,128,256]{2,1,0:T(8,128)(2,1)S(1)}, u32[]{:S(2)}, u32[]{:S(2)}) collective-permute-start(bf16[2,128,256]{2,1,0:T(8,128)(2,1)S(1)} %get-tuple-element.110), channel_id=1, source_target_pairs={{0,2},{1,3},{2,0},{3,1},{4,6},{5,7},{6,4},{7,5},{8,10},{9,11},{10,... | collective-permute-start | bytes 393224 | tf_op jit(solution)/shard_map/ppermute | solution.py:983
  131.1 7.0 %collective-permute-start.26 = (bf16[2,2,128,256]{3,2,0,1:T(8,128)(2,1)S(1)}, bf16[2,2,128,256]{3,2,0,1:T(8,128)(2,1)S(1)}, u32[]{:S(2)}, u32[]{:S(2)}) collective-permute-start(bf16[2,2,128,256]{3,2,0,1:T(8,128)(2,1)S(1)} %get-tuple-element.108), channel_id=1, source_target_pairs={{0,1},{1,0},{2,3},{3,2},{4,5},{5,4},{6,7},{7,6},{8,9},{9,8},{10,11... | collective-permute-start | bytes 786440 | tf_op jit(solution)/shard_map/ppermute | solution.py:983
  132.7 6.4 %collective-permute-start.29 = (bf16[2,2,128,256]{3,2,0,1:T(8,128)(2,1)S(1)}, bf16[2,2,128,256]{3,2,0,1:T(8,128)(2,1)S(1)}, u32[]{:S(2)}, u32[]{:S(2)}) collective-permute-start(bf16[2,2,128,256]{3,2,0,1:T(8,128)(2,1)S(1)} %get-tuple-element.106), channel_id=1, source_target_pairs={{0,16},{8,24},{16,0},{24,8},{1,17},{9,25},{17,1},{25,9},{2,18},{10... | collective-permute-start | bytes 786440 | tf_op jit(solution)/shard_map/ppermute | solution.py:983
  139.1 9.8 %collective-permute-start.30 = (bf16[2,2,2,128,256]{4,3,0,1,2:T(8,128)(2,1)S(1)}, bf16[2,2,2,128,256]{4,3,0,1,2:T(8,128)(2,1)S(1)}, u32[]{:S(2)}, u32[]{:S(2)}) collective-permute-start(bf16[2,2,2,128,256]{4,3,0,1,2:T(8,128)(2,1)S(1)} %pad_maximum_fusion.2), channel_id=1, source_target_pairs={{0,16},{8,24},{16,0},{24,8},{1,17},{9,25},{17,1},{25,9},{2,18},{10... | collective-permute-start | bytes 1572872 | tf_op jit(solution)/shard_map/ppermute | solution.py:983
  139.8 9.2 %collective-permute-start.31 = (bf16[2,2,2,128,256]{4,3,1,2,0:T(8,128)(2,1)S(1)}, bf16[2,2,2,128,256]{4,3,1,2,0:T(8,128)(2,1)S(1)}, u32[]{:S(2)}, u32[]{:S(2)}) collective-permute-start(bf16[2,2,2,128,256]{4,3,1,2,0:T(8,128)(2,1)S(1)} %pad_maximum_fusion.3), channel_id=1, source_target_pairs={{0,1},{1,0},{2,3},{3,2},{4,5},{5,4},{6,7},{7,6},{8,9},{9,8},{10,11... | collective-permute-start | bytes 1572872 | tf_op jit(solution)/shard_map/ppermute | solution.py:983
  149.3 8.1 %collective-permute-start.33 = (bf16[2,8,128,256]{3,2,1,0:T(8,128)(2,1)S(1)}, bf16[2,8,128,256]{3,2,1,0:T(8,128)(2,1)S(1)}, u32[]{:S(2)}, u32[]{:S(2)}) collective-permute-start(bf16[2,8,128,256]{3,2,1,0:T(8,128)(2,1)S(1)} %bitcast.86), channel_id=1, source_target_pairs={{0,8},{8,0},{16,24},{24,16},{1,9},{9,1},{17,25},{25,17},{2,10},{10... | collective-permute-start | bytes 3145736 | tf_op jit(solution)/shard_map/ppermute | solution.py:983
  149.4 8.0 %collective-permute-start.32 = (bf16[2,8,128,256]{3,2,1,0:T(8,128)(2,1)S(1)}, bf16[2,8,128,256]{3,2,1,0:T(8,128)(2,1)S(1)}, u32[]{:S(2)}, u32[]{:S(2)}) collective-permute-start(bf16[2,8,128,256]{3,2,1,0:T(8,128)(2,1)S(1)} %bitcast.84), channel_id=1, source_target_pairs={{0,8},{8,0},{16,24},{24,16},{1,9},{9,1},{17,25},{25,17},{2,10},{10... | collective-permute-start | bytes 3145736 | tf_op jit(solution)/shard_map/ppermute | solution.py:983
  (26 other events, 101.9 us)

commit v5 on v4

--- a/solution.py
+++ b/solution.py
@@ -114,7 +114,7 @@
         spread[pl.ds(pl.multiple_of(i * LANES, LANES), LANES), :] = row.T
         return carry
 
-    lax.fori_loop(0, window_ref.shape[0], one, 0, unroll=8)
+    lax.fori_loop(0, window_ref.shape[0], one, 0, unroll=16)
 
 
 def place_of(jr, count):
@@ -138,7 +138,7 @@
             write(jnp.bitwise_and(off + q1, TS - 1), place_of(jr, count), block)
         return carry
 
-    lax.fori_loop(0, TS, per_q1, 0)
+    lax.fori_loop(0, TS, per_q1, 0, unroll=4)
 
 
 def exchange(first, second):
@@ -184,7 +184,7 @@
                             store(place, z * TS * tile_rows + quad * tile_rows, chunk, value)
             return carry
 
-        lax.fori_loop(0, subs // 2, per_pair, 0)
+        lax.fori_loop(0, subs // 2, per_pair, 0, unroll=True)
     else:
         assert tile_rows == 1
 
@@ -294,7 +294,7 @@
                     kept_ref[jr // 2, 1, q1] = out_i
             return carry
 
-        lax.fori_loop(0, TS, per_k1, 0, unroll=4)
+        lax.fori_loop(0, TS, per_k1, 0, unroll=16)
 
     @pl.when(step >= blocks)
     def _():
@@ -718,7 +718,7 @@
                             write(k1_of(2 * pair + n), z * q2 + s * tile_rows, chunk, value)
             return carry
 
-        lax.fori_loop(0, TS // 2, per_pair, 0)
+        lax.fori_loop(0, TS // 2, per_pair, 0, unroll=4)
     else:
         assert tile_rows == 1
         for q1 in range(TS):
@@ -785,7 +785,7 @@
         out_ref[k1] = mat[k1].T.astype(BF16)
         return carry
 
-    lax.fori_loop(0, TS, per_k1, 0)
+    lax.fori_loop(0, TS, per_k1, 0, unroll=4)
     spread_window(rw_ref, spread_ref)
 
 
@@ -896,7 +896,7 @@
             middle[k1] = jnp.dot(mat[k1], rows, preferred_element_type=F32)
             return carry
 
-        lax.fori_loop(0, TS, per_k1, 0, unroll=4)
+        lax.fori_loop(0, TS, per_k1, 0, unroll=16)
 
         def butterfly(chunk, carry):
             n2 = pl.multiple_of(chunk * 16, 16)

time: 177 us -> 174 us (0.983)
  Pallas kernels: 83.3 us -> 79.1 us
  transfers between devices with their start and end apart: 34 -> 34, of which waited for: 14 -> 16; matrix products, arithmetic and copies ran while one was open for 4% -> 4% of each run, Pallas kernels for 24% -> 23%
where the time goes in v5:
time: 174 us; the launch traced here: 173 us
  Pallas kernels  79.1 us (45%)
  starting transfers between devices  45.9 us (26%)
  waiting for transfers between devices  33.5 us (19%)
  local copies, waits for them, and re-layouts  8.26 us (5%)
  other arithmetic  5.72 us (3%)
    ppermute x34, starting transfers between devices, swap(): lax.ppermute(value, axis, [(i, i ^ bit) for i in range(lax.axis_size(axis...  45.9 us
    ppermute x34, waiting for transfers between devices, swap(): lax.ppermute(value, axis, [(i, i ^ bit) for i in range(lax.axis_size(axis...  33.5 us
    pallas_call x1, Pallas kernels, forward(): pl.pallas_call(forward_kernel, grid_spec=pltpu.PrefetchScalarGridSpec(num...  17.5 us
    pallas_call x1, Pallas kernels, backward(): pl.pallas_call(backward_kernel, grid_spec=pltpu.PrefetchScalarGridSpec(nu...  15.4 us
    pallas_call x2, Pallas kernels, visit(): pl.pallas_call(visit_kernel, grid_spec=pltpu.PrefetchScalarGridSpec(num_s...  14.1 us
    pallas_call x1, Pallas kernels, cols_backward(): pl.pallas_call(partial(cols_backward_kernel, length=length), grid_spec=pl...  6.73 us
    pallas_call x1, Pallas kernels, adjoint_tables(): pl.pallas_call(adjoint_tables_kernel, in_specs=[smem] * 2 + [vmem] * 3, o...  6.69 us
    unnamed x51, local copies, waits for them, and re-layouts  6.6 us
  transfers between devices with their start and end apart: 34, of which 16 were waited for; matrix products, arithmetic and copies ran while one was open for 4% of the time, Pallas kernels for 23%

profile of v5, /device:TPU:0, one launch (start us, length us, event | category | flops | bytes accessed | tf_op | source)
XLA Modules:
  0.0 172.9 jit_solution(1763273152691555490)
XLA Ops:
  0.6 17.5 %forward.1 = (bf16[2,2,16,32,512]{4,3,2,1,0:T(8,128)(2,1)}, bf16[2,8,128,256]{3,2,1,0:T(8,128)(2,1)}, bf16[2,8,128,256]{3,2,1,0:T(8,128)(2,1)}) custom-call(s32[2]{0:T(128)} %pad_add_fusion.ids, s32[4]{0:T(128)} %row_off.7, s32[4]{0:T(128)} %col_off.5, bf16[2,4096,512]{2,1,0:T(8,128)(2,1)} %x_ref.1, f32[32,128]{1,0:T(8,128)} %bitcast.108, ...), custom_call_target="tpu_custom_call" | custom-call | flops 12000000000 | bytes 16777216 | tf_op jit(solution)/shard_map/forward/pallas_call | solution.py:328
  19.6 5.9 %cols_forward.1 = (bf16[2,8,128,256]{3,2,1,0:T(8,128)(2,1)}, bf16[2,8,128,256]{3,2,1,0:T(8,128)(2,1)}) custom-call(s32[2]{0:T(128)} %pad_add_fusion.ids, bf16[2,2,512,512]{3,2,1,0:T(8,128)(2,1)} %bitcast.110, bf16[4096,512]{1,0:T(8,128)(2,1)} %constant.22.clone.fr_ref, bf16[4096,512]{1,0:T(8,128)(2,1)} %constant.23.clone.fi_ref), custom_call_target="tpu_custom_call" | custom-call | flops 4000000000 | bytes 6291456 | tf_op jit(solution)/shard_map/cols_forward/pallas_call | solution.py:380
  25.5 1.6 add.24
  27.3 3.0 %collective-permute-start.1 = (bf16[2,2,2,128,256]{4,3,0,1,2:T(8,128)(2,1)S(1)}, bf16[2,2,2,128,256]{4,3,0,1,2:T(8,128)(2,1)S(1)}, u32[]{:S(2)}, u32[]{:S(2)}) collective-permute-start(bf16[2,2,2,128,256]{4,3,0,1,2:T(8,128)(2,1)S(1)} %copy.21), channel_id=1, source_target_pairs={{0,16},{8,24},{16,0},{24,8},{1,17},{9,25},{17,1},{25,9},{2,18},{10... | collective-permute-start | bytes 1572872 | tf_op jit(solution)/shard_map/ppermute | solution.py:983
  33.2 6.5 %kernels.1 = (bf16[64,2,128,128]{3,2,1,0:T(8,128)(2,1)}, bf16[64,128,256]{2,1,0:T(8,128)(2,1)}) custom-call(s32[3,512,128]{2,1,0:T(8,128)} %bitcast.107), custom_call_target="tpu_custom_call" | custom-call | flops 6000000000 | bytes 9437184 | tf_op jit(solution)/shard_map/kernels/pallas_call | solution.py:570
  39.8 2.7 %collective-permute-done.1 = bf16[2,2,2,128,256]{4,3,0,1,2:T(8,128)(2,1)S(1)} collective-permute-done((bf16[2,2,2,128,256]{4,3,0,1,2:T(8,128)(2,1)S(1)}, bf16[2,2,2,128,256]{4,3,0,1,2:T(8,128)(2,1)S(1)}, u32[]{:S(2)}, u32[]{:S(2)}) %collective-permute-start.1) | collective-permute-done | bytes 524320 | tf_op jit(solution)/shard_map/ppermute | solution.py:983
  42.5 2.0 %collective-permute-done.3 = bf16[2,2,2,128,256]{4,3,1,2,0:T(8,128)(2,1)S(1)} collective-permute-done((bf16[2,2,2,128,256]{4,3,1,2,0:T(8,128)(2,1)S(1)}, bf16[2,2,2,128,256]{4,3,1,2,0:T(8,128)(2,1)S(1)}, u32[]{:S(2)}, u32[]{:S(2)}) %collective-permute-start.3) | collective-permute-done | bytes 524320 | tf_op jit(solution)/shard_map/ppermute | solution.py:983
  46.9 4.9 %collective-permute-done.4 = bf16[2,2,128,256]{3,2,0,1:T(8,128)(2,1)S(1)} collective-permute-done((bf16[2,2,128,256]{3,2,0,1:T(8,128)(2,1)S(1)}, bf16[2,2,128,256]{3,2,0,1:T(8,128)(2,1)S(1)}, u32[]{:S(2)}, u32[]{:S(2)}) %collective-permute-start.4) | collective-permute-done | bytes 262176 | tf_op jit(solution)/shard_map/ppermute | solution.py:983
  51.9 1.6 collective-permute-start.5
  54.9 1.9 %collective-permute-done.5 = bf16[2,128,256]{2,1,0:T(8,128)(2,1)S(1)} collective-permute-done((bf16[2,128,256]{2,1,0:T(8,128)(2,1)S(1)}, bf16[2,128,256]{2,1,0:T(8,128)(2,1)S(1)}, u32[]{:S(2)}, u32[]{:S(2)}) %collective-permute-start.5) | collective-permute-done | bytes 131104 | tf_op jit(solution)/shard_map/ppermute | solution.py:983
  57.5 2.6 %collective-permute-start.6 = (bf16[128,256]{1,0:T(8,128)(2,1)S(1)}, bf16[128,256]{1,0:T(8,128)(2,1)S(1)}, u32[]{:S(2)}, u32[]{:S(2)}) collective-permute-start(bf16[128,256]{1,0:T(8,128)(2,1)S(1)} %get-tuple-element.115), channel_id=1, source_target_pairs={{0,4},{1,5},{2,6},{3,7},{4,0},{5,1},{6,2},{7,3},{8,12},{9,13},{10,... | collective-permute-start | bytes 196616 | tf_op jit(solution)/shard_map/ppermute | solution.py:983
  62.2 1.7 collective-permute-done.6.refs_1_
  64.0 2.0 %collective-permute-done.9.refs_3_ = bf16[128,256]{1,0:T(8,128)(2,1)S(1)} collective-permute-done((bf16[128,256]{1,0:T(8,128)(2,1)S(1)}, bf16[128,256]{1,0:T(8,128)(2,1)S(1)}, u32[]{:S(2)}, u32[]{:S(2)}) %collective-permute-start.9) | collective-permute-done | bytes 65568 | tf_op jit(solution)/shard_map/ppermute | solution.py:983
  66.6 3.5 %route.1 = (bf16[8,32,128]{2,1,0:T(8,128)(2,1)}, bf16[8,32,128]{2,1,0:T(8,128)(2,1)}, bf16[8,32,128]{2,1,0:T(8,128)(2,1)}, bf16[8,32,128]{2,1,0:T(8,128)(2,1)}, ...) custom-call(s32[2]{0:T(128)} %pad_add_fusion.ids, ...), custom_call_target="tpu_custom_call" | custom-call | tf_op jit(solution)/shard_map/route/pallas_call | solution.py:448
  75.2 2.3 %collective-permute-start.17 = (bf16[8,32,128]{2,1,0:T(8,128)(2,1)}, bf16[8,32,128]{2,1,0:T(8,128)(2,1)S(1)}, u32[]{:S(2)}, u32[]{:S(2)}) collective-permute-start(bf16[8,32,128]{2,1,0:T(8,128)(2,1)} %get-tuple-element.83), channel_id=1, source_target_pairs={{0,5},{1,4},{2,7},{3,6},{4,1},{5,0},{6,3},{7,2},{8,13},{9,12},{10,... | collective-permute-start | bytes 196616 | tf_op jit(solution)/shard_map/ppermute | solution.py:983
  77.5 2.8 %collective-permute-start.18 = (bf16[8,32,128]{2,1,0:T(8,128)(2,1)}, bf16[8,32,128]{2,1,0:T(8,128)(2,1)S(1)}, u32[]{:S(2)}, u32[]{:S(2)}) collective-permute-start(bf16[8,32,128]{2,1,0:T(8,128)(2,1)} %get-tuple-element.84), channel_id=1, source_target_pairs={{0,6},{1,7},{2,4},{3,5},{4,2},{5,3},{6,0},{7,1},{8,14},{9,15},{10,... | collective-permute-start | bytes 196616 | tf_op jit(solution)/shard_map/ppermute | solution.py:983
  81.9 6.9 %visit.2 = (bf16[8,32,128]{2,1,0:T(8,128)(2,1)}, bf16[8,32,128]{2,1,0:T(8,128)(2,1)}, bf16[8,32,128]{2,1,0:T(8,128)(2,1)}, bf16[8,32,128]{2,1,0:T(8,128)(2,1)}) custom-call(s32[2]{0:T(128)} %pad_add_fusion.ids, bf16[8,32,128]{2,1,0:T(8,128)(2,1)} %get-tuple-element.70.refs_0_, bf16[8,32,128]{2,1,0:T(8,128)(2,1)} %copy-done.21, ...), custom_call_target="tpu_custom_call" | custom-call | flops 7200000000 | bytes 5242880 | tf_op jit(solution)/shard_map/visit/pallas_call | solution.py:646
  90.4 2.0 %collective-permute-start.15 = (bf16[8,32,128]{2,1,0:T(8,128)(2,1)}, bf16[8,32,128]{2,1,0:T(8,128)(2,1)S(1)}, u32[]{:S(2)}, u32[]{:S(2)}) collective-permute-start(bf16[8,32,128]{2,1,0:T(8,128)(2,1)} %get-tuple-element.81), channel_id=1, source_target_pairs={{0,3},{1,2},{2,1},{3,0},{4,7},{5,6},{6,5},{7,4},{8,11},{9,10},{10,... | collective-permute-start | bytes 196616 | tf_op jit(solution)/shard_map/ppermute | solution.py:983
  93.6 7.1 %visit.3 = (bf16[8,32,128]{2,1,0:T(8,128)(2,1)}, bf16[8,32,128]{2,1,0:T(8,128)(2,1)}, bf16[8,32,128]{2,1,0:T(8,128)(2,1)}, bf16[8,32,128]{2,1,0:T(8,128)(2,1)}) custom-call(s32[2]{0:T(128)} %pad_add_fusion.ids, bf16[8,32,128]{2,1,0:T(8,128)(2,1)} %copy-done.17, bf16[8,32,128]{2,1,0:T(8,128)(2,1)} %copy-done.18, bf16[8,32,128]{2,1,0:T(8,128)(2,1)} %copy-done.19, ...), custom_call_target="tpu_custom_call" | custom-call | flops 7200000000 | bytes 5242880 | tf_op jit(solution)/shard_map/visit/pallas_call | solution.py:646
  102.3 2.3 %collective-permute-start.21 = (bf16[8,32,128]{2,1,0:T(8,128)(2,1)}, bf16[8,32,128]{2,1,0:T(8,128)(2,1)S(1)}, u32[]{:S(2)}, u32[]{:S(2)}) collective-permute-start(bf16[8,32,128]{2,1,0:T(8,128)(2,1)} %get-tuple-element.87), channel_id=1, source_target_pairs={{0,5},{1,4},{2,7},{3,6},{4,1},{5,0},{6,3},{7,2},{8,13},{9,12},{10,... | collective-permute-start | bytes 196616 | tf_op jit(solution)/shard_map/ppermute | solution.py:983
  104.6 2.8 %collective-permute-start.22 = (bf16[8,32,128]{2,1,0:T(8,128)(2,1)}, bf16[8,32,128]{2,1,0:T(8,128)(2,1)S(1)}, u32[]{:S(2)}, u32[]{:S(2)}) collective-permute-start(bf16[8,32,128]{2,1,0:T(8,128)(2,1)} %get-tuple-element.88), channel_id=1, source_target_pairs={{0,6},{1,7},{2,4},{3,5},{4,2},{5,3},{6,0},{7,1},{8,14},{9,15},{10,... | collective-permute-start | bytes 196616 | tf_op jit(solution)/shard_map/ppermute | solution.py:983
  108.6 2.6 %collective-permute-done.22.refs_6_ = bf16[8,32,128]{2,1,0:T(8,128)(2,1)S(1)} collective-permute-done((bf16[8,32,128]{2,1,0:T(8,128)(2,1)}, bf16[8,32,128]{2,1,0:T(8,128)(2,1)S(1)}, u32[]{:S(2)}, u32[]{:S(2)}) %collective-permute-start.22) | collective-permute-done | bytes 65568 | tf_op jit(solution)/shard_map/ppermute | solution.py:983
  111.2 3.4 %collective-permute-done.23.refs_7_ = bf16[8,32,128]{2,1,0:T(8,128)(2,1)S(1)} collective-permute-done((bf16[8,32,128]{2,1,0:T(8,128)(2,1)}, bf16[8,32,128]{2,1,0:T(8,128)(2,1)S(1)}, u32[]{:S(2)}, u32[]{:S(2)}) %collective-permute-start.23) | collective-permute-done | bytes 65568 | tf_op jit(solution)/shard_map/ppermute | solution.py:983
  115.2 2.8 %unroute.1 = (bf16[128,256]{1,0:T(8,128)(2,1)}, bf16[128,256]{1,0:T(8,128)(2,1)}) custom-call(s32[128]{0:T(128)} %get-tuple-element.69.where_ref, bf16[8,32,128]{2,1,0:T(8,128)(2,1)} %get-tuple-element.78.refs_0_, bf16[8,32,128]{2,1,0:T(8,128)(2,1)} %copy-done.7, bf16[8,32,128]{2,1,0:T(8,128)(2,1)} %copy-done.8, bf16[8,32,128]{2,1,0:T(8,128)(2,1)} %copy-done.9, ...), custom_call_target="tpu_custom_call" | custom-call | tf_op jit(solution)/shard_map/unroute/pallas_call | solution.py:497
  118.0 2.9 %collective-permute-start.27 = (bf16[128,256]{1,0:T(8,128)(2,1)}, bf16[128,256]{1,0:T(8,128)(2,1)S(1)}, u32[]{:S(2)}, u32[]{:S(2)}) collective-permute-start(bf16[128,256]{1,0:T(8,128)(2,1)} %get-tuple-element.91), channel_id=1, source_target_pairs={{0,4},{1,5},{2,6},{3,7},{4,0},{5,1},{6,2},{7,3},{8,12},{9,13},{10,... | collective-permute-start | bytes 196616 | tf_op jit(solution)/shard_map/ppermute | solution.py:983
  120.9 2.4 %collective-permute-done.24 = bf16[128,256]{1,0:T(8,128)(2,1)S(1)} collective-permute-done((bf16[128,256]{1,0:T(8,128)(2,1)}, bf16[128,256]{1,0:T(8,128)(2,1)S(1)}, u32[]{:S(2)}, u32[]{:S(2)}) %collective-permute-start.24) | collective-permute-done | bytes 65568 | tf_op jit(solution)/shard_map/ppermute | solution.py:983
  125.7 1.6 collective-permute-start.28
  127.3 2.0 %collective-permute-done.25 = bf16[2,128,256]{2,1,0:T(8,128)(2,1)S(1)} collective-permute-done((bf16[2,128,256]{2,1,0:T(8,128)(2,1)S(1)}, bf16[2,128,256]{2,1,0:T(8,128)(2,1)S(1)}, u32[]{:S(2)}, u32[]{:S(2)}) %collective-permute-start.25) | collective-permute-done | bytes 131104 | tf_op jit(solution)/shard_map/ppermute | solution.py:983
  131.4 4.9 %collective-permute-done.26 = bf16[2,2,128,256]{3,2,0,1:T(8,128)(2,1)S(1)} collective-permute-done((bf16[2,2,128,256]{3,2,0,1:T(8,128)(2,1)S(1)}, bf16[2,2,128,256]{3,2,0,1:T(8,128)(2,1)S(1)}, u32[]{:S(2)}, u32[]{:S(2)}) %collective-permute-start.26) | collective-permute-done | bytes 262176 | tf_op jit(solution)/shard_map/ppermute | solution.py:983
  139.2 6.7 %adjoint_tables.1 = (bf16[16,512,256]{2,1,0:T(8,128)(2,1)}, f32[4096,128]{1,0:T(8,128)}) custom-call(s32[2]{0:T(128)} %pad_add_fusion.ids, s32[4]{0:T(128)} %row_off.7, f32[16,32,256]{2,1,0:T(8,128)} %constant.20.clone.tr_ref, f32[16,32,256]{2,1,0:T(8,128)} %constant.21.clone.ti_ref, f32[32,128]{1,0:T(8,128)} %bitcast.109), custom_call_target="tpu_custom_call" | custom-call | flops 7000000000 | bytes 7340032 | tf_op jit(solution)/shard_map/adjoint_tables/pallas_call | solution.py:798
  148.7 6.7 %cols_backward.1.even_ref = bf16[16,128,512]{2,1,0:T(8,128)(2,1)} custom-call(s32[2]{0:T(128)} %pad_add_fusion.ids, s32[4]{0:T(128)} %row_off.7, s32[4]{0:T(128)} %col_off.5, bf16[2,8,128,256]{3,2,1,0:T(8,128)(2,1)} %bitcast.85, bf16[2,8,128,256]{3,2,1,0:T(8,128)(2,1)} %bitcast.87, bf16[4096,512]{1,0:T(8,128)(2,1)} %constant.22.clone.fr_ref, ...), custom_call_target="tpu_custom_call" | custom-call | flops 5000000000 | bytes 6291456 | tf_op jit(solution)/shard_map/cols_backward/pallas_call | solution.py:756
  157.4 15.4 %backward.1 = bf16[2,16,256,512]{3,2,1,0:T(8,128)(2,1)} custom-call(s32[2]{0:T(128)} %pad_add_fusion.ids, s32[4]{0:T(128)} %row_off.7, s32[4]{0:T(128)} %col_off.5, bf16[2,8,128,256]{3,2,1,0:T(8,128)(2,1)} %copy-done.2, bf16[2,8,128,256]{3,2,1,0:T(8,128)(2,1)} %copy-done.1, bf16[4096,512]{1,0:T(8,128)(2,1)} %constant.22.clone.fr_ref, ...), custom_call_target="tpu_custom_call" | custom-call | tf_op jit(solution)/shard_map/backward/pallas_call | solution.py:950
  (126 shorter events, 37.0 us)
Async XLA Ops:
  18.1 7.4 %collective-permute-start = (bf16[2,8,128,256]{3,2,1,0:T(8,128)(2,1)}, bf16[2,8,128,256]{3,2,1,0:T(8,128)(2,1)S(1)}, u32[]{:S(2)}, u32[]{:S(2)}) collective-permute-start(bf16[2,8,128,256]{3,2,1,0:T(8,128)(2,1)} %get-tuple-element.55), channel_id=1, source_target_pairs={{0,8},{8,0},{16,24},{24,16},{1,9},{9,1},{17,25},{25,17},{2,10},{10... | collective-permute-start | bytes 3145736 | tf_op jit(solution)/shard_map/ppermute | solution.py:983
  18.6 11.7 %collective-permute-start.2 = (bf16[2,8,128,256]{3,2,1,0:T(8,128)(2,1)}, bf16[2,8,128,256]{3,2,1,0:T(8,128)(2,1)S(1)}, u32[]{:S(2)}, u32[]{:S(2)}) collective-permute-start(bf16[2,8,128,256]{3,2,1,0:T(8,128)(2,1)} %get-tuple-element.58), channel_id=1, source_target_pairs={{0,8},{8,0},{16,24},{24,16},{1,9},{9,1},{17,25},{25,17},{2,10},{10... | collective-permute-start | bytes 3145736 | tf_op jit(solution)/shard_map/ppermute | solution.py:983
  27.3 15.2 %collective-permute-start.1 = (bf16[2,2,2,128,256]{4,3,0,1,2:T(8,128)(2,1)S(1)}, bf16[2,2,2,128,256]{4,3,0,1,2:T(8,128)(2,1)S(1)}, u32[]{:S(2)}, u32[]{:S(2)}) collective-permute-start(bf16[2,2,2,128,256]{4,3,0,1,2:T(8,128)(2,1)S(1)} %copy.21), channel_id=1, source_target_pairs={{0,16},{8,24},{16,0},{24,8},{1,17},{9,25},{17,1},{25,9},{2,18},{10... | collective-permute-start | bytes 1572872 | tf_op jit(solution)/shard_map/ppermute | solution.py:983
  30.8 13.7 %collective-permute-start.3 = (bf16[2,2,2,128,256]{4,3,1,2,0:T(8,128)(2,1)S(1)}, bf16[2,2,2,128,256]{4,3,1,2,0:T(8,128)(2,1)S(1)}, u32[]{:S(2)}, u32[]{:S(2)}) collective-permute-start(bf16[2,2,2,128,256]{4,3,1,2,0:T(8,128)(2,1)S(1)} %bitcast.90), channel_id=1, source_target_pairs={{0,1},{1,0},{2,3},{3,2},{4,5},{5,4},{6,7},{7,6},{8,9},{9,8},{10,11... | collective-permute-start | bytes 1572872 | tf_op jit(solution)/shard_map/ppermute | solution.py:983
  44.6 7.2 %collective-permute-start.4 = (bf16[2,2,128,256]{3,2,0,1:T(8,128)(2,1)S(1)}, bf16[2,2,128,256]{3,2,0,1:T(8,128)(2,1)S(1)}, u32[]{:S(2)}, u32[]{:S(2)}) collective-permute-start(bf16[2,2,128,256]{3,2,0,1:T(8,128)(2,1)S(1)} %slice_bitcast_fusion.2), channel_id=1, source_target_pairs={{0,1},{1,0},{2,3},{3,2},{4,5},{5,4},{6,7},{7,6},{8,9},{9,8},{10,11... | collective-permute-start | bytes 786440 | tf_op jit(solution)/shard_map/ppermute | solution.py:983
  46.3 7.2 %collective-permute-start.7 = (bf16[2,2,128,256]{3,2,0,1:T(8,128)(2,1)S(1)}, bf16[2,2,128,256]{3,2,0,1:T(8,128)(2,1)S(1)}, u32[]{:S(2)}, u32[]{:S(2)}) collective-permute-start(bf16[2,2,128,256]{3,2,0,1:T(8,128)(2,1)S(1)} %slice_bitcast_fusion), channel_id=1, source_target_pairs={{0,16},{8,24},{16,0},{24,8},{1,17},{9,25},{17,1},{25,9},{2,18},{10... | collective-permute-start | bytes 786440 | tf_op jit(solution)/shard_map/ppermute | solution.py:983
  53.6 6.6 %collective-permute-start.8 = (bf16[2,128,256]{2,1,0:T(8,128)(2,1)S(1)}, bf16[2,128,256]{2,1,0:T(8,128)(2,1)S(1)}, u32[]{:S(2)}, u32[]{:S(2)}) collective-permute-start(bf16[2,128,256]{2,1,0:T(8,128)(2,1)S(1)} %slice_bitcast_fusion.4), channel_id=1, source_target_pairs={{0,2},{1,3},{2,0},{3,1},{4,6},{5,7},{6,4},{7,5},{8,10},{9,11},{10,... | collective-permute-start | bytes 393224 | tf_op jit(solution)/shard_map/ppermute | solution.py:983
  57.5 6.4 %collective-permute-start.6 = (bf16[128,256]{1,0:T(8,128)(2,1)S(1)}, bf16[128,256]{1,0:T(8,128)(2,1)S(1)}, u32[]{:S(2)}, u32[]{:S(2)}) collective-permute-start(bf16[128,256]{1,0:T(8,128)(2,1)S(1)} %get-tuple-element.115), channel_id=1, source_target_pairs={{0,4},{1,5},{2,6},{3,7},{4,0},{5,1},{6,2},{7,3},{8,12},{9,13},{10,... | collective-permute-start | bytes 196616 | tf_op jit(solution)/shard_map/ppermute | solution.py:983
  60.8 5.2 %collective-permute-start.9 = (bf16[128,256]{1,0:T(8,128)(2,1)S(1)}, bf16[128,256]{1,0:T(8,128)(2,1)S(1)}, u32[]{:S(2)}, u32[]{:S(2)}) collective-permute-start(bf16[128,256]{1,0:T(8,128)(2,1)S(1)} %get-tuple-element.113), channel_id=1, source_target_pairs={{0,4},{1,5},{2,6},{3,7},{4,0},{5,1},{6,2},{7,3},{8,12},{9,13},{10,... | collective-permute-start | bytes 196616 | tf_op jit(solution)/shard_map/ppermute | solution.py:983
  70.1 7.4 %collective-permute-start.10 = (bf16[8,32,128]{2,1,0:T(8,128)(2,1)}, bf16[8,32,128]{2,1,0:T(8,128)(2,1)S(1)}, u32[]{:S(2)}, u32[]{:S(2)}) collective-permute-start(bf16[8,32,128]{2,1,0:T(8,128)(2,1)} %get-tuple-element.71), channel_id=1, source_target_pairs={{0,1},{1,0},{2,3},{3,2},{4,5},{5,4},{6,7},{7,6},{8,9},{9,8},{10,11... | collective-permute-start | bytes 196616 | tf_op jit(solution)/shard_map/ppermute | solution.py:983
  71.6 8.7 %collective-permute-start.11 = (bf16[8,32,128]{2,1,0:T(8,128)(2,1)}, bf16[8,32,128]{2,1,0:T(8,128)(2,1)S(1)}, u32[]{:S(2)}, u32[]{:S(2)}) collective-permute-start(bf16[8,32,128]{2,1,0:T(8,128)(2,1)} %get-tuple-element.72), channel_id=1, source_target_pairs={{0,2},{1,3},{2,0},{3,1},{4,6},{5,7},{6,4},{7,5},{8,10},{9,11},{10,... | collective-permute-start | bytes 196616 | tf_op jit(solution)/shard_map/ppermute | solution.py:983
  73.2 8.1 %collective-permute-start.12 = (bf16[8,32,128]{2,1,0:T(8,128)(2,1)}, bf16[8,32,128]{2,1,0:T(8,128)(2,1)S(1)}, u32[]{:S(2)}, u32[]{:S(2)}) collective-permute-start(bf16[8,32,128]{2,1,0:T(8,128)(2,1)} %get-tuple-element.73), channel_id=1, source_target_pairs={{0,3},{1,2},{2,1},{3,0},{4,7},{5,6},{6,5},{7,4},{8,11},{9,10},{10,... | collective-permute-start | bytes 196616 | tf_op jit(solution)/shard_map/ppermute | solution.py:983
  73.6 16.8 %collective-permute-start.16 = (bf16[8,32,128]{2,1,0:T(8,128)(2,1)}, bf16[8,32,128]{2,1,0:T(8,128)(2,1)S(1)}, u32[]{:S(2)}, u32[]{:S(2)}) collective-permute-start(bf16[8,32,128]{2,1,0:T(8,128)(2,1)} %get-tuple-element.82), channel_id=1, source_target_pairs={{0,4},{1,5},{2,6},{3,7},{4,0},{5,1},{6,2},{7,3},{8,12},{9,13},{10,... | collective-permute-start | bytes 196616 | tf_op jit(solution)/shard_map/ppermute | solution.py:983
  75.2 15.2 %collective-permute-start.17 = (bf16[8,32,128]{2,1,0:T(8,128)(2,1)}, bf16[8,32,128]{2,1,0:T(8,128)(2,1)S(1)}, u32[]{:S(2)}, u32[]{:S(2)}) collective-permute-start(bf16[8,32,128]{2,1,0:T(8,128)(2,1)} %get-tuple-element.83), channel_id=1, source_target_pairs={{0,5},{1,4},{2,7},{3,6},{4,1},{5,0},{6,3},{7,2},{8,13},{9,12},{10,... | collective-permute-start | bytes 196616 | tf_op jit(solution)/shard_map/ppermute | solution.py:983
  77.5 14.9 %collective-permute-start.18 = (bf16[8,32,128]{2,1,0:T(8,128)(2,1)}, bf16[8,32,128]{2,1,0:T(8,128)(2,1)S(1)}, u32[]{:S(2)}, u32[]{:S(2)}) collective-permute-start(bf16[8,32,128]{2,1,0:T(8,128)(2,1)} %get-tuple-element.84), channel_id=1, source_target_pairs={{0,6},{1,7},{2,4},{3,5},{4,2},{5,3},{6,0},{7,1},{8,14},{9,15},{10,... | collective-permute-start | bytes 196616 | tf_op jit(solution)/shard_map/ppermute | solution.py:983
  80.3 12.1 %collective-permute-start.19 = (bf16[8,32,128]{2,1,0:T(8,128)(2,1)}, bf16[8,32,128]{2,1,0:T(8,128)(2,1)S(1)}, u32[]{:S(2)}, u32[]{:S(2)}) collective-permute-start(bf16[8,32,128]{2,1,0:T(8,128)(2,1)} %get-tuple-element.85), channel_id=1, source_target_pairs={{0,7},{1,6},{2,5},{3,4},{4,3},{5,2},{6,1},{7,0},{8,15},{9,14},{10,... | collective-permute-start | bytes 196616 | tf_op jit(solution)/shard_map/ppermute | solution.py:983
  88.8 15.8 %collective-permute-start.13 = (bf16[8,32,128]{2,1,0:T(8,128)(2,1)}, bf16[8,32,128]{2,1,0:T(8,128)(2,1)S(1)}, u32[]{:S(2)}, u32[]{:S(2)}) collective-permute-start(bf16[8,32,128]{2,1,0:T(8,128)(2,1)} %get-tuple-element.79), channel_id=1, source_target_pairs={{0,1},{1,0},{2,3},{3,2},{4,5},{5,4},{6,7},{7,6},{8,9},{9,8},{10,11... | collective-permute-start | bytes 196616 | tf_op jit(solution)/shard_map/ppermute | solution.py:983
  90.4 17.1 %collective-permute-start.14 = (bf16[8,32,128]{2,1,0:T(8,128)(2,1)}, bf16[8,32,128]{2,1,0:T(8,128)(2,1)S(1)}, u32[]{:S(2)}, u32[]{:S(2)}) collective-permute-start(bf16[8,32,128]{2,1,0:T(8,128)(2,1)} %get-tuple-element.80), channel_id=1, source_target_pairs={{0,2},{1,3},{2,0},{3,1},{4,6},{5,7},{6,4},{7,5},{8,10},{9,11},{10,... | collective-permute-start | bytes 196616 | tf_op jit(solution)/shard_map/ppermute | solution.py:983
  90.4 18.1 %collective-permute-start.15 = (bf16[8,32,128]{2,1,0:T(8,128)(2,1)}, bf16[8,32,128]{2,1,0:T(8,128)(2,1)S(1)}, u32[]{:S(2)}, u32[]{:S(2)}) collective-permute-start(bf16[8,32,128]{2,1,0:T(8,128)(2,1)} %get-tuple-element.81), channel_id=1, source_target_pairs={{0,3},{1,2},{2,1},{3,0},{4,7},{5,6},{6,5},{7,4},{8,11},{9,10},{10,... | collective-permute-start | bytes 196616 | tf_op jit(solution)/shard_map/ppermute | solution.py:983
  100.8 7.7 %collective-permute-start.20 = (bf16[8,32,128]{2,1,0:T(8,128)(2,1)}, bf16[8,32,128]{2,1,0:T(8,128)(2,1)S(1)}, u32[]{:S(2)}, u32[]{:S(2)}) collective-permute-start(bf16[8,32,128]{2,1,0:T(8,128)(2,1)} %get-tuple-element.86), channel_id=1, source_target_pairs={{0,4},{1,5},{2,6},{3,7},{4,0},{5,1},{6,2},{7,3},{8,12},{9,13},{10,... | collective-permute-start | bytes 196616 | tf_op jit(solution)/shard_map/ppermute | solution.py:983
  102.3 6.3 %collective-permute-start.21 = (bf16[8,32,128]{2,1,0:T(8,128)(2,1)}, bf16[8,32,128]{2,1,0:T(8,128)(2,1)S(1)}, u32[]{:S(2)}, u32[]{:S(2)}) collective-permute-start(bf16[8,32,128]{2,1,0:T(8,128)(2,1)} %get-tuple-element.87), channel_id=1, source_target_pairs={{0,5},{1,4},{2,7},{3,6},{4,1},{5,0},{6,3},{7,2},{8,13},{9,12},{10,... | collective-permute-start | bytes 196616 | tf_op jit(solution)/shard_map/ppermute | solution.py:983
  104.6 6.5 %collective-permute-start.22 = (bf16[8,32,128]{2,1,0:T(8,128)(2,1)}, bf16[8,32,128]{2,1,0:T(8,128)(2,1)S(1)}, u32[]{:S(2)}, u32[]{:S(2)}) collective-permute-start(bf16[8,32,128]{2,1,0:T(8,128)(2,1)} %get-tuple-element.88), channel_id=1, source_target_pairs={{0,6},{1,7},{2,4},{3,5},{4,2},{5,3},{6,0},{7,1},{8,14},{9,15},{10,... | collective-permute-start | bytes 196616 | tf_op jit(solution)/shard_map/ppermute | solution.py:983
  107.4 7.2 %collective-permute-start.23 = (bf16[8,32,128]{2,1,0:T(8,128)(2,1)}, bf16[8,32,128]{2,1,0:T(8,128)(2,1)S(1)}, u32[]{:S(2)}, u32[]{:S(2)}) collective-permute-start(bf16[8,32,128]{2,1,0:T(8,128)(2,1)} %get-tuple-element.89), channel_id=1, source_target_pairs={{0,7},{1,6},{2,5},{3,4},{4,3},{5,2},{6,1},{7,0},{8,15},{9,14},{10,... | collective-permute-start | bytes 196616 | tf_op jit(solution)/shard_map/ppermute | solution.py:983
  118.0 5.4 %collective-permute-start.24 = (bf16[128,256]{1,0:T(8,128)(2,1)}, bf16[128,256]{1,0:T(8,128)(2,1)S(1)}, u32[]{:S(2)}, u32[]{:S(2)}) collective-permute-start(bf16[128,256]{1,0:T(8,128)(2,1)} %get-tuple-element.90), channel_id=1, source_target_pairs={{0,4},{1,5},{2,6},{3,7},{4,0},{5,1},{6,2},{7,3},{8,12},{9,13},{10,... | collective-permute-start | bytes 196616 | tf_op jit(solution)/shard_map/ppermute | solution.py:983
  118.0 6.8 %collective-permute-start.27 = (bf16[128,256]{1,0:T(8,128)(2,1)}, bf16[128,256]{1,0:T(8,128)(2,1)S(1)}, u32[]{:S(2)}, u32[]{:S(2)}) collective-permute-start(bf16[128,256]{1,0:T(8,128)(2,1)} %get-tuple-element.91), channel_id=1, source_target_pairs={{0,4},{1,5},{2,6},{3,7},{4,0},{5,1},{6,2},{7,3},{8,12},{9,13},{10,... | collective-permute-start | bytes 196616 | tf_op jit(solution)/shard_map/ppermute | solution.py:983
  125.7 5.2 %collective-permute-start.28 = (bf16[2,128,256]{2,1,0:T(8,128)(2,1)S(1)}, bf16[2,128,256]{2,1,0:T(8,128)(2,1)S(1)}, u32[]{:S(2)}, u32[]{:S(2)}) collective-permute-start(bf16[2,128,256]{2,1,0:T(8,128)(2,1)S(1)} %get-tuple-element.110), channel_id=1, source_target_pairs={{0,2},{1,3},{2,0},{3,1},{4,6},{5,7},{6,4},{7,5},{8,10},{9,11},{10,... | collective-permute-start | bytes 393224 | tf_op jit(solution)/shard_map/ppermute | solution.py:983
  129.3 7.0 %collective-permute-start.26 = (bf16[2,2,128,256]{3,2,0,1:T(8,128)(2,1)S(1)}, bf16[2,2,128,256]{3,2,0,1:T(8,128)(2,1)S(1)}, u32[]{:S(2)}, u32[]{:S(2)}) collective-permute-start(bf16[2,2,128,256]{3,2,0,1:T(8,128)(2,1)S(1)} %get-tuple-element.108), channel_id=1, source_target_pairs={{0,1},{1,0},{2,3},{3,2},{4,5},{5,4},{6,7},{7,6},{8,9},{9,8},{10,11... | collective-permute-start | bytes 786440 | tf_op jit(solution)/shard_map/ppermute | solution.py:983
  130.9 6.4 %collective-permute-start.29 = (bf16[2,2,128,256]{3,2,0,1:T(8,128)(2,1)S(1)}, bf16[2,2,128,256]{3,2,0,1:T(8,128)(2,1)S(1)}, u32[]{:S(2)}, u32[]{:S(2)}) collective-permute-start(bf16[2,2,128,256]{3,2,0,1:T(8,128)(2,1)S(1)} %get-tuple-element.106), channel_id=1, source_target_pairs={{0,16},{8,24},{16,0},{24,8},{1,17},{9,25},{17,1},{25,9},{2,18},{10... | collective-permute-start | bytes 786440 | tf_op jit(solution)/shard_map/ppermute | solution.py:983
  137.4 9.2 %collective-permute-start.30 = (bf16[2,2,2,128,256]{4,3,0,1,2:T(8,128)(2,1)S(1)}, bf16[2,2,2,128,256]{4,3,0,1,2:T(8,128)(2,1)S(1)}, u32[]{:S(2)}, u32[]{:S(2)}) collective-permute-start(bf16[2,2,2,128,256]{4,3,0,1,2:T(8,128)(2,1)S(1)} %pad_maximum_fusion.2), channel_id=1, source_target_pairs={{0,16},{8,24},{16,0},{24,8},{1,17},{9,25},{17,1},{25,9},{2,18},{10... | collective-permute-start | bytes 1572872 | tf_op jit(solution)/shard_map/ppermute | solution.py:983
  138.1 9.2 %collective-permute-start.31 = (bf16[2,2,2,128,256]{4,3,1,2,0:T(8,128)(2,1)S(1)}, bf16[2,2,2,128,256]{4,3,1,2,0:T(8,128)(2,1)S(1)}, u32[]{:S(2)}, u32[]{:S(2)}) collective-permute-start(bf16[2,2,2,128,256]{4,3,1,2,0:T(8,128)(2,1)S(1)} %pad_maximum_fusion.3), channel_id=1, source_target_pairs={{0,1},{1,0},{2,3},{3,2},{4,5},{5,4},{6,7},{7,6},{8,9},{9,8},{10,11... | collective-permute-start | bytes 1572872 | tf_op jit(solution)/shard_map/ppermute | solution.py:983
  147.5 7.9 %collective-permute-start.33 = (bf16[2,8,128,256]{3,2,1,0:T(8,128)(2,1)S(1)}, bf16[2,8,128,256]{3,2,1,0:T(8,128)(2,1)S(1)}, u32[]{:S(2)}, u32[]{:S(2)}) collective-permute-start(bf16[2,8,128,256]{3,2,1,0:T(8,128)(2,1)S(1)} %bitcast.86), channel_id=1, source_target_pairs={{0,8},{8,0},{16,24},{24,16},{1,9},{9,1},{17,25},{25,17},{2,10},{10... | collective-permute-start | bytes 3145736 | tf_op jit(solution)/shard_map/ppermute | solution.py:983
  147.6 7.9 %collective-permute-start.32 = (bf16[2,8,128,256]{3,2,1,0:T(8,128)(2,1)S(1)}, bf16[2,8,128,256]{3,2,1,0:T(8,128)(2,1)S(1)}, u32[]{:S(2)}, u32[]{:S(2)}) collective-permute-start(bf16[2,8,128,256]{3,2,1,0:T(8,128)(2,1)S(1)} %bitcast.84), channel_id=1, source_target_pairs={{0,8},{8,0},{16,24},{24,16},{1,9},{9,1},{17,25},{25,17},{2,10},{10... | collective-permute-start | bytes 3145736 | tf_op jit(solution)/shard_map/ppermute | solution.py:983
  (26 other events, 100.5 us)

commit v6 on v5

--- a/solution.py
+++ b/solution.py
@@ -609,8 +609,11 @@
         pred_r = jnp.sum((row_r * part_r - row_i * part_i).reshape(TS, GROUP, LANES), axis=0)
         pred_i = jnp.sum((row_r * part_i + row_i * part_r).reshape(TS, GROUP, LANES), axis=0)
         weight = weight_ref[at, :]
-        res_r = jnp.tile(weight * (meas_ref[0, at, :] - pred_r), (TS, 1))
-        res_i = jnp.tile(weight * (meas_ref[1, at, :] - pred_i), (TS, 1))
+        meas_r, meas_i = (
+            meas_ref[pl.ds(2 * GROUP * g + z, GROUP, stride=2), :] for z in range(2)
+        )
+        res_r = jnp.tile(weight * (meas_r - pred_r), (TS, 1))
+        res_i = jnp.tile(weight * (meas_i - pred_i), (TS, 1))
         s_r = (row_r * res_r + row_i * res_i).astype(BF16)
         s_i = (row_r * res_i - row_i * res_r).astype(BF16)
         both = jnp.concatenate(
@@ -650,7 +653,7 @@
             grid=(n,),
             in_specs=[whole] * n
             + [
-                pl.BlockSpec((2, slots, LANES), lambda i, m: (0, source(i, m), 0)),
+                pl.BlockSpec((2 * slots, LANES), lambda i, m: (source(i, m), 0)),
                 pl.BlockSpec((slots, LANES), lambda i, m: (source(i, m), 0)),
                 pl.BlockSpec((groups, 2, rows, LANES), lambda i, m: (source(i, m), 0, 0, 0)),
                 pl.BlockSpec((groups, rows, 2 * LANES), lambda i, m: (source(i, m), 0, 0)),
@@ -1100,7 +1103,7 @@
         pixels, values, weights, counts = operand
         live = jnp.arange(weights.shape[1], dtype=jnp.int32)[None, :] < counts[:, None]
         weights = per_slot(jnp.where(live, weights, 0.0))
-        values = jnp.transpose(per_slot(values), (1, 0, 2))
+        values = per_slot(values).reshape(-1, values.shape[2])
         pixels = jnp.transpose(per_slot(pixels), (1, 0, 2))
         return values, weights, kernels(pixels, 4)
 

time: 174 us -> 173 us (level)
    unnamed x51 -> x48, local copies, waits for them, and re-layouts: 6.6 us -> 5.74 us
where the time goes in v6:
time: 173 us; the launch traced here: 172 us
  Pallas kernels  78.9 us (46%)
  starting transfers between devices  45.8 us (26%)
  waiting for transfers between devices  33.4 us (19%)
  local copies, waits for them, and re-layouts  7.44 us (4%)
  other arithmetic  5.84 us (3%)
    ppermute x34, starting transfers between devices, swap(): lax.ppermute(value, axis, [(i, i ^ bit) for i in range(lax.axis_size(axis...  45.8 us
    ppermute x34, waiting for transfers between devices, swap(): lax.ppermute(value, axis, [(i, i ^ bit) for i in range(lax.axis_size(axis...  33.4 us
    pallas_call x1, Pallas kernels, forward(): pl.pallas_call(forward_kernel, grid_spec=pltpu.PrefetchScalarGridSpec(num...  17.4 us
    pallas_call x1, Pallas kernels, backward(): pl.pallas_call(backward_kernel, grid_spec=pltpu.PrefetchScalarGridSpec(nu...  15.4 us
    pallas_call x2, Pallas kernels, visit(): pl.pallas_call(visit_kernel, grid_spec=pltpu.PrefetchScalarGridSpec(num_s...  14 us
    pallas_call x1, Pallas kernels, cols_backward(): pl.pallas_call(partial(cols_backward_kernel, length=length), grid_spec=pl...  6.75 us
    pallas_call x1, Pallas kernels, adjoint_tables(): pl.pallas_call(adjoint_tables_kernel, in_specs=[smem] * 2 + [vmem] * 3, o...  6.7 us
    pallas_call x1, Pallas kernels, kernels(): pl.pallas_call(kernels_kernel, grid=(steps,), in_specs=[pl.BlockSpec((3,...  6.53 us
  transfers between devices with their start and end apart: 34, of which 16 were waited for; matrix products, arithmetic and copies ran while one was open for 4% of the time, Pallas kernels for 23%

profile of v6, /device:TPU:0, one launch (start us, length us, event | category | flops | bytes accessed | tf_op | source)
XLA Modules:
  0.0 172.0 jit_solution(4836950169742288382)
XLA Ops:
  0.7 17.4 %forward.1 = (bf16[2,2,16,32,512]{4,3,2,1,0:T(8,128)(2,1)}, bf16[2,8,128,256]{3,2,1,0:T(8,128)(2,1)}, bf16[2,8,128,256]{3,2,1,0:T(8,128)(2,1)}) custom-call(s32[2]{0:T(128)} %pad_add_fusion.ids, s32[4]{0:T(128)} %row_off.7, s32[4]{0:T(128)} %col_off.5, bf16[2,4096,512]{2,1,0:T(8,128)(2,1)} %x_ref.1, f32[32,128]{1,0:T(8,128)} %bitcast.106, ...), custom_call_target="tpu_custom_call" | custom-call | flops 12000000000 | bytes 16777216 | tf_op jit(solution)/shard_map/forward/pallas_call | solution.py:328
  18.7 5.9 %cols_forward.1 = (bf16[2,8,128,256]{3,2,1,0:T(8,128)(2,1)}, bf16[2,8,128,256]{3,2,1,0:T(8,128)(2,1)}) custom-call(s32[2]{0:T(128)} %pad_add_fusion.ids, bf16[2,2,512,512]{3,2,1,0:T(8,128)(2,1)} %bitcast.108, bf16[4096,512]{1,0:T(8,128)(2,1)} %constant.22.clone.fr_ref, bf16[4096,512]{1,0:T(8,128)(2,1)} %constant.23.clone.fi_ref), custom_call_target="tpu_custom_call" | custom-call | flops 4000000000 | bytes 6291456 | tf_op jit(solution)/shard_map/cols_forward/pallas_call | solution.py:380
  24.6 1.6 add.24
  26.4 3.0 %collective-permute-start.1 = (bf16[2,2,2,128,256]{4,3,0,1,2:T(8,128)(2,1)S(1)}, bf16[2,2,2,128,256]{4,3,0,1,2:T(8,128)(2,1)S(1)}, u32[]{:S(2)}, u32[]{:S(2)}) collective-permute-start(bf16[2,2,2,128,256]{4,3,0,1,2:T(8,128)(2,1)S(1)} %copy.19), channel_id=1, source_target_pairs={{0,16},{8,24},{16,0},{24,8},{1,17},{9,25},{17,1},{25,9},{2,18},{10... | collective-permute-start | bytes 1572872 | tf_op jit(solution)/shard_map/ppermute | solution.py:986
  32.3 6.5 %kernels.1 = (bf16[64,2,128,128]{3,2,1,0:T(8,128)(2,1)}, bf16[64,128,256]{2,1,0:T(8,128)(2,1)}) custom-call(s32[3,512,128]{2,1,0:T(8,128)} %bitcast.103), custom_call_target="tpu_custom_call" | custom-call | flops 6000000000 | bytes 9437184 | tf_op jit(solution)/shard_map/kernels/pallas_call | solution.py:570
  38.9 2.7 %collective-permute-done.1 = bf16[2,2,2,128,256]{4,3,0,1,2:T(8,128)(2,1)S(1)} collective-permute-done((bf16[2,2,2,128,256]{4,3,0,1,2:T(8,128)(2,1)S(1)}, bf16[2,2,2,128,256]{4,3,0,1,2:T(8,128)(2,1)S(1)}, u32[]{:S(2)}, u32[]{:S(2)}) %collective-permute-start.1) | collective-permute-done | bytes 524320 | tf_op jit(solution)/shard_map/ppermute | solution.py:986
  41.6 2.0 %collective-permute-done.3 = bf16[2,2,2,128,256]{4,3,1,2,0:T(8,128)(2,1)S(1)} collective-permute-done((bf16[2,2,2,128,256]{4,3,1,2,0:T(8,128)(2,1)S(1)}, bf16[2,2,2,128,256]{4,3,1,2,0:T(8,128)(2,1)S(1)}, u32[]{:S(2)}, u32[]{:S(2)}) %collective-permute-start.3) | collective-permute-done | bytes 524320 | tf_op jit(solution)/shard_map/ppermute | solution.py:986
  46.0 4.9 %collective-permute-done.4 = bf16[2,2,128,256]{3,2,0,1:T(8,128)(2,1)S(1)} collective-permute-done((bf16[2,2,128,256]{3,2,0,1:T(8,128)(2,1)S(1)}, bf16[2,2,128,256]{3,2,0,1:T(8,128)(2,1)S(1)}, u32[]{:S(2)}, u32[]{:S(2)}) %collective-permute-start.4) | collective-permute-done | bytes 262176 | tf_op jit(solution)/shard_map/ppermute | solution.py:986
  50.9 1.6 collective-permute-start.5
  54.0 1.9 %collective-permute-done.5 = bf16[2,128,256]{2,1,0:T(8,128)(2,1)S(1)} collective-permute-done((bf16[2,128,256]{2,1,0:T(8,128)(2,1)S(1)}, bf16[2,128,256]{2,1,0:T(8,128)(2,1)S(1)}, u32[]{:S(2)}, u32[]{:S(2)}) %collective-permute-start.5) | collective-permute-done | bytes 131104 | tf_op jit(solution)/shard_map/ppermute | solution.py:986
  56.6 2.6 %collective-permute-start.6 = (bf16[128,256]{1,0:T(8,128)(2,1)S(1)}, bf16[128,256]{1,0:T(8,128)(2,1)S(1)}, u32[]{:S(2)}, u32[]{:S(2)}) collective-permute-start(bf16[128,256]{1,0:T(8,128)(2,1)S(1)} %get-tuple-element.115), channel_id=1, source_target_pairs={{0,4},{1,5},{2,6},{3,7},{4,0},{5,1},{6,2},{7,3},{8,12},{9,13},{10,... | collective-permute-start | bytes 196616 | tf_op jit(solution)/shard_map/ppermute | solution.py:986
  61.3 1.7 %collective-permute-done.6.refs_1_ = bf16[128,256]{1,0:T(8,128)(2,1)S(1)} collective-permute-done((bf16[128,256]{1,0:T(8,128)(2,1)S(1)}, bf16[128,256]{1,0:T(8,128)(2,1)S(1)}, u32[]{:S(2)}, u32[]{:S(2)}) %collective-permute-start.6) | collective-permute-done | bytes 65568 | tf_op jit(solution)/shard_map/ppermute | solution.py:986
  63.1 2.0 %collective-permute-done.9.refs_3_ = bf16[128,256]{1,0:T(8,128)(2,1)S(1)} collective-permute-done((bf16[128,256]{1,0:T(8,128)(2,1)S(1)}, bf16[128,256]{1,0:T(8,128)(2,1)S(1)}, u32[]{:S(2)}, u32[]{:S(2)}) %collective-permute-start.9) | collective-permute-done | bytes 65568 | tf_op jit(solution)/shard_map/ppermute | solution.py:986
  65.7 3.5 %route.1 = (bf16[8,32,128]{2,1,0:T(8,128)(2,1)}, bf16[8,32,128]{2,1,0:T(8,128)(2,1)}, bf16[8,32,128]{2,1,0:T(8,128)(2,1)}, bf16[8,32,128]{2,1,0:T(8,128)(2,1)}, ...) custom-call(s32[2]{0:T(128)} %pad_add_fusion.ids, ...), custom_call_target="tpu_custom_call" | custom-call | tf_op jit(solution)/shard_map/route/pallas_call | solution.py:448
  74.3 2.3 %collective-permute-start.17 = (bf16[8,32,128]{2,1,0:T(8,128)(2,1)}, bf16[8,32,128]{2,1,0:T(8,128)(2,1)S(1)}, u32[]{:S(2)}, u32[]{:S(2)}) collective-permute-start(bf16[8,32,128]{2,1,0:T(8,128)(2,1)} %get-tuple-element.83), channel_id=1, source_target_pairs={{0,5},{1,4},{2,7},{3,6},{4,1},{5,0},{6,3},{7,2},{8,13},{9,12},{10,... | collective-permute-start | bytes 196616 | tf_op jit(solution)/shard_map/ppermute | solution.py:986
  76.6 2.7 %collective-permute-start.18 = (bf16[8,32,128]{2,1,0:T(8,128)(2,1)}, bf16[8,32,128]{2,1,0:T(8,128)(2,1)S(1)}, u32[]{:S(2)}, u32[]{:S(2)}) collective-permute-start(bf16[8,32,128]{2,1,0:T(8,128)(2,1)} %get-tuple-element.84), channel_id=1, source_target_pairs={{0,6},{1,7},{2,4},{3,5},{4,2},{5,3},{6,0},{7,1},{8,14},{9,15},{10,... | collective-permute-start | bytes 196616 | tf_op jit(solution)/shard_map/ppermute | solution.py:986
  81.0 6.9 %visit.2 = (bf16[8,32,128]{2,1,0:T(8,128)(2,1)}, bf16[8,32,128]{2,1,0:T(8,128)(2,1)}, bf16[8,32,128]{2,1,0:T(8,128)(2,1)}, bf16[8,32,128]{2,1,0:T(8,128)(2,1)}) custom-call(s32[2]{0:T(128)} %pad_add_fusion.ids, bf16[8,32,128]{2,1,0:T(8,128)(2,1)} %get-tuple-element.70.refs_0_, bf16[8,32,128]{2,1,0:T(8,128)(2,1)} %copy-done.20, ...), custom_call_target="tpu_custom_call" | custom-call | flops 7200000000 | bytes 5242880 | tf_op jit(solution)/shard_map/visit/pallas_call | solution.py:649
  89.5 2.0 %collective-permute-start.15 = (bf16[8,32,128]{2,1,0:T(8,128)(2,1)}, bf16[8,32,128]{2,1,0:T(8,128)(2,1)S(1)}, u32[]{:S(2)}, u32[]{:S(2)}) collective-permute-start(bf16[8,32,128]{2,1,0:T(8,128)(2,1)} %get-tuple-element.81), channel_id=1, source_target_pairs={{0,3},{1,2},{2,1},{3,0},{4,7},{5,6},{6,5},{7,4},{8,11},{9,10},{10,... | collective-permute-start | bytes 196616 | tf_op jit(solution)/shard_map/ppermute | solution.py:986
  92.7 7.1 %visit.3 = (bf16[8,32,128]{2,1,0:T(8,128)(2,1)}, bf16[8,32,128]{2,1,0:T(8,128)(2,1)}, bf16[8,32,128]{2,1,0:T(8,128)(2,1)}, bf16[8,32,128]{2,1,0:T(8,128)(2,1)}) custom-call(s32[2]{0:T(128)} %pad_add_fusion.ids, bf16[8,32,128]{2,1,0:T(8,128)(2,1)} %copy-done.16, bf16[8,32,128]{2,1,0:T(8,128)(2,1)} %copy-done.17, bf16[8,32,128]{2,1,0:T(8,128)(2,1)} %copy-done.18, ...), custom_call_target="tpu_custom_call" | custom-call | flops 7200000000 | bytes 5242880 | tf_op jit(solution)/shard_map/visit/pallas_call | solution.py:649
  101.3 2.4 %collective-permute-start.21 = (bf16[8,32,128]{2,1,0:T(8,128)(2,1)}, bf16[8,32,128]{2,1,0:T(8,128)(2,1)S(1)}, u32[]{:S(2)}, u32[]{:S(2)}) collective-permute-start(bf16[8,32,128]{2,1,0:T(8,128)(2,1)} %get-tuple-element.87), channel_id=1, source_target_pairs={{0,5},{1,4},{2,7},{3,6},{4,1},{5,0},{6,3},{7,2},{8,13},{9,12},{10,... | collective-permute-start | bytes 196616 | tf_op jit(solution)/shard_map/ppermute | solution.py:986
  103.7 2.7 %collective-permute-start.22 = (bf16[8,32,128]{2,1,0:T(8,128)(2,1)}, bf16[8,32,128]{2,1,0:T(8,128)(2,1)S(1)}, u32[]{:S(2)}, u32[]{:S(2)}) collective-permute-start(bf16[8,32,128]{2,1,0:T(8,128)(2,1)} %get-tuple-element.88), channel_id=1, source_target_pairs={{0,6},{1,7},{2,4},{3,5},{4,2},{5,3},{6,0},{7,1},{8,14},{9,15},{10,... | collective-permute-start | bytes 196616 | tf_op jit(solution)/shard_map/ppermute | solution.py:986
  107.6 2.6 %collective-permute-done.22.refs_6_ = bf16[8,32,128]{2,1,0:T(8,128)(2,1)S(1)} collective-permute-done((bf16[8,32,128]{2,1,0:T(8,128)(2,1)}, bf16[8,32,128]{2,1,0:T(8,128)(2,1)S(1)}, u32[]{:S(2)}, u32[]{:S(2)}) %collective-permute-start.22) | collective-permute-done | bytes 65568 | tf_op jit(solution)/shard_map/ppermute | solution.py:986
  110.2 3.4 %collective-permute-done.23.refs_7_ = bf16[8,32,128]{2,1,0:T(8,128)(2,1)S(1)} collective-permute-done((bf16[8,32,128]{2,1,0:T(8,128)(2,1)}, bf16[8,32,128]{2,1,0:T(8,128)(2,1)S(1)}, u32[]{:S(2)}, u32[]{:S(2)}) %collective-permute-start.23) | collective-permute-done | bytes 65568 | tf_op jit(solution)/shard_map/ppermute | solution.py:986
  114.3 2.8 %unroute.1 = (bf16[128,256]{1,0:T(8,128)(2,1)}, bf16[128,256]{1,0:T(8,128)(2,1)}) custom-call(s32[128]{0:T(128)} %get-tuple-element.69.where_ref, bf16[8,32,128]{2,1,0:T(8,128)(2,1)} %get-tuple-element.78.refs_0_, bf16[8,32,128]{2,1,0:T(8,128)(2,1)} %copy-done.6, bf16[8,32,128]{2,1,0:T(8,128)(2,1)} %copy-done.7, bf16[8,32,128]{2,1,0:T(8,128)(2,1)} %copy-done.8, ...), custom_call_target="tpu_custom_call" | custom-call | tf_op jit(solution)/shard_map/unroute/pallas_call | solution.py:497
  117.1 2.9 %collective-permute-start.27 = (bf16[128,256]{1,0:T(8,128)(2,1)}, bf16[128,256]{1,0:T(8,128)(2,1)S(1)}, u32[]{:S(2)}, u32[]{:S(2)}) collective-permute-start(bf16[128,256]{1,0:T(8,128)(2,1)} %get-tuple-element.91), channel_id=1, source_target_pairs={{0,4},{1,5},{2,6},{3,7},{4,0},{5,1},{6,2},{7,3},{8,12},{9,13},{10,... | collective-permute-start | bytes 196616 | tf_op jit(solution)/shard_map/ppermute | solution.py:986
  120.0 2.4 %collective-permute-done.24 = bf16[128,256]{1,0:T(8,128)(2,1)S(1)} collective-permute-done((bf16[128,256]{1,0:T(8,128)(2,1)}, bf16[128,256]{1,0:T(8,128)(2,1)S(1)}, u32[]{:S(2)}, u32[]{:S(2)}) %collective-permute-start.24) | collective-permute-done | bytes 65568 | tf_op jit(solution)/shard_map/ppermute | solution.py:986
  124.7 1.6 collective-permute-start.28
  126.3 2.0 %collective-permute-done.25 = bf16[2,128,256]{2,1,0:T(8,128)(2,1)S(1)} collective-permute-done((bf16[2,128,256]{2,1,0:T(8,128)(2,1)S(1)}, bf16[2,128,256]{2,1,0:T(8,128)(2,1)S(1)}, u32[]{:S(2)}, u32[]{:S(2)}) %collective-permute-start.25) | collective-permute-done | bytes 131104 | tf_op jit(solution)/shard_map/ppermute | solution.py:986
  130.4 5.0 %collective-permute-done.26 = bf16[2,2,128,256]{3,2,0,1:T(8,128)(2,1)S(1)} collective-permute-done((bf16[2,2,128,256]{3,2,0,1:T(8,128)(2,1)S(1)}, bf16[2,2,128,256]{3,2,0,1:T(8,128)(2,1)S(1)}, u32[]{:S(2)}, u32[]{:S(2)}) %collective-permute-start.26) | collective-permute-done | bytes 262176 | tf_op jit(solution)/shard_map/ppermute | solution.py:986
  138.3 6.7 %adjoint_tables.1 = (bf16[16,512,256]{2,1,0:T(8,128)(2,1)}, f32[4096,128]{1,0:T(8,128)}) custom-call(s32[2]{0:T(128)} %pad_add_fusion.ids, s32[4]{0:T(128)} %row_off.7, f32[16,32,256]{2,1,0:T(8,128)} %constant.20.clone.tr_ref, f32[16,32,256]{2,1,0:T(8,128)} %constant.21.clone.ti_ref, f32[32,128]{1,0:T(8,128)} %bitcast.107), custom_call_target="tpu_custom_call" | custom-call | flops 7000000000 | bytes 7340032 | tf_op jit(solution)/shard_map/adjoint_tables/pallas_call | solution.py:801
  147.8 6.7 %cols_backward.1.even_ref = bf16[16,128,512]{2,1,0:T(8,128)(2,1)} custom-call(s32[2]{0:T(128)} %pad_add_fusion.ids, s32[4]{0:T(128)} %row_off.7, s32[4]{0:T(128)} %col_off.5, bf16[2,8,128,256]{3,2,1,0:T(8,128)(2,1)} %bitcast.83, bf16[2,8,128,256]{3,2,1,0:T(8,128)(2,1)} %bitcast.85, bf16[4096,512]{1,0:T(8,128)(2,1)} %constant.22.clone.fr_ref, ...), custom_call_target="tpu_custom_call" | custom-call | flops 5000000000 | bytes 6291456 | tf_op jit(solution)/shard_map/cols_backward/pallas_call | solution.py:759
  156.4 15.4 %backward.1 = bf16[2,16,256,512]{3,2,1,0:T(8,128)(2,1)} custom-call(s32[2]{0:T(128)} %pad_add_fusion.ids, s32[4]{0:T(128)} %row_off.7, s32[4]{0:T(128)} %col_off.5, bf16[2,8,128,256]{3,2,1,0:T(8,128)(2,1)} %copy-done.2, bf16[2,8,128,256]{3,2,1,0:T(8,128)(2,1)} %copy-done.1, bf16[4096,512]{1,0:T(8,128)(2,1)} %constant.22.clone.fr_ref, ...), custom_call_target="tpu_custom_call" | custom-call | tf_op jit(solution)/shard_map/backward/pallas_call | solution.py:953
  (123 shorter events, 36.2 us)
Async XLA Ops:
  18.1 6.5 %collective-permute-start = (bf16[2,8,128,256]{3,2,1,0:T(8,128)(2,1)}, bf16[2,8,128,256]{3,2,1,0:T(8,128)(2,1)S(1)}, u32[]{:S(2)}, u32[]{:S(2)}) collective-permute-start(bf16[2,8,128,256]{3,2,1,0:T(8,128)(2,1)} %get-tuple-element.55), channel_id=1, source_target_pairs={{0,8},{8,0},{16,24},{24,16},{1,9},{9,1},{17,25},{25,17},{2,10},{10... | collective-permute-start | bytes 3145736 | tf_op jit(solution)/shard_map/ppermute | solution.py:986
  18.6 10.8 %collective-permute-start.2 = (bf16[2,8,128,256]{3,2,1,0:T(8,128)(2,1)}, bf16[2,8,128,256]{3,2,1,0:T(8,128)(2,1)S(1)}, u32[]{:S(2)}, u32[]{:S(2)}) collective-permute-start(bf16[2,8,128,256]{3,2,1,0:T(8,128)(2,1)} %get-tuple-element.58), channel_id=1, source_target_pairs={{0,8},{8,0},{16,24},{24,16},{1,9},{9,1},{17,25},{25,17},{2,10},{10... | collective-permute-start | bytes 3145736 | tf_op jit(solution)/shard_map/ppermute | solution.py:986
  26.4 15.2 %collective-permute-start.1 = (bf16[2,2,2,128,256]{4,3,0,1,2:T(8,128)(2,1)S(1)}, bf16[2,2,2,128,256]{4,3,0,1,2:T(8,128)(2,1)S(1)}, u32[]{:S(2)}, u32[]{:S(2)}) collective-permute-start(bf16[2,2,2,128,256]{4,3,0,1,2:T(8,128)(2,1)S(1)} %copy.19), channel_id=1, source_target_pairs={{0,16},{8,24},{16,0},{24,8},{1,17},{9,25},{17,1},{25,9},{2,18},{10... | collective-permute-start | bytes 1572872 | tf_op jit(solution)/shard_map/ppermute | solution.py:986
  29.9 13.7 %collective-permute-start.3 = (bf16[2,2,2,128,256]{4,3,1,2,0:T(8,128)(2,1)S(1)}, bf16[2,2,2,128,256]{4,3,1,2,0:T(8,128)(2,1)S(1)}, u32[]{:S(2)}, u32[]{:S(2)}) collective-permute-start(bf16[2,2,2,128,256]{4,3,1,2,0:T(8,128)(2,1)S(1)} %bitcast.86), channel_id=1, source_target_pairs={{0,1},{1,0},{2,3},{3,2},{4,5},{5,4},{6,7},{7,6},{8,9},{9,8},{10,11... | collective-permute-start | bytes 1572872 | tf_op jit(solution)/shard_map/ppermute | solution.py:986
  43.7 7.2 %collective-permute-start.4 = (bf16[2,2,128,256]{3,2,0,1:T(8,128)(2,1)S(1)}, bf16[2,2,128,256]{3,2,0,1:T(8,128)(2,1)S(1)}, u32[]{:S(2)}, u32[]{:S(2)}) collective-permute-start(bf16[2,2,128,256]{3,2,0,1:T(8,128)(2,1)S(1)} %slice_bitcast_fusion.2), channel_id=1, source_target_pairs={{0,1},{1,0},{2,3},{3,2},{4,5},{5,4},{6,7},{7,6},{8,9},{9,8},{10,11... | collective-permute-start | bytes 786440 | tf_op jit(solution)/shard_map/ppermute | solution.py:986
  45.4 7.2 %collective-permute-start.7 = (bf16[2,2,128,256]{3,2,0,1:T(8,128)(2,1)S(1)}, bf16[2,2,128,256]{3,2,0,1:T(8,128)(2,1)S(1)}, u32[]{:S(2)}, u32[]{:S(2)}) collective-permute-start(bf16[2,2,128,256]{3,2,0,1:T(8,128)(2,1)S(1)} %slice_bitcast_fusion), channel_id=1, source_target_pairs={{0,16},{8,24},{16,0},{24,8},{1,17},{9,25},{17,1},{25,9},{2,18},{10... | collective-permute-start | bytes 786440 | tf_op jit(solution)/shard_map/ppermute | solution.py:986
  52.6 6.6 %collective-permute-start.8 = (bf16[2,128,256]{2,1,0:T(8,128)(2,1)S(1)}, bf16[2,128,256]{2,1,0:T(8,128)(2,1)S(1)}, u32[]{:S(2)}, u32[]{:S(2)}) collective-permute-start(bf16[2,128,256]{2,1,0:T(8,128)(2,1)S(1)} %slice_bitcast_fusion.4), channel_id=1, source_target_pairs={{0,2},{1,3},{2,0},{3,1},{4,6},{5,7},{6,4},{7,5},{8,10},{9,11},{10,... | collective-permute-start | bytes 393224 | tf_op jit(solution)/shard_map/ppermute | solution.py:986
  56.6 6.4 %collective-permute-start.6 = (bf16[128,256]{1,0:T(8,128)(2,1)S(1)}, bf16[128,256]{1,0:T(8,128)(2,1)S(1)}, u32[]{:S(2)}, u32[]{:S(2)}) collective-permute-start(bf16[128,256]{1,0:T(8,128)(2,1)S(1)} %get-tuple-element.115), channel_id=1, source_target_pairs={{0,4},{1,5},{2,6},{3,7},{4,0},{5,1},{6,2},{7,3},{8,12},{9,13},{10,... | collective-permute-start | bytes 196616 | tf_op jit(solution)/shard_map/ppermute | solution.py:986
  59.9 5.2 %collective-permute-start.9 = (bf16[128,256]{1,0:T(8,128)(2,1)S(1)}, bf16[128,256]{1,0:T(8,128)(2,1)S(1)}, u32[]{:S(2)}, u32[]{:S(2)}) collective-permute-start(bf16[128,256]{1,0:T(8,128)(2,1)S(1)} %get-tuple-element.113), channel_id=1, source_target_pairs={{0,4},{1,5},{2,6},{3,7},{4,0},{5,1},{6,2},{7,3},{8,12},{9,13},{10,... | collective-permute-start | bytes 196616 | tf_op jit(solution)/shard_map/ppermute | solution.py:986
  69.2 7.4 %collective-permute-start.10 = (bf16[8,32,128]{2,1,0:T(8,128)(2,1)}, bf16[8,32,128]{2,1,0:T(8,128)(2,1)S(1)}, u32[]{:S(2)}, u32[]{:S(2)}) collective-permute-start(bf16[8,32,128]{2,1,0:T(8,128)(2,1)} %get-tuple-element.71), channel_id=1, source_target_pairs={{0,1},{1,0},{2,3},{3,2},{4,5},{5,4},{6,7},{7,6},{8,9},{9,8},{10,11... | collective-permute-start | bytes 196616 | tf_op jit(solution)/shard_map/ppermute | solution.py:986
  70.7 8.6 %collective-permute-start.11 = (bf16[8,32,128]{2,1,0:T(8,128)(2,1)}, bf16[8,32,128]{2,1,0:T(8,128)(2,1)S(1)}, u32[]{:S(2)}, u32[]{:S(2)}) collective-permute-start(bf16[8,32,128]{2,1,0:T(8,128)(2,1)} %get-tuple-element.72), channel_id=1, source_target_pairs={{0,2},{1,3},{2,0},{3,1},{4,6},{5,7},{6,4},{7,5},{8,10},{9,11},{10,... | collective-permute-start | bytes 196616 | tf_op jit(solution)/shard_map/ppermute | solution.py:986
  72.3 8.1 %collective-permute-start.12 = (bf16[8,32,128]{2,1,0:T(8,128)(2,1)}, bf16[8,32,128]{2,1,0:T(8,128)(2,1)S(1)}, u32[]{:S(2)}, u32[]{:S(2)}) collective-permute-start(bf16[8,32,128]{2,1,0:T(8,128)(2,1)} %get-tuple-element.73), channel_id=1, source_target_pairs={{0,3},{1,2},{2,1},{3,0},{4,7},{5,6},{6,5},{7,4},{8,11},{9,10},{10,... | collective-permute-start | bytes 196616 | tf_op jit(solution)/shard_map/ppermute | solution.py:986
  72.7 16.7 %collective-permute-start.16 = (bf16[8,32,128]{2,1,0:T(8,128)(2,1)}, bf16[8,32,128]{2,1,0:T(8,128)(2,1)S(1)}, u32[]{:S(2)}, u32[]{:S(2)}) collective-permute-start(bf16[8,32,128]{2,1,0:T(8,128)(2,1)} %get-tuple-element.82), channel_id=1, source_target_pairs={{0,4},{1,5},{2,6},{3,7},{4,0},{5,1},{6,2},{7,3},{8,12},{9,13},{10,... | collective-permute-start | bytes 196616 | tf_op jit(solution)/shard_map/ppermute | solution.py:986
  74.3 15.2 %collective-permute-start.17 = (bf16[8,32,128]{2,1,0:T(8,128)(2,1)}, bf16[8,32,128]{2,1,0:T(8,128)(2,1)S(1)}, u32[]{:S(2)}, u32[]{:S(2)}) collective-permute-start(bf16[8,32,128]{2,1,0:T(8,128)(2,1)} %get-tuple-element.83), channel_id=1, source_target_pairs={{0,5},{1,4},{2,7},{3,6},{4,1},{5,0},{6,3},{7,2},{8,13},{9,12},{10,... | collective-permute-start | bytes 196616 | tf_op jit(solution)/shard_map/ppermute | solution.py:986
  76.6 14.9 %collective-permute-start.18 = (bf16[8,32,128]{2,1,0:T(8,128)(2,1)}, bf16[8,32,128]{2,1,0:T(8,128)(2,1)S(1)}, u32[]{:S(2)}, u32[]{:S(2)}) collective-permute-start(bf16[8,32,128]{2,1,0:T(8,128)(2,1)} %get-tuple-element.84), channel_id=1, source_target_pairs={{0,6},{1,7},{2,4},{3,5},{4,2},{5,3},{6,0},{7,1},{8,14},{9,15},{10,... | collective-permute-start | bytes 196616 | tf_op jit(solution)/shard_map/ppermute | solution.py:986
  79.4 12.1 %collective-permute-start.19 = (bf16[8,32,128]{2,1,0:T(8,128)(2,1)}, bf16[8,32,128]{2,1,0:T(8,128)(2,1)S(1)}, u32[]{:S(2)}, u32[]{:S(2)}) collective-permute-start(bf16[8,32,128]{2,1,0:T(8,128)(2,1)} %get-tuple-element.85), channel_id=1, source_target_pairs={{0,7},{1,6},{2,5},{3,4},{4,3},{5,2},{6,1},{7,0},{8,15},{9,14},{10,... | collective-permute-start | bytes 196616 | tf_op jit(solution)/shard_map/ppermute | solution.py:986
  88.0 15.7 %collective-permute-start.13 = (bf16[8,32,128]{2,1,0:T(8,128)(2,1)}, bf16[8,32,128]{2,1,0:T(8,128)(2,1)S(1)}, u32[]{:S(2)}, u32[]{:S(2)}) collective-permute-start(bf16[8,32,128]{2,1,0:T(8,128)(2,1)} %get-tuple-element.79), channel_id=1, source_target_pairs={{0,1},{1,0},{2,3},{3,2},{4,5},{5,4},{6,7},{7,6},{8,9},{9,8},{10,11... | collective-permute-start | bytes 196616 | tf_op jit(solution)/shard_map/ppermute | solution.py:986
  89.5 17.0 %collective-permute-start.14 = (bf16[8,32,128]{2,1,0:T(8,128)(2,1)}, bf16[8,32,128]{2,1,0:T(8,128)(2,1)S(1)}, u32[]{:S(2)}, u32[]{:S(2)}) collective-permute-start(bf16[8,32,128]{2,1,0:T(8,128)(2,1)} %get-tuple-element.80), channel_id=1, source_target_pairs={{0,2},{1,3},{2,0},{3,1},{4,6},{5,7},{6,4},{7,5},{8,10},{9,11},{10,... | collective-permute-start | bytes 196616 | tf_op jit(solution)/shard_map/ppermute | solution.py:986
  89.5 18.0 %collective-permute-start.15 = (bf16[8,32,128]{2,1,0:T(8,128)(2,1)}, bf16[8,32,128]{2,1,0:T(8,128)(2,1)S(1)}, u32[]{:S(2)}, u32[]{:S(2)}) collective-permute-start(bf16[8,32,128]{2,1,0:T(8,128)(2,1)} %get-tuple-element.81), channel_id=1, source_target_pairs={{0,3},{1,2},{2,1},{3,0},{4,7},{5,6},{6,5},{7,4},{8,11},{9,10},{10,... | collective-permute-start | bytes 196616 | tf_op jit(solution)/shard_map/ppermute | solution.py:986
  99.8 7.7 %collective-permute-start.20 = (bf16[8,32,128]{2,1,0:T(8,128)(2,1)}, bf16[8,32,128]{2,1,0:T(8,128)(2,1)S(1)}, u32[]{:S(2)}, u32[]{:S(2)}) collective-permute-start(bf16[8,32,128]{2,1,0:T(8,128)(2,1)} %get-tuple-element.86), channel_id=1, source_target_pairs={{0,4},{1,5},{2,6},{3,7},{4,0},{5,1},{6,2},{7,3},{8,12},{9,13},{10,... | collective-permute-start | bytes 196616 | tf_op jit(solution)/shard_map/ppermute | solution.py:986
  101.3 6.3 %collective-permute-start.21 = (bf16[8,32,128]{2,1,0:T(8,128)(2,1)}, bf16[8,32,128]{2,1,0:T(8,128)(2,1)S(1)}, u32[]{:S(2)}, u32[]{:S(2)}) collective-permute-start(bf16[8,32,128]{2,1,0:T(8,128)(2,1)} %get-tuple-element.87), channel_id=1, source_target_pairs={{0,5},{1,4},{2,7},{3,6},{4,1},{5,0},{6,3},{7,2},{8,13},{9,12},{10,... | collective-permute-start | bytes 196616 | tf_op jit(solution)/shard_map/ppermute | solution.py:986
  103.7 6.5 %collective-permute-start.22 = (bf16[8,32,128]{2,1,0:T(8,128)(2,1)}, bf16[8,32,128]{2,1,0:T(8,128)(2,1)S(1)}, u32[]{:S(2)}, u32[]{:S(2)}) collective-permute-start(bf16[8,32,128]{2,1,0:T(8,128)(2,1)} %get-tuple-element.88), channel_id=1, source_target_pairs={{0,6},{1,7},{2,4},{3,5},{4,2},{5,3},{6,0},{7,1},{8,14},{9,15},{10,... | collective-permute-start | bytes 196616 | tf_op jit(solution)/shard_map/ppermute | solution.py:986
  106.4 7.2 %collective-permute-start.23 = (bf16[8,32,128]{2,1,0:T(8,128)(2,1)}, bf16[8,32,128]{2,1,0:T(8,128)(2,1)S(1)}, u32[]{:S(2)}, u32[]{:S(2)}) collective-permute-start(bf16[8,32,128]{2,1,0:T(8,128)(2,1)} %get-tuple-element.89), channel_id=1, source_target_pairs={{0,7},{1,6},{2,5},{3,4},{4,3},{5,2},{6,1},{7,0},{8,15},{9,14},{10,... | collective-permute-start | bytes 196616 | tf_op jit(solution)/shard_map/ppermute | solution.py:986
  117.1 5.4 %collective-permute-start.24 = (bf16[128,256]{1,0:T(8,128)(2,1)}, bf16[128,256]{1,0:T(8,128)(2,1)S(1)}, u32[]{:S(2)}, u32[]{:S(2)}) collective-permute-start(bf16[128,256]{1,0:T(8,128)(2,1)} %get-tuple-element.90), channel_id=1, source_target_pairs={{0,4},{1,5},{2,6},{3,7},{4,0},{5,1},{6,2},{7,3},{8,12},{9,13},{10,... | collective-permute-start | bytes 196616 | tf_op jit(solution)/shard_map/ppermute | solution.py:986
  117.1 6.8 %collective-permute-start.27 = (bf16[128,256]{1,0:T(8,128)(2,1)}, bf16[128,256]{1,0:T(8,128)(2,1)S(1)}, u32[]{:S(2)}, u32[]{:S(2)}) collective-permute-start(bf16[128,256]{1,0:T(8,128)(2,1)} %get-tuple-element.91), channel_id=1, source_target_pairs={{0,4},{1,5},{2,6},{3,7},{4,0},{5,1},{6,2},{7,3},{8,12},{9,13},{10,... | collective-permute-start | bytes 196616 | tf_op jit(solution)/shard_map/ppermute | solution.py:986
  124.7 5.1 %collective-permute-start.28 = (bf16[2,128,256]{2,1,0:T(8,128)(2,1)S(1)}, bf16[2,128,256]{2,1,0:T(8,128)(2,1)S(1)}, u32[]{:S(2)}, u32[]{:S(2)}) collective-permute-start(bf16[2,128,256]{2,1,0:T(8,128)(2,1)S(1)} %get-tuple-element.110), channel_id=1, source_target_pairs={{0,2},{1,3},{2,0},{3,1},{4,6},{5,7},{6,4},{7,5},{8,10},{9,11},{10,... | collective-permute-start | bytes 393224 | tf_op jit(solution)/shard_map/ppermute | solution.py:986
  128.4 7.0 %collective-permute-start.26 = (bf16[2,2,128,256]{3,2,0,1:T(8,128)(2,1)S(1)}, bf16[2,2,128,256]{3,2,0,1:T(8,128)(2,1)S(1)}, u32[]{:S(2)}, u32[]{:S(2)}) collective-permute-start(bf16[2,2,128,256]{3,2,0,1:T(8,128)(2,1)S(1)} %get-tuple-element.108), channel_id=1, source_target_pairs={{0,1},{1,0},{2,3},{3,2},{4,5},{5,4},{6,7},{7,6},{8,9},{9,8},{10,11... | collective-permute-start | bytes 786440 | tf_op jit(solution)/shard_map/ppermute | solution.py:986
  129.8 6.4 %collective-permute-start.29 = (bf16[2,2,128,256]{3,2,0,1:T(8,128)(2,1)S(1)}, bf16[2,2,128,256]{3,2,0,1:T(8,128)(2,1)S(1)}, u32[]{:S(2)}, u32[]{:S(2)}) collective-permute-start(bf16[2,2,128,256]{3,2,0,1:T(8,128)(2,1)S(1)} %get-tuple-element.106), channel_id=1, source_target_pairs={{0,16},{8,24},{16,0},{24,8},{1,17},{9,25},{17,1},{25,9},{2,18},{10... | collective-permute-start | bytes 786440 | tf_op jit(solution)/shard_map/ppermute | solution.py:986
  136.3 9.2 %collective-permute-start.30 = (bf16[2,2,2,128,256]{4,3,0,1,2:T(8,128)(2,1)S(1)}, bf16[2,2,2,128,256]{4,3,0,1,2:T(8,128)(2,1)S(1)}, u32[]{:S(2)}, u32[]{:S(2)}) collective-permute-start(bf16[2,2,2,128,256]{4,3,0,1,2:T(8,128)(2,1)S(1)} %pad_maximum_fusion.2), channel_id=1, source_target_pairs={{0,16},{8,24},{16,0},{24,8},{1,17},{9,25},{17,1},{25,9},{2,18},{10... | collective-permute-start | bytes 1572872 | tf_op jit(solution)/shard_map/ppermute | solution.py:986
  137.1 9.2 %collective-permute-start.31 = (bf16[2,2,2,128,256]{4,3,1,2,0:T(8,128)(2,1)S(1)}, bf16[2,2,2,128,256]{4,3,1,2,0:T(8,128)(2,1)S(1)}, u32[]{:S(2)}, u32[]{:S(2)}) collective-permute-start(bf16[2,2,2,128,256]{4,3,1,2,0:T(8,128)(2,1)S(1)} %pad_maximum_fusion.3), channel_id=1, source_target_pairs={{0,1},{1,0},{2,3},{3,2},{4,5},{5,4},{6,7},{7,6},{8,9},{9,8},{10,11... | collective-permute-start | bytes 1572872 | tf_op jit(solution)/shard_map/ppermute | solution.py:986
  146.6 8.0 %collective-permute-start.33 = (bf16[2,8,128,256]{3,2,1,0:T(8,128)(2,1)S(1)}, bf16[2,8,128,256]{3,2,1,0:T(8,128)(2,1)S(1)}, u32[]{:S(2)}, u32[]{:S(2)}) collective-permute-start(bf16[2,8,128,256]{3,2,1,0:T(8,128)(2,1)S(1)} %bitcast.84), channel_id=1, source_target_pairs={{0,8},{8,0},{16,24},{24,16},{1,9},{9,1},{17,25},{25,17},{2,10},{10... | collective-permute-start | bytes 3145736 | tf_op jit(solution)/shard_map/ppermute | solution.py:986
  146.6 7.9 %collective-permute-start.32 = (bf16[2,8,128,256]{3,2,1,0:T(8,128)(2,1)S(1)}, bf16[2,8,128,256]{3,2,1,0:T(8,128)(2,1)S(1)}, u32[]{:S(2)}, u32[]{:S(2)}) collective-permute-start(bf16[2,8,128,256]{3,2,1,0:T(8,128)(2,1)S(1)} %bitcast.82), channel_id=1, source_target_pairs={{0,8},{8,0},{16,24},{24,16},{1,9},{9,1},{17,25},{25,17},{2,10},{10... | collective-permute-start | bytes 3145736 | tf_op jit(solution)/shard_map/ppermute | solution.py:986
  (25 other events, 82.4 us)
